TPU v7x, 32 devices: a whole 2x2x4 slice. The times are simulated.
32 devices in a mesh: depth: 16 (over z, y, core), filt: 2 (over x).
Axes of the slice: x: 2, y: 2, z: 4, core: 2. Of those that a mesh axis runs over, the one named last changes fastest.
Arguments:
- volume: bfloat16 [64, 64, 4096], P('filt', 'depth'), may hold values from -6 to 6
- w_three: bfloat16 [1728, 128], P(None, 'filt'), may hold values from -0.15625 to 0.15625
- w_four: bfloat16 [3456, 256], P(None, 'filt'), may hold values from -0.109375 to 0.109375
- cotangent: bfloat16 [256, 16, 256], P('filt', 'depth'), may hold values from -384 to 384
Outputs:
- x_grad: float32 [64, 64, 4096], P('filt', 'depth')
- w3_grad: float32 [1728, 128], P(None, 'filt')
- w4_grad: float32 [3456, 256], P(None, 'filt')
All inputs are finite; a program needn't handle non-finite values.
Results may differ from a plain program's by a relative error of at most 0.014.
Values may be sent and summed in bfloat16 or wider, within the bound.
No kernel may reach another device: no remote copies, remote signals or barrier semaphores. Data moves between devices by JAX's collectives and lax.ppermute only.
A program may use at most 192 MiB of HBM per device.

v0:
```python
import functools
import math

import jax
import jax.numpy as jnp
import numpy as np
from jax import lax
from jax.experimental import pallas as pl
from jax.experimental.pallas import tpu as pltpu
from jax.sharding import PartitionSpec as P

HH = 32
WW = 128
LANES = 128
BF = jnp.bfloat16
F32 = jnp.float32
VMEM_LIMIT = 28 * 2**20
TILES = HH // 4
ROWS = 16


def nn(a, b):
    return jnp.dot(a, b, preferred_element_type=F32)


def nt(a, b):
    return lax.dot_general(a, b, (((1,), (1,)), ((), ())), preferred_element_type=F32)


def call(body, outs, name, scratch=(), scalars=0, inputs=0, gflop=1.0):
    specs = [pl.BlockSpec(memory_space=pltpu.SMEM)] * scalars
    specs += [pl.BlockSpec(memory_space=pltpu.VMEM)] * inputs
    return pl.pallas_call(
        body,
        out_shape=[jax.ShapeDtypeStruct(shape, dtype) for shape, dtype in outs],
        in_specs=specs,
        out_specs=[pl.BlockSpec(memory_space=pltpu.VMEM)] * len(outs),
        scratch_shapes=list(scratch),
        compiler_params=pltpu.CompilerParams(vmem_limit_bytes=VMEM_LIMIT),
        cost_estimate=pl.CostEstimate(
            flops=int(gflop * 1e9), transcendentals=0, bytes_accessed=4 * 2**20
        ),
        name=name,
    )


def sigmoid(value):
    return 0.5 * jnp.tanh(0.5 * value) + 0.5


def shifted(block, width):
    lane = lax.broadcasted_iota(jnp.int32, block.shape, 1) % width
    zero = jnp.zeros(block.shape, BF)
    before = jnp.where(lane == 0, zero, pltpu.roll(block, 1, axis=1))
    after = jnp.where(lane == width - 1, zero, pltpu.roll(block, LANES - 1, axis=1))
    return before, after


def fine_rows(source, windows, plane, offset, chans, group, first, count):
    lower = max(first - 1, 0)
    upper = min(first + count + 1, HH)

    def row(step):
        block = source(step)
        before, after = shifted(block, WW)
        lanes = pl.ds(pl.multiple_of((step - first + 1) * LANES, LANES), LANES)
        for shift, value in enumerate((before, block, after)):
            windows[plane, pl.ds(pl.multiple_of(shift * group + offset, 32), chans), lanes] = value

    def several(turn, _):
        for k in range(ROWS):
            row(lower + turn * ROWS + k)
        return 0

    zero = jnp.zeros((chans, LANES), BF)
    for shift in range(3):
        rows = pl.ds(pl.multiple_of(shift * group + offset, 32), chans)
        if first == 0:
            windows[plane, rows, 0:LANES] = zero
        if first + count == HH:
            windows[plane, rows, (count + 1) * LANES : (count + 2) * LANES] = zero
    lax.fori_loop(0, (upper - lower) // ROWS, several, 0)
    for step in range(upper - (upper - lower) % ROWS, upper):
        row(step)


def row_of(ref):
    def source(step):
        return ref[:, pl.ds(pl.multiple_of(step * LANES, LANES), LANES)]

    return source


def coarse_rows(source, windows, plane, offset, chans, group):
    half = LANES // 2
    lane = lax.broadcasted_iota(jnp.int32, (chans, LANES), 1)

    def put(shift, tile, value):
        rows = pl.ds(pl.multiple_of(shift * group + offset, 32), chans)
        windows[plane, rows, tile * LANES : (tile + 1) * LANES] = value

    for tile in range(TILES):
        block = source(tile)
        before, after = shifted(block, half)
        for shift, value in enumerate((before, block, after)):
            put(shift, tile + 1, value)
            if tile == 0 or tile == TILES - 1:
                turned = pltpu.roll(value.astype(F32), half, axis=1)
                if tile == TILES - 1:
                    put(shift, 0, jnp.where(lane < half, 0.0, turned).astype(BF))
                else:
                    put(shift, TILES + 1, jnp.where(lane < half, turned, 0.0).astype(BF))


def tile_of(ref):
    def source(tile):
        return ref[:, tile * LANES : (tile + 1) * LANES]

    return source


def each(count, build):
    def step(d, _):
        build(d)
        return 0

    lax.fori_loop(0, count, step, 0)


def volume_windows(filt, refs, windows):
    own, low, high, edge, middle, peer_low, peer_high = refs
    planes, chans, _ = own.shape
    mine = pl.multiple_of(filt[0] * chans, 32)
    theirs = pl.multiple_of((1 - filt[0]) * chans, 32)

    def put(ref, plane, offset):
        fine_rows(row_of(ref), windows, plane, offset, chans, 2 * chans, 0, HH)

    each(planes, lambda d: put(own.at[d], d + 1, mine))
    each(planes - 2, lambda d: put(middle.at[d], d + 2, theirs))
    each(2, lambda d: put(edge.at[d], 1 + d * (planes - 1), theirs))
    put(low, 0, mine)
    put(high, planes + 1, mine)
    put(peer_low, 0, theirs)
    put(peer_high, planes + 1, theirs)


def forward_fine_kernel(filt, own, low, high, edge, middle, plow, phigh, weights, pool, pooled, slope, windows):
    planes = own.shape[0]
    volume_windows(filt, (own, low, high, edge, middle, plow, phigh), windows)
    outs = weights.shape[1] // 3
    span = 2 * LANES

    def chunk(j, _):
        tops = (j * 2, HH // 2 + j * 2)
        acts = []
        for d in range(planes):
            acts.append([None, None])
        for side, top in enumerate(tops):
            totals = [None] * planes
            for p in range(planes + 2):
                value = None
                for kh in range(3):
                    lanes = pl.ds(pl.multiple_of((top + kh) * LANES, LANES), span)
                    part = nn(weights[kh], windows[p, :, lanes])
                    value = part if value is None else value + part
                for kd in range(3):
                    d = p - kd
                    if 0 <= d < planes:
                        piece = value[kd * outs : (kd + 1) * outs]
                        totals[d] = piece if totals[d] is None else totals[d] + piece
            for d in range(planes):
                pre = totals[d]
                sigma = sigmoid(pre)
                act = pre * sigma
                slope[d, :, pl.ds(pl.multiple_of(top * LANES, LANES), span)] = (
                    sigma + act * (1.0 - sigma)
                ).astype(BF)
                acts[d][side] = act[:, :LANES] + act[:, LANES:]
        for d in range(0, planes, 2):
            both = jnp.concatenate(
                [acts[d][0] + acts[d + 1][0], acts[d][1] + acts[d + 1][1]], axis=1
            )
            coarse = both.astype(BF)
            rest = (both - coarse.astype(F32)).astype(BF)
            mean = nn(coarse, pool[...]) + nn(rest, pool[...])
            pooled[d // 2, :, pl.ds(pl.multiple_of(j * LANES, LANES), LANES)] = mean.astype(BF)
        return 0

    lax.fori_loop(0, TILES, chunk, 0, unroll=2)


def forward_coarse_kernel(filt, own, peer, low, high, weights, cot, spread, grads, windows, first_out, last_out):
    planes, chans, cells = own.shape
    mine = pl.multiple_of(filt[0] * chans, 32)
    theirs = pl.multiple_of((1 - filt[0]) * chans, 32)
    sides = ((mine, low.at[0], own, high.at[0]), (theirs, low.at[1], peer, high.at[1]))
    for offset, below, middle, above in sides:
        refs = [below] + [middle.at[d] for d in range(planes)] + [above]
        for plane, ref in enumerate(refs):
            coarse_rows(tile_of(ref), windows, plane, offset, chans, 2 * chans)
    upper = nn(cot[...], spread[...])
    span = cells // 2
    for d in range(planes):
        for start in range(0, cells, span):
            pre = None
            for kd in range(3):
                for kh in range(3):
                    begin = start + kh * LANES
                    part = nn(weights[kd * 3 + kh], windows[d + kd, :, begin : begin + span])
                    pre = part if pre is None else pre + part
            sigma = sigmoid(pre)
            slope = sigma * (1.0 + pre * (1.0 - sigma))
            value = (upper[:, start : start + span] * slope).astype(BF)
            grads[d, :, start : start + span] = value
            if d == 0:
                first_out[:, start : start + span] = value
            if d == planes - 1:
                last_out[:, start : start + span] = value


def kernel_grad_coarse_kernel(windows, grads, out, total):
    deep, group, _ = windows.shape
    planes = deep - 2
    outs = grads.shape[0] // planes
    cells = grads.shape[1]
    seen = set()
    for p in range(deep):
        first, last = max(p - 2, 0), min(p, planes - 1)
        for kh in range(3):
            value = nt(
                windows[p, :, kh * LANES : kh * LANES + cells],
                grads[first * outs : (last + 1) * outs, :],
            )
            for d in range(first, last + 1):
                index = (p - d) * 3 + kh
                rows = slice(index * group, (index + 1) * group)
                part = value[:, (d - first) * outs : (d - first + 1) * outs]
                total[rows, :] = total[rows, :] + part if index in seen else part
                seen.add(index)
    out[...] = total[...].astype(out.dtype)


def backward_coarse_kernel(grads, low, high, weights, own, peer, windows):
    planes, chans, cells = grads.shape
    refs = [low] + [grads.at[d] for d in range(planes)] + [high]
    for plane, ref in enumerate(refs):
        coarse_rows(tile_of(ref), windows, plane, 0, chans, chans)
    half = weights.shape[1] // 2
    span = cells // 2
    for d in range(planes):
        for start in range(0, cells, span):
            value = None
            for kd in range(3):
                for kh in range(3):
                    begin = start + kh * LANES
                    part = nn(weights[kd * 3 + kh], windows[d + kd, :, begin : begin + span])
                    value = part if value is None else value + part
            own[d, :, start : start + span] = value[:half]
            peer[d, :, start : start + span] = value[half:].astype(BF)


def grad_fine_kernel(own, peer, slope, unpool, grads, first_out, last_out):
    planes = own.shape[0]
    for d in range(planes):
        for j in range(TILES):
            lanes = slice(j * LANES, (j + 1) * LANES)
            block = (own[d, :, lanes] + peer[d, :, lanes].astype(F32)).astype(BF)
            wide = nn(block, unpool[...])
            for side in range(2):
                part = wide[:, side * LANES : (side + 1) * LANES]
                for a in range(2):
                    for row in (side * HH // 2 + 2 * j, side * HH // 2 + 2 * j + 1):
                        cells = slice(row * LANES, (row + 1) * LANES)
                        value = (part * slope[2 * d + a, :, cells].astype(F32)).astype(BF)
                        grads[2 * d + a, :, cells] = value
                        if 2 * d + a == 0:
                            first_out[:, cells] = value
                        if 2 * d + a == 2 * planes - 1:
                            last_out[:, cells] = value


def kernel_grad_fine_kernel(filt, own, low, high, edge, middle, plow, phigh, grads, out, windows, total):
    planes, _, cells = own.shape
    volume_windows(filt, (own, low, high, edge, middle, plow, phigh), windows)
    group = windows.shape[1]
    outs = grads.shape[0] // planes
    seen = set()
    for p in range(planes + 2):
        first, last = max(p - 2, 0), min(p, planes - 1)
        for kh in range(3):
            value = nt(
                windows[p, :, kh * LANES : kh * LANES + cells],
                grads[first * outs : (last + 1) * outs, :],
            )
            for d in range(first, last + 1):
                index = (p - d) * 3 + kh
                rows = slice(index * group, (index + 1) * group)
                part = value[:, (d - first) * outs : (d - first + 1) * outs]
                total[rows, :] = total[rows, :] + part if index in seen else part
                seen.add(index)
    out[...] = total[...].astype(out.dtype)


def backward_fine_kernel(first, count, grads, low, high, weights, own, peer, windows):
    planes, chans, _ = grads.shape

    def put(ref, plane):
        fine_rows(row_of(ref), windows, plane, 0, chans, chans, first, count)

    each(planes, lambda d: put(grads.at[d], d + 1))
    put(low, 0)
    put(high, planes + 1)
    outs = weights.shape[1] // 3
    half = outs // 2
    span = 2 * LANES

    def chunk(j, _):
        totals = [None] * planes
        for p in range(planes + 2):
            value = None
            for kh in range(3):
                lanes = pl.ds(pl.multiple_of((2 * j + kh) * LANES, LANES), span)
                part = nn(weights[kh], windows[p, :, lanes])
                value = part if value is None else value + part
            for kd in range(3):
                d = p - kd
                if 0 <= d < planes:
                    piece = value[kd * outs : (kd + 1) * outs]
                    totals[d] = piece if totals[d] is None else totals[d] + piece
        cells = pl.ds(pl.multiple_of(j * span, span), span)
        for d in range(planes):
            own[d, :, cells] = totals[d][:half]
            peer[d, :, cells] = totals[d][half:].astype(BF)
        return 0

    lax.fori_loop(0, count // 2, chunk, 0, unroll=2)


def to_next(value):
    count = lax.axis_size("depth")
    return lax.ppermute(value, "depth", [(i, i + 1) for i in range(count - 1)])


def to_previous(value):
    count = lax.axis_size("depth")
    return lax.ppermute(value, "depth", [(i + 1, i) for i in range(count - 1)])


def swap(value):
    return lax.ppermute(value, "filt", [(0, 1), (1, 0)])


def halves(value, bit):
    upper = (lax.axis_index("depth") & bit) != 0
    half = value.shape[0] // 2
    return (
        jnp.where(upper, value[half:], value[:half]),
        jnp.where(upper, value[:half], value[half:]),
    )


def across(value, bit):
    count = lax.axis_size("depth")
    return lax.ppermute(value, "depth", [(i, i ^ bit) for i in range(count)])


def plus(a, b):
    return (a.astype(F32) + b.astype(F32)).astype(a.dtype)


def depth_sum(value):
    count = lax.axis_size("depth")
    rows = value.shape[0]
    value = jnp.pad(value, ((0, -rows % 64), (0, 0)))
    near = [bit for bit in (1, 2) if bit < count]
    for bit in near:
        keep, send = halves(value, bit)
        other = yield send, bit
        value = plus(keep, other)
    bit = 4
    while bit < count:
        other = yield value, bit
        value = plus(value, other)
        bit *= 2
    for bit in reversed(near):
        other = yield value, bit
        upper = (lax.axis_index("depth") & bit) != 0
        value = jnp.concatenate(
            [jnp.where(upper, other, value), jnp.where(upper, value, other)], axis=0
        )
    return value[:rows]


class Sum:
    def __init__(self, value):
        self.steps = depth_sum(value)
        self.result = None
        self.take(None)

    def take(self, other):
        try:
            self.pending = self.steps.send(other)
        except StopIteration as stop:
            self.pending, self.result = None, stop.value

    def finish(self):
        while self.pending is not None:
            self.take(across(*self.pending))
        return self.result


def beside(sums, kernel, inputs):
    sums = [one for one in sums if one.pending is not None]
    sends = [one.pending[0] for one in sums]
    inputs, sends = lax.optimization_barrier((list(inputs), sends))
    others = [across(send, one.pending[1]) for send, one in zip(sends, sums)]
    outs, others = lax.optimization_barrier((kernel(*inputs), others))
    for one, other in zip(sums, others):
        one.take(other)
    return outs


def after(value, *others):
    return lax.optimization_barrier((value, *others))[0]


def pool_matrix():
    lane = np.arange(2 * LANES)
    column = np.where(lane < LANES, lane // 2, LANES // 2 + (lane - LANES) // 2)
    return (np.arange(LANES)[None] == column[:, None]) * np.float32(0.125)


def spread_matrix(tall, broad):
    lane = np.arange(4 * tall * broad)
    tile, half, w = lane // LANES, lane % LANES // (2 * broad), lane % (2 * broad)
    row = tile + half * TILES
    cell = row // 2 * broad + w // 2
    return (np.arange(tall * broad)[:, None] == cell[None]) * np.float32(0.125)


def body(volume, w_three, w_four, cotangent):
    own_in, planes, cells = volume.shape
    mid = w_three.shape[1]
    c_mid = w_four.shape[0] // 27
    outs = w_four.shape[1]
    half_planes = planes // 2
    coarse = cells // 4
    filt = lax.axis_index("filt")
    which = filt.astype(jnp.int32).reshape(1)

    own = volume.transpose(1, 0, 2)
    edge = swap(jnp.stack([own[0], own[planes - 1]]))
    middle = swap(own[1 : planes - 1])
    low, high = to_next(own[planes - 1]), to_previous(own[0])
    plow, phigh = to_next(edge[1]), to_previous(edge[0])

    fine = w_three.reshape(3, 3, 3, 2 * own_in, mid)
    fine_forward = fine.transpose(1, 0, 4, 2, 3).reshape(3, 3 * mid, 6 * own_in)
    turned = fine[::-1, ::-1, ::-1].reshape(3, 3, 3, 2, own_in, mid)
    turned = jnp.where(filt == 0, turned, turned[:, :, :, ::-1])
    fine_backward = turned.transpose(1, 0, 3, 4, 2, 5).reshape(3, 6 * own_in, 3 * mid)
    wide = w_four.reshape(3, 3, 3, c_mid, outs)
    wide_forward = wide.transpose(0, 1, 4, 2, 3).reshape(9, outs, 3 * c_mid)
    turned = wide[::-1, ::-1, ::-1].reshape(3, 3, 3, 2, mid, outs)
    turned = jnp.where(filt == 0, turned, turned[:, :, :, ::-1])
    wide_backward = turned.transpose(0, 1, 3, 4, 2, 5).reshape(9, c_mid, 3 * outs)
    pool = jnp.asarray(pool_matrix(), BF)
    unpool = jnp.asarray(pool_matrix().T, BF)
    spread = jnp.asarray(spread_matrix(HH // 4, WW // 4), BF)

    fine_forward, fine_backward, wide_forward, wide_backward, middle = lax.optimization_barrier(
        (fine_forward, fine_backward, wide_forward, wide_backward, middle)
    )

    fine_windows = pltpu.VMEM((planes + 2, 6 * own_in, (HH + 2) * LANES), BF)
    pooled, slope = call(
        forward_fine_kernel,
        [((half_planes, mid, coarse), BF), ((planes, mid, cells), BF)],
        "forward_fine",
        [fine_windows],
        scalars=1,
        inputs=9,
        gflop=17.0,
    )(which, own, low, high, edge, middle, plow, phigh, fine_forward, pool)

    pooled_peer = swap(pooled)
    pool_low = to_next(jnp.stack([pooled[half_planes - 1], pooled_peer[half_planes - 1]]))
    pool_high = to_previous(jnp.stack([pooled[0], pooled_peer[0]]))
    coarse_lanes = (TILES + 2) * LANES
    grad_four, coarse_windows, four_first, four_last = call(
        forward_coarse_kernel,
        [
            ((half_planes, outs, coarse), BF),
            ((half_planes + 2, 3 * c_mid, coarse_lanes), BF),
            ((outs, coarse), BF),
            ((outs, coarse), BF),
        ],
        "forward_coarse",
        scalars=1,
        inputs=7,
        gflop=6.0,
    )(
        which,
        pooled,
        pooled_peer,
        pool_low,
        pool_high,
        wide_forward,
        cotangent.reshape(outs, -1),
        spread,
    )

    four_low, four_high = to_next(four_last), to_previous(four_first)
    (coarse_kernel,) = call(
        kernel_grad_coarse_kernel,
        [((27 * c_mid, outs), BF)],
        "kernel_grad_coarse",
        [pltpu.VMEM((27 * c_mid, outs), F32)],
        inputs=2,
        gflop=6.0,
    )(coarse_windows, grad_four.reshape(half_planes * outs, coarse))
    coarse_sum = Sum(coarse_kernel)
    own_back, peer_back = beside(
        [coarse_sum],
        call(
            backward_coarse_kernel,
            [((half_planes, mid, coarse), F32), ((half_planes, mid, coarse), BF)],
            "backward_coarse",
            [pltpu.VMEM((half_planes + 2, 3 * outs, coarse_lanes), BF)],
            inputs=4,
            gflop=5.0,
        ),
        (grad_four, four_low, four_high, wide_backward),
    )
    (peer_back,) = beside([coarse_sum], lambda value: (swap(value),), (peer_back,))

    grad_three, three_first, three_last = call(
        grad_fine_kernel,
        [((planes, mid, cells), BF), ((mid, cells), BF), ((mid, cells), BF)],
        "grad_fine",
        inputs=4,
        gflop=3.0,
    )(own_back, peer_back, slope, unpool)
    three_low, three_high = to_next(three_last), to_previous(three_first)
    (fine_kernel,) = beside(
        [coarse_sum],
        call(
            kernel_grad_fine_kernel,
            [((54 * own_in, mid), BF)],
            "kernel_grad_fine",
            [fine_windows, pltpu.VMEM((54 * own_in, mid), F32)],
            scalars=1,
            inputs=8,
            gflop=15.0,
        ),
        (which, own, low, high, edge, middle, plow, phigh, grad_three.reshape(planes * mid, cells)),
    )

    fine_sum = Sum(fine_kernel.reshape(27 * own_in, 2 * mid))
    parts = 4
    rows = HH // parts
    owns, peers = [], []
    for part in range(parts):
        mine, theirs = beside(
            [fine_sum, coarse_sum],
            call(
                functools.partial(backward_fine_kernel, part * rows, rows),
                [((planes, own_in, rows * WW), F32), ((planes, own_in, rows * WW), BF)],
                f"backward_fine_{part}",
                [pltpu.VMEM((planes + 2, 3 * mid, (rows + 2) * LANES), BF)],
                inputs=4,
                gflop=6.0,
            ),
            (grad_three, three_low, three_high, fine_backward),
        )
        owns.append(mine)
        peers.append(swap(theirs))
    coarse_sum = coarse_sum.finish()
    fine_sum = fine_sum.finish().reshape(54 * own_in, mid)
    x_grad = jnp.concatenate([a + b.astype(F32) for a, b in zip(owns, peers)], axis=2)
    x_grad = x_grad.transpose(1, 0, 2)

    all_cells = planes * lax.axis_size("depth") * cells
    scale_four = 1.0 / math.sqrt(all_cells / 8.0)
    scale_three = 1.0 / math.sqrt(all_cells * 1.0)
    return (x_grad, fine_sum.astype(F32) * scale_three, coarse_sum.astype(F32) * scale_four)


def solution(mesh):
    return jax.shard_map(
        body,
        mesh=mesh,
        in_specs=(
            P("filt", "depth", None),
            P(None, "filt"),
            P(None, "filt"),
            P("filt", "depth", None),
        ),
        out_specs=(P("filt", "depth", None), P(None, "filt"), P(None, "filt")),
        check_vma=False,
    )
```

profile of v0, /device:TPU:0, one launch (start us, length us, event | category | flops | bytes accessed | tf_op | source)
XLA Modules:
  0.0 191.7 jit_solution(7820054518057978215)
XLA Ops:
  0.6 1.8 copy.35
  4.2 2.9 %collective-permute-start.2 = (bf16[2,32,4096]{2,1,0:T(8,128)(2,1)}, bf16[2,32,4096]{2,1,0:T(8,128)(2,1)S(1)}, u32[]{:S(2)}, u32[]{:S(2)}) collective-permute-start(bf16[2,32,4096]{2,1,0:T(8,128)(2,1)} %pad_maximum_fusion), channel_id=1, source_target_pairs={{0,1},{1,0},{2,3},{3,2},{4,5},{5,4},{6,7},{7,6},{8,9},{9,8},{10,11... | collective-permute-start | bytes 1572872 | tf_op jit(solution)/shard_map/ppermute | solution.py:351
  8.0 2.2 %collective-permute-start = (bf16[32,4096]{1,0:T(8,128)(2,1)}, bf16[32,4096]{1,0:T(8,128)(2,1)}, u32[]{:S(2)}, u32[]{:S(2)}) collective-permute-start(bf16[32,4096]{1,0:T(8,128)(2,1)} %get-tuple-element.185), channel_id=1, source_target_pairs={{0,2},{2,4},{4,6},{6,8},{8,10},{10,12},{12,14},{14,16},{16,18},{18... | collective-permute-start | bytes 786440 | tf_op jit(solution)/shard_map/ppermute | solution.py:342
  11.9 2.9 %rev.12 = bf16[3,3,3,64,64]{3,2,1,0,4:T(4,128)(2,1)} reverse(bf16[3,3,3,64,64]{3,2,1,0,4:T(4,128)(2,1)S(1)} %reshape.51), dimensions={0,1,2} | reverse | bytes 442368 | tf_op jit(solution)/shard_map/rev | solution.py:460
  14.8 2.1 %copy.27 = bf16[3,3,3,64,64]{4,3,2,1,0:T(8,128)(2,1)} copy(bf16[3,3,3,64,64]{3,2,1,0,4:T(4,128)(2,1)} %rev.12) | data formatting | bytes 442368 | tf_op jit(solution)/shard_map/rev | solution.py:460
  16.8 1.3 fusion.1
  19.3 2.2 %reshape.54.weights = bf16[3,192,192]{2,1,0:T(8,128)(2,1)} reshape(bf16[3,3,2,32,3,64]{5,4,3,2,1,0:T(4,128)(2,1)} %copy.28) | data formatting | bytes 442368 | tf_op jit(solution)/shard_map/reshape | solution.py:462
  21.5 2.2 %rev.14 = bf16[3,3,3,128,128]{4,3,2,1,0:T(8,128)(2,1)} reverse(bf16[3,3,3,128,128]{4,3,2,1,0:T(8,128)(2,1)} %bitcast.39), dimensions={0,1,2} | reverse | bytes 1769472 | tf_op jit(solution)/shard_map/rev | solution.py:465
  23.7 1.9 %copy.30 = bf16[3,3,3,2,64,128]{5,2,4,3,1,0:T(4,128)(2,1)S(1)} copy(bf16[3,3,3,2,64,128]{5,4,3,2,1,0:T(8,128)(2,1)} %bitcast.41) | data formatting | bytes 1769472 | tf_op jit(solution)/shard_map/reshape | solution.py:465
  26.5 5.2 %collective-permute-start.4 = (bf16[32,4096]{1,0:T(8,128)(2,1)}, bf16[32,4096]{1,0:T(8,128)(2,1)}, u32[]{:S(2)}, u32[]{:S(2)}) collective-permute-start(bf16[32,4096]{1,0:T(8,128)(2,1)} %get-tuple-element.191), channel_id=1, source_target_pairs={{0,2},{2,4},{4,6},{6,8},{8,10},{10,12},{12,14},{14,16},{16,18},{18... | collective-permute-start | bytes 786440 | tf_op jit(solution)/shard_map/ppermute | solution.py:342
  32.9 1.7 fusion
  34.6 2.6 %reshape.58.weights = bf16[9,128,384]{2,1,0:T(8,128)(2,1)S(1)} reshape(bf16[3,3,2,64,3,128]{5,4,3,2,1,0:T(4,128)(2,1)} %fusion) | data formatting | bytes 1769472 | tf_op jit(solution)/shard_map/reshape | solution.py:467
  37.3 2.1 %copy.26 = bf16[3,3,64,3,64]{4,3,2,1,0:T(4,128)(2,1)} copy(bf16[3,3,64,3,64]{4,3,0,1,2:T(4,128)(2,1)} %bitcast.38) | data formatting | bytes 442368 | tf_op jit(solution)/shard_map/transpose | solution.py:459
  39.4 1.5 reshape.52.weights
  41.0 14.4 %forward_fine.1 = (bf16[2,64,1024]{2,1,0:T(8,128)(2,1)S(1)}, bf16[4,64,4096]{2,1,0:T(8,128)(2,1)S(1)}) custom-call(s32[1]{0:T(128)} %bitcast.filt, bf16[4,32,4096]{2,1,0:T(8,128)(2,1)S(1)} %bitcast.33, bf16[32,4096]{1,0:T(8,128)(2,1)} %collective-permute-done.low, bf16[32,4096]{1,0:T(8,128)(2,1)} %collective-permute-done.1.high, ...), custom_call_target="tpu_custom_call" | custom-call | flops 16999999488 | bytes 4194304 | tf_op jit(solution)/shard_map/forward_fine/pallas_call | solution.py:477
  55.4 1.3 copy-done.13
  56.7 1.5 collective-permute-start.6
  59.0 6.3 %collective-permute-done.6.peer = bf16[2,64,1024]{2,1,0:T(8,128)(2,1)S(1)} collective-permute-done((bf16[2,64,1024]{2,1,0:T(8,128)(2,1)S(1)}, bf16[2,64,1024]{2,1,0:T(8,128)(2,1)S(1)}, u32[]{:S(2)}, u32[]{:S(2)}) %collective-permute-start.6) | collective-permute-done | bytes 262176 | tf_op jit(solution)/shard_map/ppermute | solution.py:351
  68.1 3.8 %collective-permute-start.7 = (bf16[2,64,1024]{2,1,0:T(8,128)(2,1)}, bf16[2,64,1024]{2,1,0:T(8,128)(2,1)}, u32[]{:S(2)}, u32[]{:S(2)}) collective-permute-start(bf16[2,64,1024]{2,1,0:T(8,128)(2,1)} %pad_maximum_fusion.2), channel_id=1, source_target_pairs={{0,2},{2,4},{4,6},{6,8},{8,10},{10,12},{12,14},{14,16},{16,18},{18... | collective-permute-start | bytes 786440 | tf_op jit(solution)/shard_map/ppermute | solution.py:342
  71.9 1.8 copy.31.weights
  76.6 4.7 %forward_coarse.1 = (bf16[2,128,1024]{2,1,0:T(8,128)(2,1)S(1)}, bf16[4,384,1280]{2,1,0:T(8,128)(2,1)S(1)}, bf16[128,1024]{1,0:T(8,128)(2,1)S(1)}, bf16[128,1024]{1,0:T(8,128)(2,1)S(1)}) custom-call(s32[1]{0:T(128)} %bitcast.filt, bf16[2,64,1024]{2,1,0:T(8,128)(2,1)S(1)} %copy-done.2, bf16[2,64,1024]{2,1,0:T(8,128)(2,1)S(1)} %copy-done.4, ...), custom_call_target="tpu_custom_call" | custom-call | flops 6000000000 | bytes 4194304 | tf_op jit(solution)/shard_map/forward_coarse/pallas_call | solution.py:491
  81.3 1.3 collective-permute-start.10
  82.6 8.2 %collective-permute-start.9 = (bf16[128,1024]{1,0:T(8,128)(2,1)S(1)}, bf16[128,1024]{1,0:T(8,128)(2,1)S(1)}, u32[]{:S(2)}, u32[]{:S(2)}) collective-permute-start(bf16[128,1024]{1,0:T(8,128)(2,1)S(1)} %get-tuple-element.94), channel_id=1, source_target_pairs={{0,2},{2,4},{4,6},{6,8},{8,10},{10,12},{12,14},{14,16},{16,18},{18... | collective-permute-start | bytes 786440 | tf_op jit(solution)/shard_map/ppermute | solution.py:342
  90.8 2.6 %kernel_grad_coarse.1 = bf16[3456,128]{1,0:T(8,128)(2,1)S(1)} custom-call(bf16[4,384,1280]{2,1,0:T(8,128)(2,1)S(1)} %get-tuple-element.97.windows, bf16[256,1024]{1,0:T(8,128)(2,1)S(1)} %bitcast.37), custom_call_target="tpu_custom_call" | custom-call | flops 6000000000 | bytes 4194304 | tf_op jit(solution)/shard_map/kernel_grad_coarse/pallas_call | solution.py:515
  93.5 4.7 %collective-permute-start.11 = (bf16[1728,128]{1,0:T(8,128)(2,1)S(1)}, bf16[1728,128]{1,0:T(8,128)(2,1)S(1)}, u32[]{:S(2)}, u32[]{:S(2)}) collective-permute-start(bf16[1728,128]{1,0:T(8,128)(2,1)S(1)} %broadcast_select_fusion.2), channel_id=1, source_target_pairs={{0,2},{2,0},{4,6},{6,4},{8,10},{10,8},{12,14},{14,12},{16,18},{18,... | collective-permute-start | bytes 1327112 | tf_op jit(solution)/shard_map/ppermute | solution.py:365
  98.2 3.0 %backward_coarse.1 = (f32[2,64,1024]{2,1,0:T(8,128)S(1)}, bf16[2,64,1024]{2,1,0:T(8,128)(2,1)S(1)}) custom-call(bf16[2,128,1024]{2,1,0:T(8,128)(2,1)S(1)} %get-tuple-element.98.grads, bf16[128,1024]{1,0:T(8,128)(2,1)S(1)} %collective-permute-done.9.low, bf16[128,1024]{1,0:T(8,128)(2,1)S(1)} %collective-permute-done.10.high, ...), custom_call_target="tpu_custom_call" | custom-call | flops 5000000000 | bytes 4194304 | tf_op jit(solution)/shard_map/backward_coarse/pallas_call | solution.py:418
  101.4 1.5 collective-permute-start.12
  103.0 2.4 %collective-permute-start.13 = (bf16[864,128]{1,0:T(8,128)(2,1)S(1)}, bf16[864,128]{1,0:T(8,128)(2,1)S(1)}, u32[]{:S(2)}, u32[]{:S(2)}) collective-permute-start(bf16[864,128]{1,0:T(8,128)(2,1)S(1)} %broadcast_select_fusion.5), channel_id=1, source_target_pairs={{0,4},{2,6},{4,0},{6,2},{8,12},{10,14},{12,8},{14,10},{16,20},{18,... | collective-permute-start | bytes 663560 | tf_op jit(solution)/shard_map/ppermute | solution.py:365
  105.3 5.8 %collective-permute-done.13 = bf16[864,128]{1,0:T(8,128)(2,1)S(1)} collective-permute-done((bf16[864,128]{1,0:T(8,128)(2,1)S(1)}, bf16[864,128]{1,0:T(8,128)(2,1)S(1)}, u32[]{:S(2)}, u32[]{:S(2)}) %collective-permute-start.13) | collective-permute-done | bytes 221216 | tf_op jit(solution)/shard_map/ppermute | solution.py:365
  111.3 1.4 grad_fine.1
  112.7 1.7 collective-permute-start.16
  114.4 1.3 collective-permute-start.14
  115.8 1.5 collective-permute-start.15
  117.3 12.3 %kernel_grad_fine.1 = bf16[1728,64]{1,0:T(8,128)(2,1)S(1)} custom-call(s32[1]{0:T(128)} %bitcast.filt, bf16[4,32,4096]{2,1,0:T(8,128)(2,1)S(1)} %bitcast.34, bf16[32,4096]{1,0:T(8,128)(2,1)} %collective-permute-done.low, bf16[32,4096]{1,0:T(8,128)(2,1)} %collective-permute-done.1.high, bf16[2,32,4096]{2,1,0:T(8,128)(2,1)S(1)} %collective-permute-done.2.edge, ...), custom_call_target="tpu_custom_call" | custom-call | flops 15000000512 | bytes 4194304 | tf_op jit(solution)/shard_map/kernel_grad_fine/pallas_call | solution.py:418
  131.7 6.5 %collective-permute-start.18 = (bf16[864,128]{1,0:T(8,128)(2,1)S(1)}, bf16[864,128]{1,0:T(8,128)(2,1)S(1)}, u32[]{:S(2)}, u32[]{:S(2)}) collective-permute-start(bf16[864,128]{1,0:T(8,128)(2,1)S(1)} %add_convert_fusion.2), channel_id=1, source_target_pairs={{0,16},{2,18},{4,20},{6,22},{8,24},{10,26},{12,28},{14,30},{16,0},... | collective-permute-start | bytes 663560 | tf_op jit(solution)/shard_map/ppermute | solution.py:365
  138.3 1.6 copy-done.9
  139.9 4.1 %backward_fine_0.1 = (f32[4,32,1024]{2,1,0:T(8,128)S(1)}, bf16[4,32,1024]{2,1,0:T(8,128)(2,1)S(1)}) custom-call(bf16[4,64,4096]{2,1,0:T(8,128)(2,1)S(1)} %copy-done.9, bf16[64,4096]{1,0:T(8,128)(2,1)S(1)} %collective-permute-done.14.low, bf16[64,4096]{1,0:T(8,128)(2,1)} %collective-permute-done.15.high, bf16[3,192,192]{2,1,0:T(8,128)(2,1)S(1)} %copy-done), custom_call_target="tpu_custom_call" | custom-call | flops 6000000000 | bytes 4194304 | tf_op jit(solution)/shard_map/backward_fine_0/pallas_call | solution.py:418
  144.0 3.6 %collective-permute-done.18 = bf16[864,128]{1,0:T(8,128)(2,1)S(1)} collective-permute-done((bf16[864,128]{1,0:T(8,128)(2,1)S(1)}, bf16[864,128]{1,0:T(8,128)(2,1)S(1)}, u32[]{:S(2)}, u32[]{:S(2)}) %collective-permute-start.18) | collective-permute-done | bytes 221216 | tf_op jit(solution)/shard_map/ppermute | solution.py:365
  148.3 1.5 collective-permute-start.20
  151.0 4.1 %backward_fine_1.1 = (f32[4,32,1024]{2,1,0:T(8,128)S(1)}, bf16[4,32,1024]{2,1,0:T(8,128)(2,1)S(1)}) custom-call(bf16[4,64,4096]{2,1,0:T(8,128)(2,1)S(1)} %copy-done.9, bf16[64,4096]{1,0:T(8,128)(2,1)S(1)} %collective-permute-done.14.low, bf16[64,4096]{1,0:T(8,128)(2,1)} %collective-permute-done.15.high, bf16[3,192,192]{2,1,0:T(8,128)(2,1)S(1)} %copy-done), custom_call_target="tpu_custom_call" | custom-call | flops 6000000000 | bytes 4194304 | tf_op jit(solution)/shard_map/backward_fine_1/pallas_call | solution.py:418
  157.9 4.2 %backward_fine_2.1 = (f32[4,32,1024]{2,1,0:T(8,128)S(1)}, bf16[4,32,1024]{2,1,0:T(8,128)(2,1)S(1)}) custom-call(bf16[4,64,4096]{2,1,0:T(8,128)(2,1)S(1)} %copy-done.9, bf16[64,4096]{1,0:T(8,128)(2,1)S(1)} %collective-permute-done.14.low, bf16[64,4096]{1,0:T(8,128)(2,1)} %collective-permute-done.15.high, bf16[3,192,192]{2,1,0:T(8,128)(2,1)S(1)} %copy-done), custom_call_target="tpu_custom_call" | custom-call | flops 6000000000 | bytes 4194304 | tf_op jit(solution)/shard_map/backward_fine_2/pallas_call | solution.py:418
  162.1 3.2 %collective-permute-done.22 = bf16[4,32,1024]{2,1,0:T(8,128)(2,1)S(1)} collective-permute-done((bf16[4,32,1024]{2,1,0:T(8,128)(2,1)S(1)}, bf16[4,32,1024]{2,1,0:T(8,128)(2,1)S(1)}, u32[]{:S(2)}, u32[]{:S(2)}) %collective-permute-start.22) | collective-permute-done | bytes 262176 | tf_op jit(solution)/shard_map/ppermute | solution.py:351
  166.2 2.8 %collective-permute-start.26 = (bf16[224,128]{1,0:T(8,128)(2,1)S(1)}, bf16[224,128]{1,0:T(8,128)(2,1)S(1)}, u32[]{:S(2)}, u32[]{:S(2)}) collective-permute-start(bf16[224,128]{1,0:T(8,128)(2,1)S(1)} %add_convert_fusion.6), channel_id=1, source_target_pairs={{0,16},{2,18},{4,20},{6,22},{8,24},{10,26},{12,28},{14,30},{16,0},... | collective-permute-start | bytes 172040 | tf_op jit(solution)/shard_map/ppermute | solution.py:365
  169.0 4.4 %backward_fine_3.1 = (f32[4,32,1024]{2,1,0:T(8,128)S(1)}, bf16[4,32,1024]{2,1,0:T(8,128)(2,1)S(1)}) custom-call(bf16[4,64,4096]{2,1,0:T(8,128)(2,1)S(1)} %copy-done.9, bf16[64,4096]{1,0:T(8,128)(2,1)S(1)} %collective-permute-done.14.low, bf16[64,4096]{1,0:T(8,128)(2,1)} %collective-permute-done.15.high, bf16[3,192,192]{2,1,0:T(8,128)(2,1)S(1)} %copy-done), custom_call_target="tpu_custom_call" | custom-call | flops 6000000000 | bytes 4194304 | tf_op jit(solution)/shard_map/backward_fine_3/pallas_call | solution.py:418
  175.5 2.1 %collective-permute-done.28 = bf16[224,128]{1,0:T(8,128)(2,1)S(1)} collective-permute-done((bf16[224,128]{1,0:T(8,128)(2,1)S(1)}, bf16[224,128]{1,0:T(8,128)(2,1)S(1)}, u32[]{:S(2)}, u32[]{:S(2)}) %collective-permute-start.28) | collective-permute-done | bytes 57376 | tf_op jit(solution)/shard_map/ppermute | solution.py:365
  177.7 1.3 convert_multiply_fusion
  184.4 3.5 %collective-permute-done.27 = bf16[4,32,1024]{2,1,0:T(8,128)(2,1)} collective-permute-done((bf16[4,32,1024]{2,1,0:T(8,128)(2,1)S(1)}, bf16[4,32,1024]{2,1,0:T(8,128)(2,1)}, u32[]{:S(2)}, u32[]{:S(2)}) %collective-permute-start.27) | collective-permute-done | bytes 262176 | tf_op jit(solution)/shard_map/ppermute | solution.py:351
  189.1 2.7 %copy.32 = f32[32,4,4096]{2,1,0:T(4,128)} copy(f32[32,4,4096]{2,0,1:T(8,128)S(1)} %maximum_bitcast_fusion) | data formatting | bytes 4194304
  (113 shorter events, 30.8 us)
Async XLA Ops:
  2.4 9.1 %copy-start.17 = (bf16[1728,64]{0,1:T(8,128)(2,1)S(1)}, bf16[1728,64]{0,1:T(8,128)(2,1)}, u32[]{:S(2)}) copy-start(bf16[1728,64]{0,1:T(8,128)(2,1)} %param.8) | copy-start | bytes 663556
  4.2 21.4 %collective-permute-start.2 = (bf16[2,32,4096]{2,1,0:T(8,128)(2,1)}, bf16[2,32,4096]{2,1,0:T(8,128)(2,1)S(1)}, u32[]{:S(2)}, u32[]{:S(2)}) collective-permute-start(bf16[2,32,4096]{2,1,0:T(8,128)(2,1)} %pad_maximum_fusion), channel_id=1, source_target_pairs={{0,1},{1,0},{2,3},{3,2},{4,5},{5,4},{6,7},{7,6},{8,9},{9,8},{10,11... | collective-permute-start | bytes 1572872 | tf_op jit(solution)/shard_map/ppermute | solution.py:351
  8.0 32.9 %collective-permute-start.3 = (bf16[2,32,4096]{2,1,0:T(8,128)(2,1)}, bf16[2,32,4096]{2,1,0:T(8,128)(2,1)S(1)}, u32[]{:S(2)}, u32[]{:S(2)}) collective-permute-start(bf16[2,32,4096]{2,1,0:T(8,128)(2,1)} %slice.89), channel_id=1, source_target_pairs={{0,1},{1,0},{2,3},{3,2},{4,5},{5,4},{6,7},{7,6},{8,9},{9,8},{10,11... | collective-permute-start | bytes 1572872 | tf_op jit(solution)/shard_map/ppermute | solution.py:351
  8.0 32.9 %collective-permute-start = (bf16[32,4096]{1,0:T(8,128)(2,1)}, bf16[32,4096]{1,0:T(8,128)(2,1)}, u32[]{:S(2)}, u32[]{:S(2)}) collective-permute-start(bf16[32,4096]{1,0:T(8,128)(2,1)} %get-tuple-element.185), channel_id=1, source_target_pairs={{0,2},{2,4},{4,6},{6,8},{8,10},{10,12},{12,14},{14,16},{16,18},{18... | collective-permute-start | bytes 786440 | tf_op jit(solution)/shard_map/ppermute | solution.py:342
  10.2 30.7 %collective-permute-start.1 = (bf16[32,4096]{1,0:T(8,128)(2,1)}, bf16[32,4096]{1,0:T(8,128)(2,1)}, u32[]{:S(2)}, u32[]{:S(2)}) collective-permute-start(bf16[32,4096]{1,0:T(8,128)(2,1)} %get-tuple-element.186), channel_id=1, source_target_pairs={{2,0},{4,2},{6,4},{8,6},{10,8},{12,10},{14,12},{16,14},{18,16},{20... | collective-permute-start | bytes 786440 | tf_op jit(solution)/shard_map/ppermute | solution.py:347
  11.8 21.1 %copy-start.15 = (bf16[3,3,3,64,64]{3,2,1,0,4:T(4,128)(2,1)}, bf16[3,3,3,64,64]{3,2,1,0,4:T(4,128)(2,1)S(1)}, u32[]{:S(2)}) copy-start(bf16[3,3,3,64,64]{3,2,1,0,4:T(4,128)(2,1)S(1)} %reshape.51) | copy-start | bytes 663556
  26.5 14.5 %collective-permute-start.4 = (bf16[32,4096]{1,0:T(8,128)(2,1)}, bf16[32,4096]{1,0:T(8,128)(2,1)}, u32[]{:S(2)}, u32[]{:S(2)}) collective-permute-start(bf16[32,4096]{1,0:T(8,128)(2,1)} %get-tuple-element.191), channel_id=1, source_target_pairs={{0,2},{2,4},{4,6},{6,8},{8,10},{10,12},{12,14},{14,16},{16,18},{18... | collective-permute-start | bytes 786440 | tf_op jit(solution)/shard_map/ppermute | solution.py:342
  31.6 9.3 %collective-permute-start.5 = (bf16[32,4096]{1,0:T(8,128)(2,1)}, bf16[32,4096]{1,0:T(8,128)(2,1)}, u32[]{:S(2)}, u32[]{:S(2)}) collective-permute-start(bf16[32,4096]{1,0:T(8,128)(2,1)} %get-tuple-element.190), channel_id=1, source_target_pairs={{2,0},{4,2},{6,4},{8,6},{10,8},{12,10},{14,12},{16,14},{18,16},{20... | collective-permute-start | bytes 786440 | tf_op jit(solution)/shard_map/ppermute | solution.py:347
  34.6 6.4 %copy-start.12 = (bf16[256,128]{1,0:T(8,128)(2,1)S(1)}, bf16[256,128]{1,0:T(8,128)(2,1)}, u32[]{:S(2)}) copy-start(bf16[256,128]{1,0:T(8,128)(2,1)} %constant.26.clone.pool) | copy-start | bytes 196612
  40.9 14.5 %copy-start.5 = (bf16[2,32,4096]{2,1,0:T(8,128)(2,1)}, bf16[2,32,4096]{2,1,0:T(8,128)(2,1)S(1)}, u32[]{:S(2)}) copy-start(bf16[2,32,4096]{2,1,0:T(8,128)(2,1)S(1)} %collective-permute-done.3.middle) | copy-start | bytes 1572868
  55.4 1.3 copy-start.13
  56.7 16.9 %copy-start.7 = (bf16[128,1,256]{2,0,1:T(8,128)(2,1)S(1)}, bf16[128,1,256]{2,0,1:T(8,128)(2,1)}, u32[]{:S(2)}) copy-start(bf16[128,1,256]{2,0,1:T(8,128)(2,1)} %param.10) | copy-start | bytes 196612
  56.7 8.5 %collective-permute-start.6 = (bf16[2,64,1024]{2,1,0:T(8,128)(2,1)S(1)}, bf16[2,64,1024]{2,1,0:T(8,128)(2,1)S(1)}, u32[]{:S(2)}, u32[]{:S(2)}) collective-permute-start(bf16[2,64,1024]{2,1,0:T(8,128)(2,1)S(1)} %get-tuple-element.91.own), channel_id=1, source_target_pairs={{0,1},{1,0},{2,3},{3,2},{4,5},{5,4},{6,7},{7,6},{8,9},{9,8},{10,11... | collective-permute-start | bytes 786440 | tf_op jit(solution)/shard_map/ppermute | solution.py:351
  58.3 0.7 copy-start.1
  65.3 6.6 %copy-start.3 = (bf16[2,64,1024]{2,1,0:T(8,128)(2,1)}, bf16[2,64,1024]{2,1,0:T(8,128)(2,1)S(1)}, u32[]{:S(2)}) copy-start(bf16[2,64,1024]{2,1,0:T(8,128)(2,1)S(1)} %collective-permute-done.6.peer) | copy-start | bytes 786436
  66.1 7.5 %collective-permute-start.8 = (bf16[2,64,1024]{2,1,0:T(8,128)(2,1)}, bf16[2,64,1024]{2,1,0:T(8,128)(2,1)}, u32[]{:S(2)}, u32[]{:S(2)}) collective-permute-start(bf16[2,64,1024]{2,1,0:T(8,128)(2,1)} %pad_maximum_fusion.3), channel_id=1, source_target_pairs={{2,0},{4,2},{6,4},{8,6},{10,8},{12,10},{14,12},{16,14},{18,16},{20... | collective-permute-start | bytes 786440 | tf_op jit(solution)/shard_map/ppermute | solution.py:347
  68.1 5.5 %collective-permute-start.7 = (bf16[2,64,1024]{2,1,0:T(8,128)(2,1)}, bf16[2,64,1024]{2,1,0:T(8,128)(2,1)}, u32[]{:S(2)}, u32[]{:S(2)}) collective-permute-start(bf16[2,64,1024]{2,1,0:T(8,128)(2,1)} %pad_maximum_fusion.2), channel_id=1, source_target_pairs={{0,2},{2,4},{4,6},{6,8},{8,10},{10,12},{12,14},{14,16},{16,18},{18... | collective-permute-start | bytes 786440 | tf_op jit(solution)/shard_map/ppermute | solution.py:342
  73.7 1.0 copy-start.2
  74.6 0.9 copy-start.4
  75.6 1.0 copy-start.10
  81.3 12.2 %collective-permute-start.10 = (bf16[128,1024]{1,0:T(8,128)(2,1)S(1)}, bf16[128,1024]{1,0:T(8,128)(2,1)S(1)}, u32[]{:S(2)}, u32[]{:S(2)}) collective-permute-start(bf16[128,1024]{1,0:T(8,128)(2,1)S(1)} %get-tuple-element.95), channel_id=1, source_target_pairs={{2,0},{4,2},{6,4},{8,6},{10,8},{12,10},{14,12},{16,14},{18,16},{20... | collective-permute-start | bytes 786440 | tf_op jit(solution)/shard_map/ppermute | solution.py:347
  82.6 10.9 %collective-permute-start.9 = (bf16[128,1024]{1,0:T(8,128)(2,1)S(1)}, bf16[128,1024]{1,0:T(8,128)(2,1)S(1)}, u32[]{:S(2)}, u32[]{:S(2)}) collective-permute-start(bf16[128,1024]{1,0:T(8,128)(2,1)S(1)} %get-tuple-element.94), channel_id=1, source_target_pairs={{0,2},{2,4},{4,6},{6,8},{8,10},{10,12},{12,14},{14,16},{16,18},{18... | collective-permute-start | bytes 786440 | tf_op jit(solution)/shard_map/ppermute | solution.py:342
  93.5 7.7 %collective-permute-start.11 = (bf16[1728,128]{1,0:T(8,128)(2,1)S(1)}, bf16[1728,128]{1,0:T(8,128)(2,1)S(1)}, u32[]{:S(2)}, u32[]{:S(2)}) collective-permute-start(bf16[1728,128]{1,0:T(8,128)(2,1)S(1)} %broadcast_select_fusion.2), channel_id=1, source_target_pairs={{0,2},{2,0},{4,6},{6,4},{8,10},{10,8},{12,14},{14,12},{16,18},{18,... | collective-permute-start | bytes 1327112 | tf_op jit(solution)/shard_map/ppermute | solution.py:365
  101.2 10.1 %copy-start.11 = (bf16[128,256]{1,0:T(8,128)(2,1)S(1)}, bf16[128,256]{1,0:T(8,128)(2,1)}, u32[]{:S(2)}) copy-start(bf16[128,256]{1,0:T(8,128)(2,1)} %constant.27.clone.unpool) | copy-start | bytes 196612
  101.2 10.1 %copy-start.14 = (bf16[4,64,4096]{2,1,0:T(8,128)(2,1)S(1)}, bf16[4,64,4096]{2,1,0:T(8,128)(2,1)}, u32[]{:S(2)}) copy-start(bf16[4,64,4096]{2,1,0:T(8,128)(2,1)} %copy-done.13) | copy-start | bytes 6291460
  101.4 9.7 %collective-permute-start.12 = (bf16[2,64,1024]{2,1,0:T(8,128)(2,1)S(1)}, bf16[2,64,1024]{2,1,0:T(8,128)(2,1)S(1)}, u32[]{:S(2)}, u32[]{:S(2)}) collective-permute-start(bf16[2,64,1024]{2,1,0:T(8,128)(2,1)S(1)} %get-tuple-element.108), channel_id=1, source_target_pairs={{0,1},{1,0},{2,3},{3,2},{4,5},{5,4},{6,7},{7,6},{8,9},{9,8},{10,11... | collective-permute-start | bytes 786440 | tf_op jit(solution)/shard_map/ppermute | solution.py:351
  103.0 8.2 %collective-permute-start.13 = (bf16[864,128]{1,0:T(8,128)(2,1)S(1)}, bf16[864,128]{1,0:T(8,128)(2,1)S(1)}, u32[]{:S(2)}, u32[]{:S(2)}) collective-permute-start(bf16[864,128]{1,0:T(8,128)(2,1)S(1)} %broadcast_select_fusion.5), channel_id=1, source_target_pairs={{0,4},{2,6},{4,0},{6,2},{8,12},{10,14},{12,8},{14,10},{16,20},{18,... | collective-permute-start | bytes 663560 | tf_op jit(solution)/shard_map/ppermute | solution.py:365
  111.3 6.0 %copy-start.6 = (bf16[2,32,4096]{2,1,0:T(8,128)(2,1)S(1)}, bf16[2,32,4096]{2,1,0:T(8,128)(2,1)}, u32[]{:S(2)}) copy-start(bf16[2,32,4096]{2,1,0:T(8,128)(2,1)} %copy-done.5) | copy-start | bytes 1572868
  112.7 16.8 %copy-start.8 = (bf16[4,64,4096]{2,1,0:T(8,128)(2,1)}, bf16[4,64,4096]{2,1,0:T(8,128)(2,1)S(1)}, u32[]{:S(2)}) copy-start(bf16[4,64,4096]{2,1,0:T(8,128)(2,1)S(1)} %get-tuple-element.164.grads) | copy-start | bytes 6291460
  112.7 16.9 %collective-permute-start.16 = (bf16[864,128]{1,0:T(8,128)(2,1)S(1)}, bf16[864,128]{1,0:T(8,128)(2,1)S(1)}, u32[]{:S(2)}, u32[]{:S(2)}) collective-permute-start(bf16[864,128]{1,0:T(8,128)(2,1)S(1)} %add_convert_fusion.3), channel_id=1, source_target_pairs={{0,8},{2,10},{4,12},{6,14},{8,0},{10,2},{12,4},{14,6},{16,24},{18,... | collective-permute-start | bytes 663560 | tf_op jit(solution)/shard_map/ppermute | solution.py:365
  114.4 17.3 %collective-permute-start.14 = (bf16[64,4096]{1,0:T(8,128)(2,1)}, bf16[64,4096]{1,0:T(8,128)(2,1)S(1)}, u32[]{:S(2)}, u32[]{:S(2)}) collective-permute-start(bf16[64,4096]{1,0:T(8,128)(2,1)} %get-tuple-element.113), channel_id=1, source_target_pairs={{0,2},{2,4},{4,6},{6,8},{8,10},{10,12},{12,14},{14,16},{16,18},{18... | collective-permute-start | bytes 1572872 | tf_op jit(solution)/shard_map/ppermute | solution.py:342
  115.8 16.0 %collective-permute-start.15 = (bf16[64,4096]{1,0:T(8,128)(2,1)}, bf16[64,4096]{1,0:T(8,128)(2,1)}, u32[]{:S(2)}, u32[]{:S(2)}) collective-permute-start(bf16[64,4096]{1,0:T(8,128)(2,1)} %get-tuple-element.114), channel_id=1, source_target_pairs={{2,0},{4,2},{6,4},{8,6},{10,8},{12,10},{14,12},{16,14},{18,16},{20... | collective-permute-start | bytes 1572872 | tf_op jit(solution)/shard_map/ppermute | solution.py:347
  129.6 8.7 %copy-start = (bf16[3,192,192]{2,1,0:T(8,128)(2,1)S(1)}, bf16[3,192,192]{2,1,0:T(8,128)(2,1)}, u32[]{:S(2)}) copy-start(bf16[3,192,192]{2,1,0:T(8,128)(2,1)} %reshape.54.weights) | copy-start | bytes 663556
  131.7 15.8 %collective-permute-start.18 = (bf16[864,128]{1,0:T(8,128)(2,1)S(1)}, bf16[864,128]{1,0:T(8,128)(2,1)S(1)}, u32[]{:S(2)}, u32[]{:S(2)}) collective-permute-start(bf16[864,128]{1,0:T(8,128)(2,1)S(1)} %add_convert_fusion.2), channel_id=1, source_target_pairs={{0,16},{2,18},{4,20},{6,22},{8,24},{10,26},{12,28},{14,30},{16,0},... | collective-permute-start | bytes 663560 | tf_op jit(solution)/shard_map/ppermute | solution.py:365
  138.3 5.7 %collective-permute-start.17 = (bf16[448,128]{1,0:T(8,128)(2,1)S(1)}, bf16[448,128]{1,0:T(8,128)(2,1)S(1)}, u32[]{:S(2)}, u32[]{:S(2)}) collective-permute-start(bf16[448,128]{1,0:T(8,128)(2,1)S(1)} %broadcast_select_fusion.8), channel_id=1, source_target_pairs={{0,2},{2,0},{4,6},{6,4},{8,10},{10,8},{12,14},{14,12},{16,18},{18,... | collective-permute-start | bytes 344072 | tf_op jit(solution)/shard_map/ppermute | solution.py:365
  138.3 1.6 copy-start.9
  147.7 8.6 %collective-permute-start.21 = (bf16[864,128]{1,0:T(8,128)(2,1)S(1)}, bf16[864,128]{1,0:T(8,128)(2,1)S(1)}, u32[]{:S(2)}, u32[]{:S(2)}) collective-permute-start(bf16[864,128]{1,0:T(8,128)(2,1)S(1)} %add_convert_fusion.1), channel_id=1, source_target_pairs={{0,4},{2,6},{4,0},{6,2},{8,12},{10,14},{12,8},{14,10},{16,20},{18,... | collective-permute-start | bytes 663560 | tf_op jit(solution)/shard_map/ppermute | solution.py:365
  148.3 8.1 %collective-permute-start.20 = (bf16[224,128]{1,0:T(8,128)(2,1)S(1)}, bf16[224,128]{1,0:T(8,128)(2,1)S(1)}, u32[]{:S(2)}, u32[]{:S(2)}) collective-permute-start(bf16[224,128]{1,0:T(8,128)(2,1)S(1)} %broadcast_select_fusion.11), channel_id=1, source_target_pairs={{0,4},{2,6},{4,0},{6,2},{8,12},{10,14},{12,8},{14,10},{16,20},{18,... | collective-permute-start | bytes 172040 | tf_op jit(solution)/shard_map/ppermute | solution.py:365
  149.8 12.2 %collective-permute-start.19 = (bf16[4,32,1024]{2,1,0:T(8,128)(2,1)S(1)}, bf16[4,32,1024]{2,1,0:T(8,128)(2,1)S(1)}, u32[]{:S(2)}, u32[]{:S(2)}) collective-permute-start(bf16[4,32,1024]{2,1,0:T(8,128)(2,1)S(1)} %get-tuple-element.138), channel_id=1, source_target_pairs={{0,1},{1,0},{2,3},{3,2},{4,5},{5,4},{6,7},{7,6},{8,9},{9,8},{10,11... | collective-permute-start | bytes 786440 | tf_op jit(solution)/shard_map/ppermute | solution.py:351
  156.5 9.7 %collective-permute-start.24 = (bf16[1728,128]{1,0:T(8,128)(2,1)S(1)}, bf16[1728,128]{1,0:T(8,128)(2,1)S(1)}, u32[]{:S(2)}, u32[]{:S(2)}) collective-permute-start(bf16[1728,128]{1,0:T(8,128)(2,1)S(1)} %pad_maximum_fusion.1), channel_id=1, source_target_pairs={{0,2},{2,0},{4,6},{6,4},{8,10},{10,8},{12,14},{14,12},{16,18},{18,... | collective-permute-start | bytes 1327112 | tf_op jit(solution)/shard_map/ppermute | solution.py:365
  156.6 9.6 %collective-permute-start.23 = (bf16[224,128]{1,0:T(8,128)(2,1)S(1)}, bf16[224,128]{1,0:T(8,128)(2,1)S(1)}, u32[]{:S(2)}, u32[]{:S(2)}) collective-permute-start(bf16[224,128]{1,0:T(8,128)(2,1)S(1)} %add_convert_fusion.7), channel_id=1, source_target_pairs={{0,8},{2,10},{4,12},{6,14},{8,0},{10,2},{12,4},{14,6},{16,24},{18,... | collective-permute-start | bytes 172040 | tf_op jit(solution)/shard_map/ppermute | solution.py:365
  156.6 8.6 %collective-permute-start.22 = (bf16[4,32,1024]{2,1,0:T(8,128)(2,1)S(1)}, bf16[4,32,1024]{2,1,0:T(8,128)(2,1)S(1)}, u32[]{:S(2)}, u32[]{:S(2)}) collective-permute-start(bf16[4,32,1024]{2,1,0:T(8,128)(2,1)S(1)} %get-tuple-element.150), channel_id=1, source_target_pairs={{0,1},{1,0},{2,3},{3,2},{4,5},{5,4},{6,7},{7,6},{8,9},{9,8},{10,11... | collective-permute-start | bytes 786440 | tf_op jit(solution)/shard_map/ppermute | solution.py:351
  166.2 7.2 %collective-permute-start.26 = (bf16[224,128]{1,0:T(8,128)(2,1)S(1)}, bf16[224,128]{1,0:T(8,128)(2,1)S(1)}, u32[]{:S(2)}, u32[]{:S(2)}) collective-permute-start(bf16[224,128]{1,0:T(8,128)(2,1)S(1)} %add_convert_fusion.6), channel_id=1, source_target_pairs={{0,16},{2,18},{4,20},{6,22},{8,24},{10,26},{12,28},{14,30},{16,0},... | collective-permute-start | bytes 172040 | tf_op jit(solution)/shard_map/ppermute | solution.py:365
  173.4 4.2 %collective-permute-start.28 = (bf16[224,128]{1,0:T(8,128)(2,1)S(1)}, bf16[224,128]{1,0:T(8,128)(2,1)S(1)}, u32[]{:S(2)}, u32[]{:S(2)}) collective-permute-start(bf16[224,128]{1,0:T(8,128)(2,1)S(1)} %add_convert_fusion.5), channel_id=1, source_target_pairs={{0,4},{2,6},{4,0},{6,2},{8,12},{10,14},{12,8},{14,10},{16,20},{18,... | collective-permute-start | bytes 172040 | tf_op jit(solution)/shard_map/ppermute | solution.py:365
  174.3 9.0 %collective-permute-start.25 = (bf16[4,32,1024]{2,1,0:T(8,128)(2,1)S(1)}, bf16[4,32,1024]{2,1,0:T(8,128)(2,1)}, u32[]{:S(2)}, u32[]{:S(2)}) collective-permute-start(bf16[4,32,1024]{2,1,0:T(8,128)(2,1)S(1)} %get-tuple-element.162), channel_id=1, source_target_pairs={{0,1},{1,0},{2,3},{3,2},{4,5},{5,4},{6,7},{7,6},{8,9},{9,8},{10,11... | collective-permute-start | bytes 786440 | tf_op jit(solution)/shard_map/ppermute | solution.py:351
  177.6 2.6 %collective-permute-start.29 = (bf16[448,128]{1,0:T(8,128)(2,1)S(1)}, bf16[448,128]{1,0:T(8,128)(2,1)S(1)}, u32[]{:S(2)}, u32[]{:S(2)}) collective-permute-start(bf16[448,128]{1,0:T(8,128)(2,1)S(1)} %pad_maximum_fusion.5), channel_id=1, source_target_pairs={{0,2},{2,0},{4,6},{6,4},{8,10},{10,8},{12,14},{14,12},{16,18},{18,... | collective-permute-start | bytes 344072 | tf_op jit(solution)/shard_map/ppermute | solution.py:365
  179.1 8.8 %collective-permute-start.27 = (bf16[4,32,1024]{2,1,0:T(8,128)(2,1)S(1)}, bf16[4,32,1024]{2,1,0:T(8,128)(2,1)}, u32[]{:S(2)}, u32[]{:S(2)}) collective-permute-start(bf16[4,32,1024]{2,1,0:T(8,128)(2,1)S(1)} %get-tuple-element.172), channel_id=1, source_target_pairs={{0,1},{1,0},{2,3},{3,2},{4,5},{5,4},{6,7},{7,6},{8,9},{9,8},{10,11... | collective-permute-start | bytes 786440 | tf_op jit(solution)/shard_map/ppermute | solution.py:351
  183.3 5.6 %copy-start.16 = (f32[4,32,1024]{2,1,0:T(8,128)S(1)}, f32[4,32,1024]{2,1,0:T(8,128)}, u32[]{:S(2)}) copy-start(f32[4,32,1024]{2,1,0:T(8,128)} %convert_add_fusion.2) | copy-start | bytes 1572868
  (1 other events, 0.7 us)
where the time goes:
time: 193 us; the launch traced here: 192 us
  starting transfers between devices  59.1 us (31%)
  Pallas kernels  55.1 us (29%)
  local copies, waits for them, and re-layouts  37.9 us (20%)
  waiting for transfers between devices  25.8 us (13%)
  other arithmetic  12.5 us (6%)
    pallas_call x6, Pallas kernels, beside(): outs, others = lax.optimization_barrier((kernel(*inputs), others))  32 us
    ppermute x12, starting transfers between devices, across(): return lax.ppermute(value, 'depth', [(i, i ^ bit) for i in range(count)])  21.1 us
    ppermute x5, starting transfers between devices, to_next(): return lax.ppermute(value, 'depth', [(i, i + 1) for i in range(count - 1)])  20.6 us
    pallas_call x1, Pallas kernels, body(): call(forward_fine_kernel, [((half_planes, mid, coarse), BF), ((planes, mi...  14.4 us
    ppermute x8, waiting for transfers between devices, swap(): return lax.ppermute(value, 'filt', [(0, 1), (1, 0)])  13 us
    unnamed x41, local copies, waits for them, and re-layouts  12.8 us
    ppermute x12, waiting for transfers between devices, across(): return lax.ppermute(value, 'depth', [(i, i ^ bit) for i in range(count)])  12.8 us
    ppermute x8, starting transfers between devices, swap(): return lax.ppermute(value, 'filt', [(0, 1), (1, 0)])  10.7 us
  transfers between devices with their start and end apart: 30, of which 7 were waited for; matrix products, arithmetic and copies ran while one was open for 18% of the time, Pallas kernels for 18%

commit v1 on v0

--- a/solution.py
+++ b/solution.py
@@ -17,6 +17,7 @@
 VMEM_LIMIT = 28 * 2**20
 TILES = HH // 4
 ROWS = 16
+EARLY = HH // 2 + 1
 
 
 def nn(a, b):
@@ -27,7 +28,7 @@
     return lax.dot_general(a, b, (((1,), (1,)), ((), ())), preferred_element_type=F32)
 
 
-def call(body, outs, name, scratch=(), scalars=0, inputs=0, gflop=1.0):
+def call(body, outs, name, scratch=(), scalars=0, inputs=0):
     specs = [pl.BlockSpec(memory_space=pltpu.SMEM)] * scalars
     specs += [pl.BlockSpec(memory_space=pltpu.VMEM)] * inputs
     return pl.pallas_call(
@@ -37,9 +38,6 @@
         out_specs=[pl.BlockSpec(memory_space=pltpu.VMEM)] * len(outs),
         scratch_shapes=list(scratch),
         compiler_params=pltpu.CompilerParams(vmem_limit_bytes=VMEM_LIMIT),
-        cost_estimate=pl.CostEstimate(
-            flops=int(gflop * 1e9), transcendentals=0, bytes_accessed=4 * 2**20
-        ),
         name=name,
     )
 
@@ -56,9 +54,7 @@
     return before, after
 
 
-def fine_rows(source, windows, plane, offset, chans, group, first, count):
-    lower = max(first - 1, 0)
-    upper = min(first + count + 1, HH)
+def fine_rows(source, windows, plane, offset, chans, group, first, lower, upper):
 
     def row(step):
         block = source(step)
@@ -75,18 +71,19 @@
     zero = jnp.zeros((chans, LANES), BF)
     for shift in range(3):
         rows = pl.ds(pl.multiple_of(shift * group + offset, 32), chans)
-        if first == 0:
+        if lower == 0 and first == 0:
             windows[plane, rows, 0:LANES] = zero
-        if first + count == HH:
-            windows[plane, rows, (count + 1) * LANES : (count + 2) * LANES] = zero
-    lax.fori_loop(0, (upper - lower) // ROWS, several, 0)
+        if upper == HH:
+            windows[plane, rows, (HH + 1 - first) * LANES : (HH + 2 - first) * LANES] = zero
+    if upper - lower >= ROWS:
+        lax.fori_loop(0, (upper - lower) // ROWS, several, 0)
     for step in range(upper - (upper - lower) % ROWS, upper):
         row(step)
 
 
-def row_of(ref):
+def row_of(ref, base=0):
     def source(step):
-        return ref[:, pl.ds(pl.multiple_of(step * LANES, LANES), LANES)]
+        return ref[:, pl.ds(pl.multiple_of((step - base) * LANES, LANES), LANES)]
 
     return source
 
@@ -127,67 +124,76 @@
     lax.fori_loop(0, count, step, 0)
 
 
-def volume_windows(filt, refs, windows):
-    own, low, high, edge, middle, peer_low, peer_high = refs
+def volume_windows(filt, refs, windows, first, count):
+    own, low, high, peer_low, peer_high, edge, early = refs[:7]
     planes, chans, _ = own.shape
     mine = pl.multiple_of(filt[0] * chans, 32)
     theirs = pl.multiple_of((1 - filt[0]) * chans, 32)
-
-    def put(ref, plane, offset):
-        fine_rows(row_of(ref), windows, plane, offset, chans, 2 * chans, 0, HH)
-
-    each(planes, lambda d: put(own.at[d], d + 1, mine))
-    each(planes - 2, lambda d: put(middle.at[d], d + 2, theirs))
-    each(2, lambda d: put(edge.at[d], 1 + d * (planes - 1), theirs))
-    put(low, 0, mine)
-    put(high, planes + 1, mine)
-    put(peer_low, 0, theirs)
-    put(peer_high, planes + 1, theirs)
-
-
-def forward_fine_kernel(filt, own, low, high, edge, middle, plow, phigh, weights, pool, pooled, slope, windows):
-    planes = own.shape[0]
-    volume_windows(filt, (own, low, high, edge, middle, plow, phigh), windows)
+    lower = max(first - 1, 0)
+    upper = min(first + count + 1, HH)
+
+    def put(source, plane, offset, start=lower, end=upper):
+        fine_rows(source, windows, plane, offset, chans, 2 * chans, first, start, end)
+
+    def inner(d):
+        if lower < EARLY:
+            put(row_of(early.at[d]), d + 2, theirs, lower, min(upper, EARLY))
+        if upper > EARLY:
+            put(row_of(refs[7].at[d], EARLY), d + 2, theirs, max(lower, EARLY), upper)
+
+    each(planes, lambda d: put(row_of(own.at[d]), d + 1, mine))
+    each(planes - 2, inner)
+    each(2, lambda d: put(row_of(edge.at[d]), 1 + d * (planes - 1), theirs))
+    put(row_of(low), 0, mine)
+    put(row_of(high), planes + 1, mine)
+    put(row_of(peer_low), 0, theirs)
+    put(row_of(peer_high), planes + 1, theirs)
+
+
+def forward_fine_kernel(first, count, volumes, filt, *refs):
+    weights, pool = refs[volumes : volumes + 2]
+    pooled, slope, windows = refs[-3:]
+    before = refs[volumes + 2] if first > 0 else None
+    planes = refs[0].shape[0]
+    volume_windows(filt, refs[:volumes], windows, first, count)
     outs = weights.shape[1] // 3
     span = 2 * LANES
+    side = slice(0, LANES) if first == 0 else slice(LANES, 2 * LANES)
 
     def chunk(j, _):
-        tops = (j * 2, HH // 2 + j * 2)
+        totals = [None] * planes
+        for p in range(planes + 2):
+            value = None
+            for kh in range(3):
+                lanes = pl.ds(pl.multiple_of((2 * j + kh) * LANES, LANES), span)
+                part = nn(weights[kh], windows[p, :, lanes])
+                value = part if value is None else value + part
+            for kd in range(3):
+                d = p - kd
+                if 0 <= d < planes:
+                    piece = value[kd * outs : (kd + 1) * outs]
+                    totals[d] = piece if totals[d] is None else totals[d] + piece
         acts = []
         for d in range(planes):
-            acts.append([None, None])
-        for side, top in enumerate(tops):
-            totals = [None] * planes
-            for p in range(planes + 2):
-                value = None
-                for kh in range(3):
-                    lanes = pl.ds(pl.multiple_of((top + kh) * LANES, LANES), span)
-                    part = nn(weights[kh], windows[p, :, lanes])
-                    value = part if value is None else value + part
-                for kd in range(3):
-                    d = p - kd
-                    if 0 <= d < planes:
-                        piece = value[kd * outs : (kd + 1) * outs]
-                        totals[d] = piece if totals[d] is None else totals[d] + piece
-            for d in range(planes):
-                pre = totals[d]
-                sigma = sigmoid(pre)
-                act = pre * sigma
-                slope[d, :, pl.ds(pl.multiple_of(top * LANES, LANES), span)] = (
-                    sigma + act * (1.0 - sigma)
-                ).astype(BF)
-                acts[d][side] = act[:, :LANES] + act[:, LANES:]
-        for d in range(0, planes, 2):
-            both = jnp.concatenate(
-                [acts[d][0] + acts[d + 1][0], acts[d][1] + acts[d + 1][1]], axis=1
-            )
+            pre = totals[d]
+            sigma = sigmoid(pre)
+            act = pre * sigma
+            slope[d, :, pl.ds(pl.multiple_of(j * span, span), span)] = (
+                sigma + act * (1.0 - sigma)
+            ).astype(BF)
+            acts.append(act[:, :LANES] + act[:, LANES:])
+        tile = pl.ds(pl.multiple_of(j * LANES, LANES), LANES)
+        for d in range(planes // 2):
+            both = acts[2 * d] + acts[2 * d + 1]
             coarse = both.astype(BF)
             rest = (both - coarse.astype(F32)).astype(BF)
-            mean = nn(coarse, pool[...]) + nn(rest, pool[...])
-            pooled[d // 2, :, pl.ds(pl.multiple_of(j * LANES, LANES), LANES)] = mean.astype(BF)
+            mean = nn(coarse, pool[side, :]) + nn(rest, pool[side, :])
+            if before is not None:
+                mean = mean + before[d, :, tile].astype(F32)
+            pooled[d, :, tile] = mean.astype(BF)
         return 0
 
-    lax.fori_loop(0, TILES, chunk, 0, unroll=2)
+    lax.fori_loop(0, count // 2, chunk, 0, unroll=2)
 
 
 def forward_coarse_kernel(filt, own, peer, low, high, weights, cot, spread, grads, windows, first_out, last_out):
@@ -241,26 +247,59 @@
     out[...] = total[...].astype(out.dtype)
 
 
-def backward_coarse_kernel(grads, low, high, weights, own, peer, windows):
+def pick(filt, value):
+    half = value.shape[0] // 2
+    first = filt[0] == 0
+    return (
+        jnp.where(first, value[:half], value[half:]),
+        jnp.where(first, value[half:], value[:half]),
+    )
+
+
+def backward_coarse_kernel(filt, grads, low, high, weights, own, peer, windows):
     planes, chans, cells = grads.shape
     refs = [low] + [grads.at[d] for d in range(planes)] + [high]
     for plane, ref in enumerate(refs):
         coarse_rows(tile_of(ref), windows, plane, 0, chans, chans)
-    half = weights.shape[1] // 2
+    rows = weights.shape[0] // 27
     span = cells // 2
     for d in range(planes):
         for start in range(0, cells, span):
             value = None
             for kd in range(3):
                 for kh in range(3):
+                    base = ((2 - kd) * 9 + (2 - kh) * 3) * rows
+                    taps = jnp.concatenate(
+                        [weights[base + k * rows : base + (k + 1) * rows, :] for k in (2, 1, 0)],
+                        axis=1,
+                    )
                     begin = start + kh * LANES
-                    part = nn(weights[kd * 3 + kh], windows[d + kd, :, begin : begin + span])
+                    part = nn(taps, windows[d + kd, :, begin : begin + span])
                     value = part if value is None else value + part
-            own[d, :, start : start + span] = value[:half]
-            peer[d, :, start : start + span] = value[half:].astype(BF)
-
-
-def grad_fine_kernel(own, peer, slope, unpool, grads, first_out, last_out):
+            mine, theirs = pick(filt, value)
+            own[d, :, start : start + span] = mine
+            peer[d, :, start : start + span] = theirs.astype(BF)
+
+
+def weights_kernel(fine, wide, fine_forward, fine_backward, wide_forward):
+    chans = fine.shape[0] // 27
+    outs = fine.shape[1]
+    for kd in range(3):
+        for kh in range(3):
+            base = (kd * 3 + kh) * 3 * chans
+            block = fine[base : base + 3 * chans, :].astype(F32).T
+            fine_forward[kh, kd * outs : (kd + 1) * outs, :] = block.astype(BF)
+            base = ((2 - kd) * 9 + (2 - kh) * 3) * chans
+            fine_backward[kh, kd * chans : (kd + 1) * chans, :] = jnp.concatenate(
+                [fine[base + k * chans : base + (k + 1) * chans, :] for k in (2, 1, 0)], axis=1
+            )
+    group = wide.shape[0] // 9
+    for k in range(9):
+        block = wide[k * group : (k + 1) * group, :].astype(F32).T
+        wide_forward[k] = block.astype(BF)
+
+
+def grad_fine_kernel(own, peer, upper, lower, unpool, grads, first_out, last_out):
     planes = own.shape[0]
     for d in range(planes):
         for j in range(TILES):
@@ -272,7 +311,10 @@
                 for a in range(2):
                     for row in (side * HH // 2 + 2 * j, side * HH // 2 + 2 * j + 1):
                         cells = slice(row * LANES, (row + 1) * LANES)
-                        value = (part * slope[2 * d + a, :, cells].astype(F32)).astype(BF)
+                        slope = lower if side else upper
+                        begin = (row - side * HH // 2) * LANES
+                        factor = slope[2 * d + a, :, begin : begin + LANES].astype(F32)
+                        value = (part * factor).astype(BF)
                         grads[2 * d + a, :, cells] = value
                         if 2 * d + a == 0:
                             first_out[:, cells] = value
@@ -280,9 +322,10 @@
                             last_out[:, cells] = value
 
 
-def kernel_grad_fine_kernel(filt, own, low, high, edge, middle, plow, phigh, grads, out, windows, total):
-    planes, _, cells = own.shape
-    volume_windows(filt, (own, low, high, edge, middle, plow, phigh), windows)
+def kernel_grad_fine_kernel(filt, *refs):
+    grads, out, windows, total = refs[-4:]
+    planes, _, cells = refs[0].shape
+    volume_windows(filt, refs[:-4], windows, 0, HH)
     group = windows.shape[1]
     outs = grads.shape[0] // planes
     seen = set()
@@ -302,17 +345,17 @@
     out[...] = total[...].astype(out.dtype)
 
 
-def backward_fine_kernel(first, count, grads, low, high, weights, own, peer, windows):
+def backward_fine_kernel(first, count, filt, grads, low, high, weights, own, peer, windows):
     planes, chans, _ = grads.shape
 
     def put(ref, plane):
-        fine_rows(row_of(ref), windows, plane, 0, chans, chans, first, count)
+        lower, upper = max(first - 1, 0), min(first + count + 1, HH)
+        fine_rows(row_of(ref), windows, plane, 0, chans, chans, first, lower, upper)
 
     each(planes, lambda d: put(grads.at[d], d + 1))
     put(low, 0)
     put(high, planes + 1)
     outs = weights.shape[1] // 3
-    half = outs // 2
     span = 2 * LANES
 
     def chunk(j, _):
@@ -330,8 +373,9 @@
                     totals[d] = piece if totals[d] is None else totals[d] + piece
         cells = pl.ds(pl.multiple_of(j * span, span), span)
         for d in range(planes):
-            own[d, :, cells] = totals[d][:half]
-            peer[d, :, cells] = totals[d][half:].astype(BF)
+            mine, theirs = pick(filt, totals[d])
+            own[d, :, cells] = mine
+            peer[d, :, cells] = theirs.astype(BF)
         return 0
 
     lax.fori_loop(0, count // 2, chunk, 0, unroll=2)
@@ -410,15 +454,16 @@
         return self.result
 
 
-def beside(sums, kernel, inputs):
+def beside(sums, kernel, inputs, swapped=()):
     sums = [one for one in sums if one.pending is not None]
     sends = [one.pending[0] for one in sums]
-    inputs, sends = lax.optimization_barrier((list(inputs), sends))
+    inputs, sends, swapped = lax.optimization_barrier((list(inputs), sends, list(swapped)))
     others = [across(send, one.pending[1]) for send, one in zip(sends, sums)]
-    outs, others = lax.optimization_barrier((kernel(*inputs), others))
+    swapped = [swap(value) for value in swapped]
+    outs, others, swapped = lax.optimization_barrier((kernel(*inputs), others, swapped))
     for one, other in zip(sums, others):
         one.take(other)
-    return outs
+    return outs, swapped
 
 
 def after(value, *others):
@@ -451,38 +496,47 @@
 
     own = volume.transpose(1, 0, 2)
     edge = swap(jnp.stack([own[0], own[planes - 1]]))
-    middle = swap(own[1 : planes - 1])
+    early = swap(own[1 : planes - 1, :, : EARLY * WW])
     low, high = to_next(own[planes - 1]), to_previous(own[0])
+    late, edge = lax.optimization_barrier((own[1 : planes - 1, :, EARLY * WW :], edge))
+    late = swap(late)
     plow, phigh = to_next(edge[1]), to_previous(edge[0])
-
-    fine = w_three.reshape(3, 3, 3, 2 * own_in, mid)
-    fine_forward = fine.transpose(1, 0, 4, 2, 3).reshape(3, 3 * mid, 6 * own_in)
-    turned = fine[::-1, ::-1, ::-1].reshape(3, 3, 3, 2, own_in, mid)
-    turned = jnp.where(filt == 0, turned, turned[:, :, :, ::-1])
-    fine_backward = turned.transpose(1, 0, 3, 4, 2, 5).reshape(3, 6 * own_in, 3 * mid)
-    wide = w_four.reshape(3, 3, 3, c_mid, outs)
-    wide_forward = wide.transpose(0, 1, 4, 2, 3).reshape(9, outs, 3 * c_mid)
-    turned = wide[::-1, ::-1, ::-1].reshape(3, 3, 3, 2, mid, outs)
-    turned = jnp.where(filt == 0, turned, turned[:, :, :, ::-1])
-    wide_backward = turned.transpose(0, 1, 3, 4, 2, 5).reshape(9, c_mid, 3 * outs)
+    volumes = (own, low, high, plow, phigh, edge, early, late)
+
+    fine_forward, fine_backward, wide_forward = call(
+        weights_kernel,
+        [
+            ((3, 3 * mid, 6 * own_in), BF),
+            ((3, 6 * own_in, 3 * mid), BF),
+            ((9, outs, 3 * c_mid), BF),
+        ],
+        "weights",
+        inputs=2,
+    )(w_three, w_four)
     pool = jnp.asarray(pool_matrix(), BF)
     unpool = jnp.asarray(pool_matrix().T, BF)
     spread = jnp.asarray(spread_matrix(HH // 4, WW // 4), BF)
 
-    fine_forward, fine_backward, wide_forward, wide_backward, middle = lax.optimization_barrier(
-        (fine_forward, fine_backward, wide_forward, wide_backward, middle)
-    )
-
+    half = HH // 2
+    part_outs = [((half_planes, mid, coarse), BF), ((planes, mid, cells // 2), BF)]
+    part_windows = pltpu.VMEM((planes + 2, 6 * own_in, (half + 2) * LANES), BF)
     fine_windows = pltpu.VMEM((planes + 2, 6 * own_in, (HH + 2) * LANES), BF)
-    pooled, slope = call(
-        forward_fine_kernel,
-        [((half_planes, mid, coarse), BF), ((planes, mid, cells), BF)],
-        "forward_fine",
-        [fine_windows],
+    pooled, slope_upper = call(
+        functools.partial(forward_fine_kernel, 0, half, 7),
+        part_outs,
+        "forward_fine_upper",
+        [part_windows],
         scalars=1,
         inputs=9,
-        gflop=17.0,
-    )(which, own, low, high, edge, middle, plow, phigh, fine_forward, pool)
+    )(which, *volumes[:7], fine_forward, pool)
+    pooled, slope_lower = call(
+        functools.partial(forward_fine_kernel, half, half, 8),
+        part_outs,
+        "forward_fine_lower",
+        [part_windows],
+        scalars=1,
+        inputs=11,
+    )(which, *volumes, fine_forward, pool, pooled)
 
     pooled_peer = swap(pooled)
     pool_low = to_next(jnp.stack([pooled[half_planes - 1], pooled_peer[half_planes - 1]]))
@@ -499,7 +553,6 @@
         "forward_coarse",
         scalars=1,
         inputs=7,
-        gflop=6.0,
     )(
         which,
         pooled,
@@ -518,32 +571,30 @@
         "kernel_grad_coarse",
         [pltpu.VMEM((27 * c_mid, outs), F32)],
         inputs=2,
-        gflop=6.0,
     )(coarse_windows, grad_four.reshape(half_planes * outs, coarse))
     coarse_sum = Sum(coarse_kernel)
-    own_back, peer_back = beside(
+    (own_back, peer_back), _ = beside(
         [coarse_sum],
         call(
             backward_coarse_kernel,
             [((half_planes, mid, coarse), F32), ((half_planes, mid, coarse), BF)],
             "backward_coarse",
             [pltpu.VMEM((half_planes + 2, 3 * outs, coarse_lanes), BF)],
+            scalars=1,
             inputs=4,
-            gflop=5.0,
         ),
-        (grad_four, four_low, four_high, wide_backward),
+        (which, grad_four, four_low, four_high, w_four),
     )
-    (peer_back,) = beside([coarse_sum], lambda value: (swap(value),), (peer_back,))
+    _, (peer_back,) = beside([coarse_sum], lambda: (), (), [peer_back])
 
     grad_three, three_first, three_last = call(
         grad_fine_kernel,
         [((planes, mid, cells), BF), ((mid, cells), BF), ((mid, cells), BF)],
         "grad_fine",
-        inputs=4,
-        gflop=3.0,
-    )(own_back, peer_back, slope, unpool)
+        inputs=5,
+    )(own_back, peer_back, slope_upper, slope_lower, unpool)
     three_low, three_high = to_next(three_last), to_previous(three_first)
-    (fine_kernel,) = beside(
+    (fine_kernel,), _ = beside(
         [coarse_sum],
         call(
             kernel_grad_fine_kernel,
@@ -551,31 +602,33 @@
             "kernel_grad_fine",
             [fine_windows, pltpu.VMEM((54 * own_in, mid), F32)],
             scalars=1,
-            inputs=8,
-            gflop=15.0,
+            inputs=9,
         ),
-        (which, own, low, high, edge, middle, plow, phigh, grad_three.reshape(planes * mid, cells)),
+        (which, *volumes, grad_three.reshape(planes * mid, cells)),
     )
 
     fine_sum = Sum(fine_kernel.reshape(27 * own_in, 2 * mid))
     parts = 4
     rows = HH // parts
-    owns, peers = [], []
+    owns, peers, theirs = [], [], []
     for part in range(parts):
-        mine, theirs = beside(
+        (mine, *theirs), came = beside(
             [fine_sum, coarse_sum],
             call(
                 functools.partial(backward_fine_kernel, part * rows, rows),
                 [((planes, own_in, rows * WW), F32), ((planes, own_in, rows * WW), BF)],
                 f"backward_fine_{part}",
                 [pltpu.VMEM((planes + 2, 3 * mid, (rows + 2) * LANES), BF)],
+                scalars=1,
                 inputs=4,
-                gflop=6.0,
             ),
-            (grad_three, three_low, three_high, fine_backward),
+            (which, grad_three, three_low, three_high, fine_backward),
+            theirs,
         )
         owns.append(mine)
-        peers.append(swap(theirs))
+        peers += came
+    _, came = beside([fine_sum, coarse_sum], lambda: (), (), theirs)
+    peers += came
     coarse_sum = coarse_sum.finish()
     fine_sum = fine_sum.finish().reshape(54 * own_in, mid)
     x_grad = jnp.concatenate([a + b.astype(F32) for a, b in zip(owns, peers)], axis=2)

time: 193 us -> 191 us (0.990)
  waiting for transfers between devices: 25.8 us -> 39.9 us
  local copies, waits for them, and re-layouts: 37.9 us -> 25.2 us
  Pallas kernels: 55.1 us -> 64.1 us
  starting transfers between devices: 59.1 us -> 53 us
  other arithmetic: 12.5 us -> 6.56 us
    pallas_call x7 -> x9, Pallas kernels: 46.4 us -> 56.6 us  [the longest x6 32.5 us: beside(): kernel(*inputs)]
    reshape x5 -> x0, local copies, waits for them, and re-layouts: 8.61 us -> none  [the longest x1 2.64 us: body(): turned.transpose(0, 1, 3, 4, 2, 5).reshape(9, c_mid, 3 * outs)]
    ppermute x8 -> x9, waiting for transfers between devices: 13 us -> 20.9 us  [swap(): return lax.ppermute(value, 'filt', [(0, 1), (1, 0)])]
    unnamed x41 -> x68, local copies, waits for them, and re-layouts: 12.8 us -> 20.3 us
    rev x3 -> x0, local copies, waits for them, and re-layouts: 7.15 us -> none  [the longest x2 4.98 us: body(): turned = fine[::-1, ::-1, ::-1].reshape(3, 3, 3, 2, own_in, mid)]
    ppermute x12, waiting for transfers between devices: 12.8 us -> 17.3 us  [across(): return lax.ppermute(value, 'depth', [(i, i ^ bit) for i in range(count)])]
    ppermute x12, starting transfers between devices: 21.1 us -> 17.3 us  [across(): return lax.ppermute(value, 'depth', [(i, i ^ bit) for i in range(count)])]
    transpose x2 -> x0, local copies, waits for them, and re-layouts: 3.31 us -> none  [the longest x1 2.11 us: body(): fine_forward = fine.transpose(1, 0, 4, 2, 3).reshape(3, 3 * mid, 6 * own_in)]
  transfers between devices with their start and end apart: 30 -> 31, of which waited for: 7 -> 11; matrix products, arithmetic and copies ran while one was open for 18% -> 7% of each run, Pallas kernels for 18% -> 25%
where the time goes in v1:
time: 191 us; the launch traced here: 190 us
  Pallas kernels  64.1 us (34%)
  starting transfers between devices  53 us (28%)
  waiting for transfers between devices  39.9 us (21%)
  local copies, waits for them, and re-layouts  25.2 us (13%)
  other arithmetic  6.56 us (3%)
    pallas_call x6, Pallas kernels, beside(): kernel(*inputs)  32.5 us
    ppermute x9, waiting for transfers between devices, swap(): return lax.ppermute(value, 'filt', [(0, 1), (1, 0)])  20.9 us
    unnamed x68, local copies, waits for them, and re-layouts  20.3 us
    ppermute x5, starting transfers between devices, to_next(): return lax.ppermute(value, 'depth', [(i, i + 1) for i in range(count - 1)])  18.3 us
    ppermute x12, starting transfers between devices, across(): return lax.ppermute(value, 'depth', [(i, i ^ bit) for i in range(count)])  17.3 us
    ppermute x12, waiting for transfers between devices, across(): return lax.ppermute(value, 'depth', [(i, i ^ bit) for i in range(count)])  17.3 us
    pallas_call x1, Pallas kernels, body(): call(functools.partial(forward_fine_kernel, half, half, 8), part_outs, 'f...  11.8 us
    pallas_call x1, Pallas kernels, body(): call(functools.partial(forward_fine_kernel, 0, half, 7), part_outs, 'forw...  11.8 us
  transfers between devices with their start and end apart: 31, of which 11 were waited for; matrix products, arithmetic and copies ran while one was open for 7% of the time, Pallas kernels for 25%

profile of v1, /device:TPU:0, one launch (start us, length us, event | category | flops | bytes accessed | tf_op | source)
XLA Modules:
  0.0 190.1 jit_solution(12119742278695803657)
XLA Ops:
  0.6 1.8 copy.18
  3.3 3.0 %collective-permute-start.2 = (bf16[2,32,4096]{2,1,0:T(8,128)(2,1)S(1)}, bf16[2,32,4096]{2,1,0:T(8,128)(2,1)S(1)}, u32[]{:S(2)}, u32[]{:S(2)}) collective-permute-start(bf16[2,32,4096]{2,1,0:T(8,128)(2,1)S(1)} %pad_maximum_fusion), channel_id=1, source_target_pairs={{0,1},{1,0},{2,3},{3,2},{4,5},{5,4},{6,7},{7,6},{8,9},{9,8},{10,11... | collective-permute-start | bytes 1572872 | tf_op jit(solution)/shard_map/ppermute | solution.py:395
  6.3 1.5 collective-permute-start
  7.8 1.3 collective-permute-start.1
  11.0 8.1 %collective-permute-done.2.refs_5_ = bf16[2,32,4096]{2,1,0:T(8,128)(2,1)S(1)} collective-permute-done((bf16[2,32,4096]{2,1,0:T(8,128)(2,1)S(1)}, bf16[2,32,4096]{2,1,0:T(8,128)(2,1)S(1)}, u32[]{:S(2)}, u32[]{:S(2)}) %collective-permute-start.2) | collective-permute-done | bytes 524320 | tf_op jit(solution)/shard_map/ppermute | solution.py:395
  20.0 2.0 %collective-permute-start.3 = (bf16[32,4096]{1,0:T(8,128)(2,1)}, bf16[32,4096]{1,0:T(8,128)(2,1)}, u32[]{:S(2)}, u32[]{:S(2)}) collective-permute-start(bf16[32,4096]{1,0:T(8,128)(2,1)} %get-tuple-element.224), channel_id=1, source_target_pairs={{0,2},{2,4},{4,6},{6,8},{8,10},{10,12},{12,14},{14,16},{16,18},{18... | collective-permute-start | bytes 786440 | tf_op jit(solution)/shard_map/ppermute | solution.py:386
  21.9 1.3 collective-permute-start.4
  23.2 2.1 %collective-permute-start.6 = (bf16[2,32,1920]{2,1,0:T(8,128)(2,1)}, bf16[2,32,1920]{2,1,0:T(8,128)(2,1)}, u32[]{:S(2)}, u32[]{:S(2)}) collective-permute-start(bf16[2,32,1920]{2,1,0:T(8,128)(2,1)} %slice.93), channel_id=1, source_target_pairs={{0,1},{1,0},{2,3},{3,2},{4,5},{5,4},{6,7},{7,6},{8,9},{9,8},{10,11... | collective-permute-start | bytes 737288 | tf_op jit(solution)/shard_map/ppermute | solution.py:395
  25.4 1.9 %copy.14.fine = bf16[1728,64]{1,0:T(8,128)(2,1)} copy(bf16[1728,64]{0,1:T(8,128)(2,1)} %param.8) | data formatting | bytes 442368 | tf_op args[1]
  30.7 11.8 %forward_fine_upper.1 = (bf16[2,64,1024]{2,1,0:T(8,128)(2,1)S(1)}, bf16[4,64,2048]{2,1,0:T(8,128)(2,1)S(1)}) custom-call(s32[1]{0:T(128)} %bitcast.filt, bf16[4,32,4096]{2,1,0:T(8,128)(2,1)S(1)} %bitcast.21, bf16[32,4096]{1,0:T(8,128)(2,1)S(1)} %collective-permute-done.refs_1_, bf16[32,4096]{1,0:T(8,128)(2,1)S(1)} %collective-permute-done.1.refs_2_, ...), custom_call_target="tpu_custom_call" | custom-call | tf_op jit(solution)/shard_map/forward_fine_upper/pallas_call | solution.py:524
  43.5 11.8 %forward_fine_lower.1 = (bf16[2,64,1024]{2,1,0:T(8,128)(2,1)S(1)}, bf16[4,64,2048]{2,1,0:T(8,128)(2,1)S(1)}) custom-call(s32[1]{0:T(128)} %bitcast.filt, bf16[4,32,4096]{2,1,0:T(8,128)(2,1)S(1)} %bitcast.22, bf16[32,4096]{1,0:T(8,128)(2,1)S(1)} %collective-permute-done.refs_1_, bf16[32,4096]{1,0:T(8,128)(2,1)S(1)} %collective-permute-done.1.refs_2_, ...), custom_call_target="tpu_custom_call" | custom-call | tf_op jit(solution)/shard_map/forward_fine_lower/pallas_call | solution.py:532
  57.1 7.2 %collective-permute-done.7.peer = bf16[2,64,1024]{2,1,0:T(8,128)(2,1)S(1)} collective-permute-done((bf16[2,64,1024]{2,1,0:T(8,128)(2,1)S(1)}, bf16[2,64,1024]{2,1,0:T(8,128)(2,1)S(1)}, u32[]{:S(2)}, u32[]{:S(2)}) %collective-permute-start.7) | collective-permute-done | bytes 262176 | tf_op jit(solution)/shard_map/ppermute | solution.py:395
  64.3 1.3 collective-permute-start.9
  66.3 3.6 %collective-permute-start.8 = (bf16[2,64,1024]{2,1,0:T(8,128)(2,1)}, bf16[2,64,1024]{2,1,0:T(8,128)(2,1)S(1)}, u32[]{:S(2)}, u32[]{:S(2)}) collective-permute-start(bf16[2,64,1024]{2,1,0:T(8,128)(2,1)} %pad_maximum_fusion.2), channel_id=1, source_target_pairs={{0,2},{2,4},{4,6},{6,8},{8,10},{10,12},{12,14},{14,16},{16,18},{18... | collective-permute-start | bytes 786440 | tf_op jit(solution)/shard_map/ppermute | solution.py:386
  70.0 1.3 collective-permute-done.8.low
  72.2 1.2 copy-done.20
  74.4 3.6 %forward_coarse.1 = (bf16[2,128,1024]{2,1,0:T(8,128)(2,1)S(1)}, bf16[4,384,1280]{2,1,0:T(8,128)(2,1)S(1)}, bf16[128,1024]{1,0:T(8,128)(2,1)S(1)}, bf16[128,1024]{1,0:T(8,128)(2,1)S(1)}) custom-call(s32[1]{0:T(128)} %bitcast.filt, bf16[2,64,1024]{2,1,0:T(8,128)(2,1)S(1)} %copy-done.18, bf16[2,64,1024]{2,1,0:T(8,128)(2,1)S(1)} %collective-permute-done.7.peer, ...), custom_call_target="tpu_custom_call" | custom-call | tf_op jit(solution)/shard_map/forward_coarse/pallas_call | solution.py:545
  78.0 9.1 %collective-permute-start.10 = (bf16[128,1024]{1,0:T(8,128)(2,1)S(1)}, bf16[128,1024]{1,0:T(8,128)(2,1)S(1)}, u32[]{:S(2)}, u32[]{:S(2)}) collective-permute-start(bf16[128,1024]{1,0:T(8,128)(2,1)S(1)} %get-tuple-element.114), channel_id=1, source_target_pairs={{0,2},{2,4},{4,6},{6,8},{8,10},{10,12},{12,14},{14,16},{16,18},{18... | collective-permute-start | bytes 786440 | tf_op jit(solution)/shard_map/ppermute | solution.py:386
  87.1 1.5 collective-permute-start.11
  88.6 2.6 %kernel_grad_coarse.1 = bf16[3456,128]{1,0:T(8,128)(2,1)S(1)} custom-call(bf16[4,384,1280]{2,1,0:T(8,128)(2,1)S(1)} %get-tuple-element.116.windows, bf16[256,1024]{1,0:T(8,128)(2,1)S(1)} %bitcast.24), custom_call_target="tpu_custom_call" | custom-call | tf_op jit(solution)/shard_map/kernel_grad_coarse/pallas_call | solution.py:568
  93.1 4.8 %collective-permute-start.12 = (bf16[1728,128]{1,0:T(8,128)(2,1)}, bf16[1728,128]{1,0:T(8,128)(2,1)}, u32[]{:S(2)}, u32[]{:S(2)}) collective-permute-start(bf16[1728,128]{1,0:T(8,128)(2,1)} %broadcast_select_fusion.2), channel_id=1, source_target_pairs={{0,2},{2,0},{4,6},{6,4},{8,10},{10,8},{12,14},{14,12},{16,18},{18,... | collective-permute-start | bytes 1327112 | tf_op jit(solution)/shard_map/ppermute | solution.py:409
  99.9 3.0 %backward_coarse.1 = (f32[2,64,1024]{2,1,0:T(8,128)S(1)}, bf16[2,64,1024]{2,1,0:T(8,128)(2,1)S(1)}) custom-call(s32[1]{0:T(128)} %bitcast.filt, bf16[2,128,1024]{2,1,0:T(8,128)(2,1)S(1)} %copy-done.11, bf16[128,1024]{1,0:T(8,128)(2,1)S(1)} %collective-permute-done.10.low, bf16[128,1024]{1,0:T(8,128)(2,1)S(1)} %copy-done.25, bf16[3456,128]{1,0:T(8,128)(2,1)S(1)} %copy-done.2), custom_call_target="tpu_custom_call" | custom-call | tf_op jit(solution)/shard_map/backward_coarse/pallas_call | solution.py:463
  102.9 1.3 add_convert_fusion
  105.0 3.3 %collective-permute-start.13 = (bf16[864,128]{1,0:T(8,128)(2,1)S(1)}, bf16[864,128]{1,0:T(8,128)(2,1)S(1)}, u32[]{:S(2)}, u32[]{:S(2)}) collective-permute-start(bf16[864,128]{1,0:T(8,128)(2,1)S(1)} %broadcast_select_fusion.5), channel_id=1, source_target_pairs={{0,4},{2,6},{4,0},{6,2},{8,12},{10,14},{12,8},{14,10},{16,20},{18,... | collective-permute-start | bytes 663560 | tf_op jit(solution)/shard_map/ppermute | solution.py:409
  108.3 5.3 %collective-permute-done.13 = bf16[864,128]{1,0:T(8,128)(2,1)S(1)} collective-permute-done((bf16[864,128]{1,0:T(8,128)(2,1)S(1)}, bf16[864,128]{1,0:T(8,128)(2,1)S(1)}, u32[]{:S(2)}, u32[]{:S(2)}) %collective-permute-start.13) | collective-permute-done | bytes 221216 | tf_op jit(solution)/shard_map/ppermute | solution.py:409
  113.7 1.4 grad_fine.1
  115.1 1.6 collective-permute-start.17
  116.7 2.1 %collective-permute-start.15 = (bf16[64,4096]{1,0:T(8,128)(2,1)}, bf16[64,4096]{1,0:T(8,128)(2,1)}, u32[]{:S(2)}, u32[]{:S(2)}) collective-permute-start(bf16[64,4096]{1,0:T(8,128)(2,1)} %get-tuple-element.134), channel_id=1, source_target_pairs={{0,2},{2,4},{4,6},{6,8},{8,10},{10,12},{12,14},{14,16},{16,18},{18... | collective-permute-start | bytes 1572872 | tf_op jit(solution)/shard_map/ppermute | solution.py:386
  118.8 1.3 collective-permute-start.16
  120.1 12.0 %kernel_grad_fine.1 = bf16[1728,64]{1,0:T(8,128)(2,1)S(1)} custom-call(s32[1]{0:T(128)} %bitcast.filt, bf16[4,32,4096]{2,1,0:T(8,128)(2,1)S(1)} %bitcast.23, bf16[32,4096]{1,0:T(8,128)(2,1)S(1)} %copy-done.7, bf16[32,4096]{1,0:T(8,128)(2,1)S(1)} %copy-done.9, bf16[32,4096]{1,0:T(8,128)(2,1)} %collective-permute-done.3.refs_3_, ...), custom_call_target="tpu_custom_call" | custom-call | tf_op jit(solution)/shard_map/kernel_grad_fine/pallas_call | solution.py:463
  133.6 1.3 reshape.30
  135.1 1.1 add_convert_fusion.2
  136.3 5.2 %collective-permute-start.19 = (bf16[864,128]{1,0:T(8,128)(2,1)S(1)}, bf16[864,128]{1,0:T(8,128)(2,1)S(1)}, u32[]{:S(2)}, u32[]{:S(2)}) collective-permute-start(bf16[864,128]{1,0:T(8,128)(2,1)S(1)} %add_convert_fusion.2), channel_id=1, source_target_pairs={{0,16},{2,18},{4,20},{6,22},{8,24},{10,26},{12,28},{14,30},{16,0},... | collective-permute-start | bytes 663560 | tf_op jit(solution)/shard_map/ppermute | solution.py:409
  141.5 4.3 %backward_fine_0.1 = (f32[4,32,1024]{2,1,0:T(8,128)S(1)}, bf16[4,32,1024]{2,1,0:T(8,128)(2,1)S(1)}) custom-call(s32[1]{0:T(128)} %bitcast.filt, bf16[4,64,4096]{2,1,0:T(8,128)(2,1)S(1)} %get-tuple-element.194.grads, bf16[64,4096]{1,0:T(8,128)(2,1)} %collective-permute-done.15.low, bf16[64,4096]{1,0:T(8,128)(2,1)} %collective-permute-done.16.high, ...), custom_call_target="tpu_custom_call" | custom-call | tf_op jit(solution)/shard_map/backward_fine_0/pallas_call | solution.py:463
  145.8 6.2 %collective-permute-done.19 = bf16[864,128]{1,0:T(8,128)(2,1)S(1)} collective-permute-done((bf16[864,128]{1,0:T(8,128)(2,1)S(1)}, bf16[864,128]{1,0:T(8,128)(2,1)S(1)}, u32[]{:S(2)}, u32[]{:S(2)}) %collective-permute-start.19) | collective-permute-done | bytes 221216 | tf_op jit(solution)/shard_map/ppermute | solution.py:409
  153.6 1.5 collective-permute-start.20
  155.2 4.3 %backward_fine_1.1 = (f32[4,32,1024]{2,1,0:T(8,128)S(1)}, bf16[4,32,1024]{2,1,0:T(8,128)(2,1)S(1)}) custom-call(s32[1]{0:T(128)} %bitcast.filt, bf16[4,64,4096]{2,1,0:T(8,128)(2,1)S(1)} %get-tuple-element.194.grads, bf16[64,4096]{1,0:T(8,128)(2,1)} %collective-permute-done.15.low, bf16[64,4096]{1,0:T(8,128)(2,1)} %collective-permute-done.16.high, ...), custom_call_target="tpu_custom_call" | custom-call | tf_op jit(solution)/shard_map/backward_fine_1/pallas_call | solution.py:463
  159.5 2.0 %collective-permute-done.20 = bf16[224,128]{1,0:T(8,128)(2,1)S(1)} collective-permute-done((bf16[224,128]{1,0:T(8,128)(2,1)S(1)}, bf16[224,128]{1,0:T(8,128)(2,1)S(1)}, u32[]{:S(2)}, u32[]{:S(2)}) %collective-permute-start.20) | collective-permute-done | bytes 57376 | tf_op jit(solution)/shard_map/ppermute | solution.py:409
  161.7 1.2 collective-permute-start.25
  162.9 4.5 %backward_fine_2.1 = (f32[4,32,1024]{2,1,0:T(8,128)S(1)}, bf16[4,32,1024]{2,1,0:T(8,128)(2,1)S(1)}) custom-call(s32[1]{0:T(128)} %bitcast.filt, bf16[4,64,4096]{2,1,0:T(8,128)(2,1)S(1)} %get-tuple-element.194.grads, bf16[64,4096]{1,0:T(8,128)(2,1)} %collective-permute-done.15.low, bf16[64,4096]{1,0:T(8,128)(2,1)} %collective-permute-done.16.high, ...), custom_call_target="tpu_custom_call" | custom-call | tf_op jit(solution)/shard_map/backward_fine_2/pallas_call | solution.py:463
  167.5 2.9 %collective-permute-done.25 = bf16[4,32,1024]{2,1,0:T(8,128)(2,1)S(1)} collective-permute-done((bf16[4,32,1024]{2,1,0:T(8,128)(2,1)S(1)}, bf16[4,32,1024]{2,1,0:T(8,128)(2,1)S(1)}, u32[]{:S(2)}, u32[]{:S(2)}) %collective-permute-start.25) | collective-permute-done | bytes 262176 | tf_op jit(solution)/shard_map/ppermute | solution.py:395
  170.7 1.2 collective-permute-start.27
  171.9 1.3 convert_multiply_fusion
  173.2 4.3 %backward_fine_3.1 = (f32[4,32,1024]{2,1,0:T(8,128)S(1)}, bf16[4,32,1024]{2,1,0:T(8,128)(2,1)S(1)}) custom-call(s32[1]{0:T(128)} %bitcast.filt, bf16[4,64,4096]{2,1,0:T(8,128)(2,1)S(1)} %get-tuple-element.194.grads, bf16[64,4096]{1,0:T(8,128)(2,1)} %collective-permute-done.15.low, bf16[64,4096]{1,0:T(8,128)(2,1)} %collective-permute-done.16.high, ...), custom_call_target="tpu_custom_call" | custom-call | tf_op jit(solution)/shard_map/backward_fine_3/pallas_call | solution.py:463
  178.6 1.2 collective-permute-start.29
  180.3 3.7 %collective-permute-done.28 = bf16[224,128]{1,0:T(8,128)(2,1)S(1)} collective-permute-done((bf16[224,128]{1,0:T(8,128)(2,1)S(1)}, bf16[224,128]{1,0:T(8,128)(2,1)S(1)}, u32[]{:S(2)}, u32[]{:S(2)}) %collective-permute-start.28) | collective-permute-done | bytes 57376 | tf_op jit(solution)/shard_map/ppermute | solution.py:409
  184.0 1.6 collective-permute-done.29
  186.1 2.7 %copy.15 = f32[32,4,4096]{2,1,0:T(4,128)} copy(f32[32,4,4096]{2,0,1:T(8,128)S(1)} %maximum_bitcast_fusion) | data formatting | bytes 4194304
  (130 shorter events, 24.1 us)
Async XLA Ops:
  3.3 24.0 %copy-start.2 = (bf16[3456,128]{1,0:T(8,128)(2,1)S(1)}, bf16[3456,128]{1,0:T(8,128)(2,1)}, u32[]{:S(2)}) copy-start(bf16[3456,128]{1,0:T(8,128)(2,1)} %weights.2) | copy-start | bytes 2654212
  3.3 15.8 %collective-permute-start.2 = (bf16[2,32,4096]{2,1,0:T(8,128)(2,1)S(1)}, bf16[2,32,4096]{2,1,0:T(8,128)(2,1)S(1)}, u32[]{:S(2)}, u32[]{:S(2)}) collective-permute-start(bf16[2,32,4096]{2,1,0:T(8,128)(2,1)S(1)} %pad_maximum_fusion), channel_id=1, source_target_pairs={{0,1},{1,0},{2,3},{3,2},{4,5},{5,4},{6,7},{7,6},{8,9},{9,8},{10,11... | collective-permute-start | bytes 1572872 | tf_op jit(solution)/shard_map/ppermute | solution.py:395
  6.3 16.9 %collective-permute-start = (bf16[32,4096]{1,0:T(8,128)(2,1)S(1)}, bf16[32,4096]{1,0:T(8,128)(2,1)S(1)}, u32[]{:S(2)}, u32[]{:S(2)}) collective-permute-start(bf16[32,4096]{1,0:T(8,128)(2,1)S(1)} %get-tuple-element.218), channel_id=1, source_target_pairs={{0,2},{2,4},{4,6},{6,8},{8,10},{10,12},{12,14},{14,16},{16,18},{18... | collective-permute-start | bytes 786440 | tf_op jit(solution)/shard_map/ppermute | solution.py:386
  7.8 22.0 %collective-permute-start.1 = (bf16[32,4096]{1,0:T(8,128)(2,1)}, bf16[32,4096]{1,0:T(8,128)(2,1)S(1)}, u32[]{:S(2)}, u32[]{:S(2)}) collective-permute-start(bf16[32,4096]{1,0:T(8,128)(2,1)} %get-tuple-element.219), channel_id=1, source_target_pairs={{2,0},{4,2},{6,4},{8,6},{10,8},{12,10},{14,12},{16,14},{18,16},{20... | collective-permute-start | bytes 786440 | tf_op jit(solution)/shard_map/ppermute | solution.py:391
  9.8 19.9 %collective-permute-start.5 = (bf16[2,32,2176]{2,1,0:T(8,128)(2,1)}, bf16[2,32,2176]{2,1,0:T(8,128)(2,1)S(1)}, u32[]{:S(2)}, u32[]{:S(2)}) collective-permute-start(bf16[2,32,2176]{2,1,0:T(8,128)(2,1)} %slice.94), channel_id=1, source_target_pairs={{0,1},{1,0},{2,3},{3,2},{4,5},{5,4},{6,7},{7,6},{8,9},{9,8},{10,11... | collective-permute-start | bytes 835592 | tf_op jit(solution)/shard_map/ppermute | solution.py:395
  19.1 24.4 %copy-start = (bf16[2,32,4096]{2,1,0:T(8,128)(2,1)}, bf16[2,32,4096]{2,1,0:T(8,128)(2,1)S(1)}, u32[]{:S(2)}) copy-start(bf16[2,32,4096]{2,1,0:T(8,128)(2,1)S(1)} %collective-permute-done.2.refs_5_) | copy-start | bytes 1572868
  20.0 9.8 %collective-permute-start.3 = (bf16[32,4096]{1,0:T(8,128)(2,1)}, bf16[32,4096]{1,0:T(8,128)(2,1)}, u32[]{:S(2)}, u32[]{:S(2)}) collective-permute-start(bf16[32,4096]{1,0:T(8,128)(2,1)} %get-tuple-element.224), channel_id=1, source_target_pairs={{0,2},{2,4},{4,6},{6,8},{8,10},{10,12},{12,14},{14,16},{16,18},{18... | collective-permute-start | bytes 786440 | tf_op jit(solution)/shard_map/ppermute | solution.py:386
  21.9 7.9 %collective-permute-start.4 = (bf16[32,4096]{1,0:T(8,128)(2,1)}, bf16[32,4096]{1,0:T(8,128)(2,1)}, u32[]{:S(2)}, u32[]{:S(2)}) collective-permute-start(bf16[32,4096]{1,0:T(8,128)(2,1)} %get-tuple-element.223), channel_id=1, source_target_pairs={{2,0},{4,2},{6,4},{8,6},{10,8},{12,10},{14,12},{16,14},{18,16},{20... | collective-permute-start | bytes 786440 | tf_op jit(solution)/shard_map/ppermute | solution.py:391
  23.2 20.2 %copy-start.6 = (bf16[32,4096]{1,0:T(8,128)(2,1)}, bf16[32,4096]{1,0:T(8,128)(2,1)S(1)}, u32[]{:S(2)}) copy-start(bf16[32,4096]{1,0:T(8,128)(2,1)S(1)} %collective-permute-done.refs_1_) | copy-start | bytes 786436
  23.2 20.2 %collective-permute-start.6 = (bf16[2,32,1920]{2,1,0:T(8,128)(2,1)}, bf16[2,32,1920]{2,1,0:T(8,128)(2,1)}, u32[]{:S(2)}, u32[]{:S(2)}) collective-permute-start(bf16[2,32,1920]{2,1,0:T(8,128)(2,1)} %slice.93), channel_id=1, source_target_pairs={{0,1},{1,0},{2,3},{3,2},{4,5},{5,4},{6,7},{7,6},{8,9},{9,8},{10,11... | collective-permute-start | bytes 737288 | tf_op jit(solution)/shard_map/ppermute | solution.py:395
  28.3 15.2 %copy-start.23 = (bf16[256,128]{1,0:T(8,128)(2,1)S(1)}, bf16[256,128]{1,0:T(8,128)(2,1)}, u32[]{:S(2)}) copy-start(bf16[256,128]{1,0:T(8,128)(2,1)} %constant.26.clone.refs_8_.refs_9_) | copy-start | bytes 196612
  29.8 25.6 %copy-start.8 = (bf16[32,4096]{1,0:T(8,128)(2,1)}, bf16[32,4096]{1,0:T(8,128)(2,1)S(1)}, u32[]{:S(2)}) copy-start(bf16[32,4096]{1,0:T(8,128)(2,1)S(1)} %collective-permute-done.1.refs_2_) | copy-start | bytes 786436
  29.8 25.6 %copy-start.4 = (bf16[2,32,2176]{2,1,0:T(8,128)(2,1)}, bf16[2,32,2176]{2,1,0:T(8,128)(2,1)S(1)}, u32[]{:S(2)}) copy-start(bf16[2,32,2176]{2,1,0:T(8,128)(2,1)S(1)} %collective-permute-done.5.refs_6_) | copy-start | bytes 835588
  56.3 15.0 %copy-start.26 = (bf16[128,1,256]{2,0,1:T(8,128)(2,1)S(1)}, bf16[128,1,256]{2,0,1:T(8,128)(2,1)}, u32[]{:S(2)}) copy-start(bf16[128,1,256]{2,0,1:T(8,128)(2,1)} %param.10) | copy-start | bytes 196612
  56.3 7.9 %collective-permute-start.7 = (bf16[2,64,1024]{2,1,0:T(8,128)(2,1)S(1)}, bf16[2,64,1024]{2,1,0:T(8,128)(2,1)S(1)}, u32[]{:S(2)}, u32[]{:S(2)}) collective-permute-start(bf16[2,64,1024]{2,1,0:T(8,128)(2,1)S(1)} %get-tuple-element.111.own), channel_id=1, source_target_pairs={{0,1},{1,0},{2,3},{3,2},{4,5},{5,4},{6,7},{7,6},{8,9},{9,8},{10,11... | collective-permute-start | bytes 786440 | tf_op jit(solution)/shard_map/ppermute | solution.py:395
  64.3 5.7 %collective-permute-start.9 = (bf16[2,64,1024]{2,1,0:T(8,128)(2,1)S(1)}, bf16[2,64,1024]{2,1,0:T(8,128)(2,1)S(1)}, u32[]{:S(2)}, u32[]{:S(2)}) collective-permute-start(bf16[2,64,1024]{2,1,0:T(8,128)(2,1)S(1)} %pad_maximum_fusion.3), channel_id=1, source_target_pairs={{2,0},{4,2},{6,4},{8,6},{10,8},{12,10},{14,12},{16,14},{18,16},{20... | collective-permute-start | bytes 786440 | tf_op jit(solution)/shard_map/ppermute | solution.py:391
  66.3 5.0 %collective-permute-start.8 = (bf16[2,64,1024]{2,1,0:T(8,128)(2,1)}, bf16[2,64,1024]{2,1,0:T(8,128)(2,1)S(1)}, u32[]{:S(2)}, u32[]{:S(2)}) collective-permute-start(bf16[2,64,1024]{2,1,0:T(8,128)(2,1)} %pad_maximum_fusion.2), channel_id=1, source_target_pairs={{0,2},{2,4},{4,6},{6,8},{8,10},{10,12},{12,14},{14,16},{16,18},{18... | collective-permute-start | bytes 786440 | tf_op jit(solution)/shard_map/ppermute | solution.py:386
  78.0 13.2 %copy-start.10 = (bf16[2,128,1024]{2,1,0:T(8,128)(2,1)}, bf16[2,128,1024]{2,1,0:T(8,128)(2,1)S(1)}, u32[]{:S(2)}) copy-start(bf16[2,128,1024]{2,1,0:T(8,128)(2,1)S(1)} %get-tuple-element.118.grads) | copy-start | bytes 1572868
  78.0 14.0 %collective-permute-start.10 = (bf16[128,1024]{1,0:T(8,128)(2,1)S(1)}, bf16[128,1024]{1,0:T(8,128)(2,1)S(1)}, u32[]{:S(2)}, u32[]{:S(2)}) collective-permute-start(bf16[128,1024]{1,0:T(8,128)(2,1)S(1)} %get-tuple-element.114), channel_id=1, source_target_pairs={{0,2},{2,4},{4,6},{6,8},{8,10},{10,12},{12,14},{14,16},{16,18},{18... | collective-permute-start | bytes 786440 | tf_op jit(solution)/shard_map/ppermute | solution.py:386
  87.1 5.3 %collective-permute-start.11 = (bf16[128,1024]{1,0:T(8,128)(2,1)S(1)}, bf16[128,1024]{1,0:T(8,128)(2,1)S(1)}, u32[]{:S(2)}, u32[]{:S(2)}) collective-permute-start(bf16[128,1024]{1,0:T(8,128)(2,1)S(1)} %get-tuple-element.115), channel_id=1, source_target_pairs={{2,0},{4,2},{6,4},{8,6},{10,8},{12,10},{14,12},{16,14},{18,16},{20... | collective-permute-start | bytes 786440 | tf_op jit(solution)/shard_map/ppermute | solution.py:391
  93.1 9.8 %collective-permute-start.12 = (bf16[1728,128]{1,0:T(8,128)(2,1)}, bf16[1728,128]{1,0:T(8,128)(2,1)}, u32[]{:S(2)}, u32[]{:S(2)}) collective-permute-start(bf16[1728,128]{1,0:T(8,128)(2,1)} %broadcast_select_fusion.2), channel_id=1, source_target_pairs={{0,2},{2,0},{4,6},{6,4},{8,10},{10,8},{12,14},{14,12},{16,18},{18,... | collective-permute-start | bytes 1327112 | tf_op jit(solution)/shard_map/ppermute | solution.py:409
  102.9 10.8 %copy-start.14 = (bf16[4,64,2048]{2,1,0:T(8,128)(2,1)S(1)}, bf16[4,64,2048]{2,1,0:T(8,128)(2,1)}, u32[]{:S(2)}) copy-start(bf16[4,64,2048]{2,1,0:T(8,128)(2,1)} %copy-done.13) | copy-start | bytes 3145732
  102.9 10.8 %copy-start.16 = (bf16[4,64,2048]{2,1,0:T(8,128)(2,1)S(1)}, bf16[4,64,2048]{2,1,0:T(8,128)(2,1)}, u32[]{:S(2)}) copy-start(bf16[4,64,2048]{2,1,0:T(8,128)(2,1)} %copy-done.15) | copy-start | bytes 3145732
  102.9 10.8 %copy-start.27 = (bf16[128,256]{1,0:T(8,128)(2,1)S(1)}, bf16[128,256]{1,0:T(8,128)(2,1)}, u32[]{:S(2)}) copy-start(bf16[128,256]{1,0:T(8,128)(2,1)} %constant.27.clone.unpool) | copy-start | bytes 196612
  104.2 15.9 %copy-start.1 = (bf16[2,32,4096]{2,1,0:T(8,128)(2,1)S(1)}, bf16[2,32,4096]{2,1,0:T(8,128)(2,1)}, u32[]{:S(2)}) copy-start(bf16[2,32,4096]{2,1,0:T(8,128)(2,1)} %copy-done) | copy-start | bytes 1572868
  104.3 15.9 %copy-start.5 = (bf16[2,32,2176]{2,1,0:T(8,128)(2,1)S(1)}, bf16[2,32,2176]{2,1,0:T(8,128)(2,1)}, u32[]{:S(2)}) copy-start(bf16[2,32,2176]{2,1,0:T(8,128)(2,1)} %copy-done.4) | copy-start | bytes 835588
  104.3 15.9 %copy-start.7 = (bf16[32,4096]{1,0:T(8,128)(2,1)S(1)}, bf16[32,4096]{1,0:T(8,128)(2,1)}, u32[]{:S(2)}) copy-start(bf16[32,4096]{1,0:T(8,128)(2,1)} %copy-done.6) | copy-start | bytes 786436
  104.3 15.9 %copy-start.9 = (bf16[32,4096]{1,0:T(8,128)(2,1)S(1)}, bf16[32,4096]{1,0:T(8,128)(2,1)}, u32[]{:S(2)}) copy-start(bf16[32,4096]{1,0:T(8,128)(2,1)} %copy-done.8) | copy-start | bytes 786436
  104.3 9.3 %collective-permute-start.14 = (bf16[2,64,1024]{2,1,0:T(8,128)(2,1)S(1)}, bf16[2,64,1024]{2,1,0:T(8,128)(2,1)S(1)}, u32[]{:S(2)}, u32[]{:S(2)}) collective-permute-start(bf16[2,64,1024]{2,1,0:T(8,128)(2,1)S(1)} %get-tuple-element.129), channel_id=1, source_target_pairs={{0,1},{1,0},{2,3},{3,2},{4,5},{5,4},{6,7},{7,6},{8,9},{9,8},{10,11... | collective-permute-start | bytes 786440 | tf_op jit(solution)/shard_map/ppermute | solution.py:395
  105.0 8.6 %collective-permute-start.13 = (bf16[864,128]{1,0:T(8,128)(2,1)S(1)}, bf16[864,128]{1,0:T(8,128)(2,1)S(1)}, u32[]{:S(2)}, u32[]{:S(2)}) collective-permute-start(bf16[864,128]{1,0:T(8,128)(2,1)S(1)} %broadcast_select_fusion.5), channel_id=1, source_target_pairs={{0,4},{2,6},{4,0},{6,2},{8,12},{10,14},{12,8},{14,10},{16,20},{18,... | collective-permute-start | bytes 663560 | tf_op jit(solution)/shard_map/ppermute | solution.py:409
  113.7 18.5 %copy-start.30 = (bf16[864,128]{1,0:T(8,128)(2,1)}, bf16[864,128]{1,0:T(8,128)(2,1)S(1)}, u32[]{:S(2)}) copy-start(bf16[864,128]{1,0:T(8,128)(2,1)S(1)} %add_convert_fusion.3) | copy-start | bytes 663556
  115.1 17.0 %collective-permute-start.17 = (bf16[864,128]{1,0:T(8,128)(2,1)S(1)}, bf16[864,128]{1,0:T(8,128)(2,1)S(1)}, u32[]{:S(2)}, u32[]{:S(2)}) collective-permute-start(bf16[864,128]{1,0:T(8,128)(2,1)S(1)} %add_convert_fusion.3), channel_id=1, source_target_pairs={{0,8},{2,10},{4,12},{6,14},{8,0},{10,2},{12,4},{14,6},{16,24},{18,... | collective-permute-start | bytes 663560 | tf_op jit(solution)/shard_map/ppermute | solution.py:409
  116.7 19.5 %collective-permute-start.15 = (bf16[64,4096]{1,0:T(8,128)(2,1)}, bf16[64,4096]{1,0:T(8,128)(2,1)}, u32[]{:S(2)}, u32[]{:S(2)}) collective-permute-start(bf16[64,4096]{1,0:T(8,128)(2,1)} %get-tuple-element.134), channel_id=1, source_target_pairs={{0,2},{2,4},{4,6},{6,8},{8,10},{10,12},{12,14},{14,16},{16,18},{18... | collective-permute-start | bytes 1572872 | tf_op jit(solution)/shard_map/ppermute | solution.py:386
  118.8 17.4 %collective-permute-start.16 = (bf16[64,4096]{1,0:T(8,128)(2,1)}, bf16[64,4096]{1,0:T(8,128)(2,1)}, u32[]{:S(2)}, u32[]{:S(2)}) collective-permute-start(bf16[64,4096]{1,0:T(8,128)(2,1)} %get-tuple-element.135), channel_id=1, source_target_pairs={{2,0},{4,2},{6,4},{8,6},{10,8},{12,10},{14,12},{16,14},{18,16},{20... | collective-permute-start | bytes 1572872 | tf_op jit(solution)/shard_map/ppermute | solution.py:391
  136.3 15.8 %collective-permute-start.19 = (bf16[864,128]{1,0:T(8,128)(2,1)S(1)}, bf16[864,128]{1,0:T(8,128)(2,1)S(1)}, u32[]{:S(2)}, u32[]{:S(2)}) collective-permute-start(bf16[864,128]{1,0:T(8,128)(2,1)S(1)} %add_convert_fusion.2), channel_id=1, source_target_pairs={{0,16},{2,18},{4,20},{6,22},{8,24},{10,26},{12,28},{14,30},{16,0},... | collective-permute-start | bytes 663560 | tf_op jit(solution)/shard_map/ppermute | solution.py:409
  141.5 4.3 %collective-permute-start.18 = (bf16[448,128]{1,0:T(8,128)(2,1)S(1)}, bf16[448,128]{1,0:T(8,128)(2,1)S(1)}, u32[]{:S(2)}, u32[]{:S(2)}) collective-permute-start(bf16[448,128]{1,0:T(8,128)(2,1)S(1)} %broadcast_select_fusion.8), channel_id=1, source_target_pairs={{0,2},{2,0},{4,6},{6,4},{8,10},{10,8},{12,14},{14,12},{16,18},{18,... | collective-permute-start | bytes 344072 | tf_op jit(solution)/shard_map/ppermute | solution.py:409
  141.5 10.6 %copy-start.29 = (bf16[864,128]{1,0:T(8,128)(2,1)S(1)}, bf16[864,128]{1,0:T(8,128)(2,1)}, u32[]{:S(2)}) copy-start(bf16[864,128]{1,0:T(8,128)(2,1)} %copy-done.28) | copy-start | bytes 663556
  152.2 9.3 %collective-permute-start.22 = (bf16[4,32,1024]{2,1,0:T(8,128)(2,1)S(1)}, bf16[4,32,1024]{2,1,0:T(8,128)(2,1)S(1)}, u32[]{:S(2)}, u32[]{:S(2)}) collective-permute-start(bf16[4,32,1024]{2,1,0:T(8,128)(2,1)S(1)} %get-tuple-element.173), channel_id=1, source_target_pairs={{0,1},{1,0},{2,3},{3,2},{4,5},{5,4},{6,7},{7,6},{8,9},{9,8},{10,11... | collective-permute-start | bytes 786440 | tf_op jit(solution)/shard_map/ppermute | solution.py:395
  153.1 8.4 %collective-permute-start.21 = (bf16[864,128]{1,0:T(8,128)(2,1)S(1)}, bf16[864,128]{1,0:T(8,128)(2,1)S(1)}, u32[]{:S(2)}, u32[]{:S(2)}) collective-permute-start(bf16[864,128]{1,0:T(8,128)(2,1)S(1)} %add_convert_fusion.1), channel_id=1, source_target_pairs={{0,4},{2,6},{4,0},{6,2},{8,12},{10,14},{12,8},{14,10},{16,20},{18,... | collective-permute-start | bytes 663560 | tf_op jit(solution)/shard_map/ppermute | solution.py:409
  153.6 7.9 %collective-permute-start.20 = (bf16[224,128]{1,0:T(8,128)(2,1)S(1)}, bf16[224,128]{1,0:T(8,128)(2,1)S(1)}, u32[]{:S(2)}, u32[]{:S(2)}) collective-permute-start(bf16[224,128]{1,0:T(8,128)(2,1)S(1)} %broadcast_select_fusion.11), channel_id=1, source_target_pairs={{0,4},{2,6},{4,0},{6,2},{8,12},{10,14},{12,8},{14,10},{16,20},{18,... | collective-permute-start | bytes 172040 | tf_op jit(solution)/shard_map/ppermute | solution.py:409
  161.6 8.8 %collective-permute-start.24 = (bf16[1728,128]{1,0:T(8,128)(2,1)S(1)}, bf16[1728,128]{1,0:T(8,128)(2,1)S(1)}, u32[]{:S(2)}, u32[]{:S(2)}) collective-permute-start(bf16[1728,128]{1,0:T(8,128)(2,1)S(1)} %pad_maximum_fusion.1), channel_id=1, source_target_pairs={{0,2},{2,0},{4,6},{6,4},{8,10},{10,8},{12,14},{14,12},{16,18},{18,... | collective-permute-start | bytes 1327112 | tf_op jit(solution)/shard_map/ppermute | solution.py:409
  161.7 8.7 %collective-permute-start.25 = (bf16[4,32,1024]{2,1,0:T(8,128)(2,1)S(1)}, bf16[4,32,1024]{2,1,0:T(8,128)(2,1)S(1)}, u32[]{:S(2)}, u32[]{:S(2)}) collective-permute-start(bf16[4,32,1024]{2,1,0:T(8,128)(2,1)S(1)} %get-tuple-element.188), channel_id=1, source_target_pairs={{0,1},{1,0},{2,3},{3,2},{4,5},{5,4},{6,7},{7,6},{8,9},{9,8},{10,11... | collective-permute-start | bytes 786440 | tf_op jit(solution)/shard_map/ppermute | solution.py:395
  162.9 4.6 %collective-permute-start.23 = (bf16[224,128]{1,0:T(8,128)(2,1)S(1)}, bf16[224,128]{1,0:T(8,128)(2,1)S(1)}, u32[]{:S(2)}, u32[]{:S(2)}) collective-permute-start(bf16[224,128]{1,0:T(8,128)(2,1)S(1)} %add_convert_fusion.7), channel_id=1, source_target_pairs={{0,8},{2,10},{4,12},{6,14},{8,0},{10,2},{12,4},{14,6},{16,24},{18,... | collective-permute-start | bytes 172040 | tf_op jit(solution)/shard_map/ppermute | solution.py:409
  170.7 7.9 %collective-permute-start.27 = (bf16[4,32,1024]{2,1,0:T(8,128)(2,1)S(1)}, bf16[4,32,1024]{2,1,0:T(8,128)(2,1)S(1)}, u32[]{:S(2)}, u32[]{:S(2)}) collective-permute-start(bf16[4,32,1024]{2,1,0:T(8,128)(2,1)S(1)} %get-tuple-element.201), channel_id=1, source_target_pairs={{0,1},{1,0},{2,3},{3,2},{4,5},{5,4},{6,7},{7,6},{8,9},{9,8},{10,11... | collective-permute-start | bytes 786440 | tf_op jit(solution)/shard_map/ppermute | solution.py:395
  171.9 5.6 %collective-permute-start.26 = (bf16[224,128]{1,0:T(8,128)(2,1)S(1)}, bf16[224,128]{1,0:T(8,128)(2,1)S(1)}, u32[]{:S(2)}, u32[]{:S(2)}) collective-permute-start(bf16[224,128]{1,0:T(8,128)(2,1)S(1)} %add_convert_fusion.6), channel_id=1, source_target_pairs={{0,16},{2,18},{4,20},{6,22},{8,24},{10,26},{12,28},{14,30},{16,0},... | collective-permute-start | bytes 172040 | tf_op jit(solution)/shard_map/ppermute | solution.py:409
  178.6 7.0 %collective-permute-start.29 = (bf16[4,32,1024]{2,1,0:T(8,128)(2,1)S(1)}, bf16[4,32,1024]{2,1,0:T(8,128)(2,1)S(1)}, u32[]{:S(2)}, u32[]{:S(2)}) collective-permute-start(bf16[4,32,1024]{2,1,0:T(8,128)(2,1)S(1)} %get-tuple-element.207), channel_id=1, source_target_pairs={{0,1},{1,0},{2,3},{3,2},{4,5},{5,4},{6,7},{7,6},{8,9},{9,8},{10,11... | collective-permute-start | bytes 786440 | tf_op jit(solution)/shard_map/ppermute | solution.py:395
  179.8 4.2 %collective-permute-start.28 = (bf16[224,128]{1,0:T(8,128)(2,1)S(1)}, bf16[224,128]{1,0:T(8,128)(2,1)S(1)}, u32[]{:S(2)}, u32[]{:S(2)}) collective-permute-start(bf16[224,128]{1,0:T(8,128)(2,1)S(1)} %add_convert_fusion.5), channel_id=1, source_target_pairs={{0,4},{2,6},{4,0},{6,2},{8,12},{10,14},{12,8},{14,10},{16,20},{18,... | collective-permute-start | bytes 172040 | tf_op jit(solution)/shard_map/ppermute | solution.py:409
  185.7 3.1 %collective-permute-start.30 = (bf16[448,128]{1,0:T(8,128)(2,1)S(1)}, bf16[448,128]{1,0:T(8,128)(2,1)S(1)}, u32[]{:S(2)}, u32[]{:S(2)}) collective-permute-start(bf16[448,128]{1,0:T(8,128)(2,1)S(1)} %pad_maximum_fusion.5), channel_id=1, source_target_pairs={{0,2},{2,0},{4,6},{6,4},{8,10},{10,8},{12,14},{14,12},{16,18},{18,... | collective-permute-start | bytes 344072 | tf_op jit(solution)/shard_map/ppermute | solution.py:409
  (15 other events, 19.4 us)

commit v2 on v1

--- a/solution.py
+++ b/solution.py
@@ -14,10 +14,9 @@
 LANES = 128
 BF = jnp.bfloat16
 F32 = jnp.float32
-VMEM_LIMIT = 28 * 2**20
+VMEM_LIMIT = 24 * 2**20
 TILES = HH // 4
 ROWS = 16
-EARLY = HH // 2 + 1
 
 
 def nn(a, b):
@@ -124,76 +123,75 @@
     lax.fori_loop(0, count, step, 0)
 
 
-def volume_windows(filt, refs, windows, first, count):
-    own, low, high, peer_low, peer_high, edge, early = refs[:7]
+def volume_windows(filt, refs, windows, first, last):
+    own, low, high, peer_low, peer_high, edge, middle = refs
     planes, chans, _ = own.shape
     mine = pl.multiple_of(filt[0] * chans, 32)
     theirs = pl.multiple_of((1 - filt[0]) * chans, 32)
-    lower = max(first - 1, 0)
-    upper = min(first + count + 1, HH)
-
-    def put(source, plane, offset, start=lower, end=upper):
-        fine_rows(source, windows, plane, offset, chans, 2 * chans, first, start, end)
-
-    def inner(d):
-        if lower < EARLY:
-            put(row_of(early.at[d]), d + 2, theirs, lower, min(upper, EARLY))
-        if upper > EARLY:
-            put(row_of(refs[7].at[d], EARLY), d + 2, theirs, max(lower, EARLY), upper)
-
-    each(planes, lambda d: put(row_of(own.at[d]), d + 1, mine))
-    each(planes - 2, inner)
-    each(2, lambda d: put(row_of(edge.at[d]), 1 + d * (planes - 1), theirs))
-    put(row_of(low), 0, mine)
-    put(row_of(high), planes + 1, mine)
-    put(row_of(peer_low), 0, theirs)
-    put(row_of(peer_high), planes + 1, theirs)
-
-
-def forward_fine_kernel(first, count, volumes, filt, *refs):
-    weights, pool = refs[volumes : volumes + 2]
-    pooled, slope, windows = refs[-3:]
-    before = refs[volumes + 2] if first > 0 else None
+
+    def put(ref, plane, offset):
+        fine_rows(row_of(ref), windows, plane - first, offset, chans, 2 * chans, 0, 0, HH)
+
+    lower, upper = max(first, 1), min(last, planes + 1)
+    each(upper - lower, lambda d: put(own.at[d + lower - 1], d + lower, mine))
+    lower, upper = max(first, 2), min(last, planes)
+    each(upper - lower, lambda d: put(middle.at[d + lower - 2], d + lower, theirs))
+    if first == 0 and last == planes + 2:
+        each(2, lambda d: put(edge.at[d], 1 + d * (planes - 1), theirs))
+    elif first == 0:
+        put(edge.at[0], 1, theirs)
+    else:
+        put(edge.at[1], planes, theirs)
+    if first == 0:
+        put(low, 0, mine)
+        put(peer_low, 0, theirs)
+    if last == planes + 2:
+        put(high, planes + 1, mine)
+        put(peer_high, planes + 1, theirs)
+
+
+def forward_fine_kernel(filt, *refs):
+    weights, pool, pooled, slope, windows = refs[-5:]
     planes = refs[0].shape[0]
-    volume_windows(filt, refs[:volumes], windows, first, count)
+    volume_windows(filt, refs[:-5], windows, 0, planes + 2)
     outs = weights.shape[1] // 3
     span = 2 * LANES
-    side = slice(0, LANES) if first == 0 else slice(LANES, 2 * LANES)
 
     def chunk(j, _):
-        totals = [None] * planes
-        for p in range(planes + 2):
-            value = None
-            for kh in range(3):
-                lanes = pl.ds(pl.multiple_of((2 * j + kh) * LANES, LANES), span)
-                part = nn(weights[kh], windows[p, :, lanes])
-                value = part if value is None else value + part
-            for kd in range(3):
-                d = p - kd
-                if 0 <= d < planes:
-                    piece = value[kd * outs : (kd + 1) * outs]
-                    totals[d] = piece if totals[d] is None else totals[d] + piece
-        acts = []
-        for d in range(planes):
-            pre = totals[d]
-            sigma = sigmoid(pre)
-            act = pre * sigma
-            slope[d, :, pl.ds(pl.multiple_of(j * span, span), span)] = (
-                sigma + act * (1.0 - sigma)
-            ).astype(BF)
-            acts.append(act[:, :LANES] + act[:, LANES:])
-        tile = pl.ds(pl.multiple_of(j * LANES, LANES), LANES)
-        for d in range(planes // 2):
-            both = acts[2 * d] + acts[2 * d + 1]
+        acts = [[None, None] for _ in range(planes)]
+        for side in range(2):
+            top = side * (HH // 2) + j * 2
+            totals = [None] * planes
+            for p in range(planes + 2):
+                value = None
+                for kh in range(3):
+                    lanes = pl.ds(pl.multiple_of((top + kh) * LANES, LANES), span)
+                    part = nn(weights[kh], windows[p, :, lanes])
+                    value = part if value is None else value + part
+                for kd in range(3):
+                    d = p - kd
+                    if 0 <= d < planes:
+                        piece = value[kd * outs : (kd + 1) * outs]
+                        totals[d] = piece if totals[d] is None else totals[d] + piece
+            for d in range(planes):
+                pre = totals[d]
+                sigma = sigmoid(pre)
+                act = pre * sigma
+                slope[d, :, pl.ds(pl.multiple_of(top * LANES, LANES), span)] = (
+                    sigma + act * (1.0 - sigma)
+                ).astype(BF)
+                acts[d][side] = act[:, :LANES] + act[:, LANES:]
+        for d in range(0, planes, 2):
+            both = jnp.concatenate(
+                [acts[d][0] + acts[d + 1][0], acts[d][1] + acts[d + 1][1]], axis=1
+            )
             coarse = both.astype(BF)
             rest = (both - coarse.astype(F32)).astype(BF)
-            mean = nn(coarse, pool[side, :]) + nn(rest, pool[side, :])
-            if before is not None:
-                mean = mean + before[d, :, tile].astype(F32)
-            pooled[d, :, tile] = mean.astype(BF)
+            mean = nn(coarse, pool[...]) + nn(rest, pool[...])
+            pooled[d // 2, :, pl.ds(pl.multiple_of(j * LANES, LANES), LANES)] = mean.astype(BF)
         return 0
 
-    lax.fori_loop(0, count // 2, chunk, 0, unroll=2)
+    lax.fori_loop(0, TILES, chunk, 0, unroll=2)
 
 
 def forward_coarse_kernel(filt, own, peer, low, high, weights, cot, spread, grads, windows, first_out, last_out):
@@ -299,7 +297,7 @@
         wide_forward[k] = block.astype(BF)
 
 
-def grad_fine_kernel(own, peer, upper, lower, unpool, grads, first_out, last_out):
+def grad_fine_kernel(own, peer, slope, unpool, grads, first_out, last_out):
     planes = own.shape[0]
     for d in range(planes):
         for j in range(TILES):
@@ -311,9 +309,7 @@
                 for a in range(2):
                     for row in (side * HH // 2 + 2 * j, side * HH // 2 + 2 * j + 1):
                         cells = slice(row * LANES, (row + 1) * LANES)
-                        slope = lower if side else upper
-                        begin = (row - side * HH // 2) * LANES
-                        factor = slope[2 * d + a, :, begin : begin + LANES].astype(F32)
+                        factor = slope[2 * d + a, :, cells].astype(F32)
                         value = (part * factor).astype(BF)
                         grads[2 * d + a, :, cells] = value
                         if 2 * d + a == 0:
@@ -322,27 +318,32 @@
                             last_out[:, cells] = value
 
 
-def kernel_grad_fine_kernel(filt, *refs):
-    grads, out, windows, total = refs[-4:]
+def kernel_grad_fine_kernel(start, end, filt, *refs):
+    grads = refs[7]
+    out, windows = refs[-2:]
+    before = refs[8] if start > 0 else None
     planes, _, cells = refs[0].shape
-    volume_windows(filt, refs[:-4], windows, 0, HH)
+    volume_windows(filt, refs[:7], windows, start, end)
     group = windows.shape[1]
     outs = grads.shape[0] // planes
     seen = set()
-    for p in range(planes + 2):
+    for p in range(start, end):
         first, last = max(p - 2, 0), min(p, planes - 1)
         for kh in range(3):
             value = nt(
-                windows[p, :, kh * LANES : kh * LANES + cells],
+                windows[p - start, :, kh * LANES : kh * LANES + cells],
                 grads[first * outs : (last + 1) * outs, :],
             )
             for d in range(first, last + 1):
                 index = (p - d) * 3 + kh
                 rows = slice(index * group, (index + 1) * group)
                 part = value[:, (d - first) * outs : (d - first + 1) * outs]
-                total[rows, :] = total[rows, :] + part if index in seen else part
+                if index in seen:
+                    part = out[rows, :] + part
+                elif before is not None:
+                    part = before[rows, :] + part
+                out[rows, :] = part
                 seen.add(index)
-    out[...] = total[...].astype(out.dtype)
 
 
 def backward_fine_kernel(first, count, filt, grads, low, high, weights, own, peer, windows):
@@ -496,12 +497,10 @@
 
     own = volume.transpose(1, 0, 2)
     edge = swap(jnp.stack([own[0], own[planes - 1]]))
-    early = swap(own[1 : planes - 1, :, : EARLY * WW])
+    middle = swap(own[1 : planes - 1])
     low, high = to_next(own[planes - 1]), to_previous(own[0])
-    late, edge = lax.optimization_barrier((own[1 : planes - 1, :, EARLY * WW :], edge))
-    late = swap(late)
     plow, phigh = to_next(edge[1]), to_previous(edge[0])
-    volumes = (own, low, high, plow, phigh, edge, early, late)
+    volumes = (own, low, high, plow, phigh, edge, middle)
 
     fine_forward, fine_backward, wide_forward = call(
         weights_kernel,
@@ -517,26 +516,14 @@
     unpool = jnp.asarray(pool_matrix().T, BF)
     spread = jnp.asarray(spread_matrix(HH // 4, WW // 4), BF)
 
-    half = HH // 2
-    part_outs = [((half_planes, mid, coarse), BF), ((planes, mid, cells // 2), BF)]
-    part_windows = pltpu.VMEM((planes + 2, 6 * own_in, (half + 2) * LANES), BF)
-    fine_windows = pltpu.VMEM((planes + 2, 6 * own_in, (HH + 2) * LANES), BF)
-    pooled, slope_upper = call(
-        functools.partial(forward_fine_kernel, 0, half, 7),
-        part_outs,
-        "forward_fine_upper",
-        [part_windows],
+    pooled, slope = call(
+        forward_fine_kernel,
+        [((half_planes, mid, coarse), BF), ((planes, mid, cells), BF)],
+        "forward_fine",
+        [pltpu.VMEM((planes + 2, 6 * own_in, (HH + 2) * LANES), BF)],
         scalars=1,
         inputs=9,
-    )(which, *volumes[:7], fine_forward, pool)
-    pooled, slope_lower = call(
-        functools.partial(forward_fine_kernel, half, half, 8),
-        part_outs,
-        "forward_fine_lower",
-        [part_windows],
-        scalars=1,
-        inputs=11,
-    )(which, *volumes, fine_forward, pool, pooled)
+    )(which, *volumes, fine_forward, pool)
 
     pooled_peer = swap(pooled)
     pool_low = to_next(jnp.stack([pooled[half_planes - 1], pooled_peer[half_planes - 1]]))
@@ -591,21 +578,25 @@
         grad_fine_kernel,
         [((planes, mid, cells), BF), ((mid, cells), BF), ((mid, cells), BF)],
         "grad_fine",
-        inputs=5,
-    )(own_back, peer_back, slope_upper, slope_lower, unpool)
+        inputs=4,
+    )(own_back, peer_back, slope, unpool)
     three_low, three_high = to_next(three_last), to_previous(three_first)
-    (fine_kernel,), _ = beside(
-        [coarse_sum],
-        call(
-            kernel_grad_fine_kernel,
-            [((54 * own_in, mid), BF)],
-            "kernel_grad_fine",
-            [fine_windows, pltpu.VMEM((54 * own_in, mid), F32)],
-            scalars=1,
-            inputs=9,
-        ),
-        (which, *volumes, grad_three.reshape(planes * mid, cells)),
-    )
+    fine_kernel = []
+    cut = planes // 2 + 1
+    for start, end in ((0, cut), (cut, planes + 2)):
+        fine_kernel, _ = beside(
+            [coarse_sum],
+            call(
+                functools.partial(kernel_grad_fine_kernel, start, end),
+                [((54 * own_in, mid), F32)],
+                f"kernel_grad_fine_{start}",
+                [pltpu.VMEM((end - start, 6 * own_in, (HH + 2) * LANES), BF)],
+                scalars=1,
+                inputs=8 + len(fine_kernel),
+            ),
+            (which, *volumes, grad_three.reshape(planes * mid, cells), *fine_kernel),
+        )
+    fine_kernel = fine_kernel[0].astype(BF)
 
     fine_sum = Sum(fine_kernel.reshape(27 * own_in, 2 * mid))
     parts = 4

time: 191 us -> 176 us (0.921)
  waiting for transfers between devices: 39.9 us -> 31.1 us
  Pallas kernels: 64.1 us -> 56.5 us
  starting transfers between devices: 53 us -> 58.3 us
  local copies, waits for them, and re-layouts: 25.2 us -> 21.9 us
    pallas_call x2 -> x1, Pallas kernels: 23.6 us -> 14.5 us  [body(): call(forward_fine_kernel, [((half_planes, mid, coarse), BF), ((planes, mi...]
    ppermute x12, waiting for transfers between devices: 17.3 us -> 9.56 us  [across(): return lax.ppermute(value, 'depth', [(i, i ^ bit) for i in range(count)])]
    ppermute x12, starting transfers between devices: 17.3 us -> 22.1 us  [across(): return lax.ppermute(value, 'depth', [(i, i ^ bit) for i in range(count)])]
    unnamed x68 -> x54, local copies, waits for them, and re-layouts: 20.3 us -> 17 us
    pallas_call x6 -> x7, Pallas kernels: 32.5 us -> 34 us  [beside(): kernel(*inputs)]
    ppermute x9 -> x8, waiting for transfers between devices: 20.9 us -> 20.2 us  [swap(): return lax.ppermute(value, 'filt', [(0, 1), (1, 0)])]
    ppermute x9 -> x8, starting transfers between devices: 10.8 us -> 11.2 us  [swap(): return lax.ppermute(value, 'filt', [(0, 1), (1, 0)])]
  transfers between devices with their start and end apart: 31 -> 30, of which waited for: 11 -> 9; matrix products, arithmetic and copies ran while one was open for 7% -> 7% of each run, Pallas kernels for 25% -> 21%
where the time goes in v2:
time: 176 us; the launch traced here: 175 us
  starting transfers between devices  58.3 us (33%)
  Pallas kernels  56.5 us (32%)
  waiting for transfers between devices  31.1 us (18%)
  local copies, waits for them, and re-layouts  21.9 us (12%)
  other arithmetic  5.9 us (3%)
    pallas_call x7, Pallas kernels, beside(): kernel(*inputs)  34 us
    ppermute x12, starting transfers between devices, across(): return lax.ppermute(value, 'depth', [(i, i ^ bit) for i in range(count)])  22.1 us
    ppermute x8, waiting for transfers between devices, swap(): return lax.ppermute(value, 'filt', [(0, 1), (1, 0)])  20.2 us
    ppermute x5, starting transfers between devices, to_next(): return lax.ppermute(value, 'depth', [(i, i + 1) for i in range(count - 1)])  18.3 us
    unnamed x54, local copies, waits for them, and re-layouts  17 us
    pallas_call x1, Pallas kernels, body(): call(forward_fine_kernel, [((half_planes, mid, coarse), BF), ((planes, mi...  14.5 us
    ppermute x8, starting transfers between devices, swap(): return lax.ppermute(value, 'filt', [(0, 1), (1, 0)])  11.2 us
    ppermute x12, waiting for transfers between devices, across(): return lax.ppermute(value, 'depth', [(i, i ^ bit) for i in range(count)])  9.56 us
  transfers between devices with their start and end apart: 30, of which 9 were waited for; matrix products, arithmetic and copies ran while one was open for 7% of the time, Pallas kernels for 21%

profile of v2, /device:TPU:0, one launch (start us, length us, event | category | flops | bytes accessed | tf_op | source)
XLA Modules:
  0.0 175.0 jit_solution(688268808434094801)
XLA Ops:
  0.6 1.8 %copy.18 = bf16[32,4,4096]{2,0,1:T(8,128)(2,1)S(1)} copy(bf16[32,4,4096]{2,1,0:T(4,128)(2,1)} %param.7) | data formatting | bytes 2097152 | tf_op args[0]
  3.4 3.0 %collective-permute-start.2 = (bf16[2,32,4096]{2,1,0:T(8,128)(2,1)S(1)}, bf16[2,32,4096]{2,1,0:T(8,128)(2,1)S(1)}, u32[]{:S(2)}, u32[]{:S(2)}) collective-permute-start(bf16[2,32,4096]{2,1,0:T(8,128)(2,1)S(1)} %pad_maximum_fusion), channel_id=1, source_target_pairs={{0,1},{1,0},{2,3},{3,2},{4,5},{5,4},{6,7},{7,6},{8,9},{9,8},{10,11... | collective-permute-start | bytes 1572872 | tf_op jit(solution)/shard_map/ppermute | solution.py:396
  6.4 2.2 %collective-permute-start = (bf16[32,4096]{1,0:T(8,128)(2,1)}, bf16[32,4096]{1,0:T(8,128)(2,1)}, u32[]{:S(2)}, u32[]{:S(2)}) collective-permute-start(bf16[32,4096]{1,0:T(8,128)(2,1)} %get-tuple-element.230), channel_id=1, source_target_pairs={{0,2},{2,4},{4,6},{6,8},{8,10},{10,12},{12,14},{14,16},{16,18},{18... | collective-permute-start | bytes 786440 | tf_op jit(solution)/shard_map/ppermute | solution.py:387
  8.6 1.3 collective-permute-start.1
  11.1 8.0 %collective-permute-done.2.refs_5_ = bf16[2,32,4096]{2,1,0:T(8,128)(2,1)S(1)} collective-permute-done((bf16[2,32,4096]{2,1,0:T(8,128)(2,1)S(1)}, bf16[2,32,4096]{2,1,0:T(8,128)(2,1)S(1)}, u32[]{:S(2)}, u32[]{:S(2)}) %collective-permute-start.2) | collective-permute-done | bytes 524320 | tf_op jit(solution)/shard_map/ppermute | solution.py:396
  20.0 2.0 %collective-permute-start.3 = (bf16[32,4096]{1,0:T(8,128)(2,1)}, bf16[32,4096]{1,0:T(8,128)(2,1)}, u32[]{:S(2)}, u32[]{:S(2)}) collective-permute-start(bf16[32,4096]{1,0:T(8,128)(2,1)} %get-tuple-element.236), channel_id=1, source_target_pairs={{0,2},{2,4},{4,6},{6,8},{8,10},{10,12},{12,14},{14,16},{16,18},{18... | collective-permute-start | bytes 786440 | tf_op jit(solution)/shard_map/ppermute | solution.py:387
  22.0 1.3 collective-permute-start.4
  25.9 3.7 %collective-permute-done.5.refs_6_ = bf16[2,32,4096]{2,1,0:T(8,128)(2,1)S(1)} collective-permute-done((bf16[2,32,4096]{2,1,0:T(8,128)(2,1)}, bf16[2,32,4096]{2,1,0:T(8,128)(2,1)S(1)}, u32[]{:S(2)}, u32[]{:S(2)}) %collective-permute-start.5) | collective-permute-done | bytes 524320 | tf_op jit(solution)/shard_map/ppermute | solution.py:396
  29.6 14.5 %forward_fine.1 = (bf16[2,64,1024]{2,1,0:T(8,128)(2,1)S(1)}, bf16[4,64,4096]{2,1,0:T(8,128)(2,1)S(1)}) custom-call(s32[1]{0:T(128)} %bitcast.filt, bf16[4,32,4096]{2,1,0:T(8,128)(2,1)S(1)} %bitcast.21, bf16[32,4096]{1,0:T(8,128)(2,1)} %collective-permute-done.refs_1_, bf16[32,4096]{1,0:T(8,128)(2,1)} %collective-permute-done.1.refs_2_, ...), custom_call_target="tpu_custom_call" | custom-call | tf_op jit(solution)/shard_map/forward_fine/pallas_call | solution.py:519
  44.1 1.3 copy-done.5
  45.4 1.7 collective-permute-start.6
  47.2 5.9 %collective-permute-done.6.peer = bf16[2,64,1024]{2,1,0:T(8,128)(2,1)S(1)} collective-permute-done((bf16[2,64,1024]{2,1,0:T(8,128)(2,1)S(1)}, bf16[2,64,1024]{2,1,0:T(8,128)(2,1)S(1)}, u32[]{:S(2)}, u32[]{:S(2)}) %collective-permute-start.6) | collective-permute-done | bytes 262176 | tf_op jit(solution)/shard_map/ppermute | solution.py:396
  53.2 1.3 collective-permute-start.8
  55.2 3.8 %collective-permute-start.7 = (bf16[2,64,1024]{2,1,0:T(8,128)(2,1)}, bf16[2,64,1024]{2,1,0:T(8,128)(2,1)S(1)}, u32[]{:S(2)}, u32[]{:S(2)}) collective-permute-start(bf16[2,64,1024]{2,1,0:T(8,128)(2,1)} %pad_maximum_fusion.2), channel_id=1, source_target_pairs={{0,2},{2,4},{4,6},{6,8},{8,10},{10,12},{12,14},{14,16},{16,18},{18... | collective-permute-start | bytes 786440 | tf_op jit(solution)/shard_map/ppermute | solution.py:387
  59.1 1.3 collective-permute-done.7.low
  63.6 3.6 %forward_coarse.1 = (bf16[2,128,1024]{2,1,0:T(8,128)(2,1)S(1)}, bf16[4,384,1280]{2,1,0:T(8,128)(2,1)S(1)}, bf16[128,1024]{1,0:T(8,128)(2,1)S(1)}, bf16[128,1024]{1,0:T(8,128)(2,1)S(1)}) custom-call(s32[1]{0:T(128)} %bitcast.filt, bf16[2,64,1024]{2,1,0:T(8,128)(2,1)S(1)} %copy-done.11, bf16[2,64,1024]{2,1,0:T(8,128)(2,1)S(1)} %collective-permute-done.6.peer, ...), custom_call_target="tpu_custom_call" | custom-call | tf_op jit(solution)/shard_map/forward_coarse/pallas_call | solution.py:532
  67.2 1.3 collective-permute-start.10
  68.5 8.3 %collective-permute-start.9 = (bf16[128,1024]{1,0:T(8,128)(2,1)S(1)}, bf16[128,1024]{1,0:T(8,128)(2,1)S(1)}, u32[]{:S(2)}, u32[]{:S(2)}) collective-permute-start(bf16[128,1024]{1,0:T(8,128)(2,1)S(1)} %get-tuple-element.117), channel_id=1, source_target_pairs={{0,2},{2,4},{4,6},{6,8},{8,10},{10,12},{12,14},{14,16},{16,18},{18... | collective-permute-start | bytes 786440 | tf_op jit(solution)/shard_map/ppermute | solution.py:387
  76.7 2.6 %kernel_grad_coarse.1 = bf16[3456,128]{1,0:T(8,128)(2,1)S(1)} custom-call(bf16[4,384,1280]{2,1,0:T(8,128)(2,1)S(1)} %get-tuple-element.119.windows, bf16[256,1024]{1,0:T(8,128)(2,1)S(1)} %bitcast.24), custom_call_target="tpu_custom_call" | custom-call | tf_op jit(solution)/shard_map/kernel_grad_coarse/pallas_call | solution.py:555
  80.8 3.9 %collective-permute-start.11 = (bf16[1728,128]{1,0:T(8,128)(2,1)S(1)}, bf16[1728,128]{1,0:T(8,128)(2,1)}, u32[]{:S(2)}, u32[]{:S(2)}) collective-permute-start(bf16[1728,128]{1,0:T(8,128)(2,1)S(1)} %broadcast_select_fusion.2), channel_id=1, source_target_pairs={{0,2},{2,0},{4,6},{6,4},{8,10},{10,8},{12,14},{14,12},{16,18},{18,... | collective-permute-start | bytes 1327112 | tf_op jit(solution)/shard_map/ppermute | solution.py:410
  87.7 3.0 %backward_coarse.1 = (f32[2,64,1024]{2,1,0:T(8,128)S(1)}, bf16[2,64,1024]{2,1,0:T(8,128)(2,1)S(1)}) custom-call(s32[1]{0:T(128)} %bitcast.filt, bf16[2,128,1024]{2,1,0:T(8,128)(2,1)S(1)} %copy-done.8, bf16[128,1024]{1,0:T(8,128)(2,1)S(1)} %copy-done.18, bf16[128,1024]{1,0:T(8,128)(2,1)S(1)} %copy-done.16, bf16[3456,128]{1,0:T(8,128)(2,1)S(1)} %copy-done.4), custom_call_target="tpu_custom_call" | custom-call | tf_op jit(solution)/shard_map/backward_coarse/pallas_call | solution.py:464
  90.7 1.3 add_convert_fusion
  92.1 1.6 collective-permute-start.13
  93.7 2.4 %collective-permute-start.12 = (bf16[864,128]{1,0:T(8,128)(2,1)S(1)}, bf16[864,128]{1,0:T(8,128)(2,1)S(1)}, u32[]{:S(2)}, u32[]{:S(2)}) collective-permute-start(bf16[864,128]{1,0:T(8,128)(2,1)S(1)} %broadcast_select_fusion.5), channel_id=1, source_target_pairs={{0,4},{2,6},{4,0},{6,2},{8,12},{10,14},{12,8},{14,10},{16,20},{18,... | collective-permute-start | bytes 663560 | tf_op jit(solution)/shard_map/ppermute | solution.py:410
  96.0 5.8 %collective-permute-done.12 = bf16[864,128]{1,0:T(8,128)(2,1)S(1)} collective-permute-done((bf16[864,128]{1,0:T(8,128)(2,1)S(1)}, bf16[864,128]{1,0:T(8,128)(2,1)S(1)}, u32[]{:S(2)}, u32[]{:S(2)}) %collective-permute-start.12) | collective-permute-done | bytes 221216 | tf_op jit(solution)/shard_map/ppermute | solution.py:410
  102.0 1.4 grad_fine.1
  103.4 1.7 collective-permute-start.16
  105.1 6.7 %kernel_grad_fine_0.1.refs_8_ = f32[1728,64]{1,0:T(8,128)S(1)} custom-call(s32[1]{0:T(128)} %bitcast.filt, bf16[4,32,4096]{2,1,0:T(8,128)(2,1)S(1)} %bitcast.22, bf16[32,4096]{1,0:T(8,128)(2,1)} %collective-permute-done.refs_1_, bf16[32,4096]{1,0:T(8,128)(2,1)} %collective-permute-done.1.refs_2_, bf16[32,4096]{1,0:T(8,128)(2,1)} %collective-permute-done.3.refs_3_, ...), custom_call_target="tpu_custom_call" | custom-call | tf_op jit(solution)/shard_map/kernel_grad_fine_0/pallas_call | solution.py:464
  112.0 2.7 %collective-permute-start.17 = (bf16[864,128]{1,0:T(8,128)(2,1)S(1)}, bf16[864,128]{1,0:T(8,128)(2,1)S(1)}, u32[]{:S(2)}, u32[]{:S(2)}) collective-permute-start(bf16[864,128]{1,0:T(8,128)(2,1)S(1)} %add_convert_fusion.2), channel_id=1, source_target_pairs={{0,16},{2,18},{4,20},{6,22},{8,24},{10,26},{12,28},{14,30},{16,0},... | collective-permute-start | bytes 663560 | tf_op jit(solution)/shard_map/ppermute | solution.py:410
  114.6 2.1 %collective-permute-start.14 = (bf16[64,4096]{1,0:T(8,128)(2,1)}, bf16[64,4096]{1,0:T(8,128)(2,1)}, u32[]{:S(2)}, u32[]{:S(2)}) collective-permute-start(bf16[64,4096]{1,0:T(8,128)(2,1)} %get-tuple-element.136), channel_id=1, source_target_pairs={{0,2},{2,4},{4,6},{6,8},{8,10},{10,12},{12,14},{14,16},{16,18},{18... | collective-permute-start | bytes 1572872 | tf_op jit(solution)/shard_map/ppermute | solution.py:387
  116.7 1.5 collective-permute-start.15
  118.2 6.8 %kernel_grad_fine_3.1 = f32[1728,64]{1,0:T(8,128)S(1)} custom-call(s32[1]{0:T(128)} %bitcast.filt, bf16[4,32,4096]{2,1,0:T(8,128)(2,1)S(1)} %bitcast.23, bf16[32,4096]{1,0:T(8,128)(2,1)} %collective-permute-done.refs_1_, bf16[32,4096]{1,0:T(8,128)(2,1)} %collective-permute-done.1.refs_2_, bf16[32,4096]{1,0:T(8,128)(2,1)} %collective-permute-done.3.refs_3_, ...), custom_call_target="tpu_custom_call" | custom-call | tf_op jit(solution)/shard_map/kernel_grad_fine_3/pallas_call | solution.py:464
  128.9 2.5 %collective-permute-start.19 = (bf16[864,128]{1,0:T(8,128)(2,1)S(1)}, bf16[864,128]{1,0:T(8,128)(2,1)S(1)}, u32[]{:S(2)}, u32[]{:S(2)}) collective-permute-start(bf16[864,128]{1,0:T(8,128)(2,1)S(1)} %add_convert_fusion.1), channel_id=1, source_target_pairs={{0,4},{2,6},{4,0},{6,2},{8,12},{10,14},{12,8},{14,10},{16,20},{18,... | collective-permute-start | bytes 663560 | tf_op jit(solution)/shard_map/ppermute | solution.py:410
  131.4 4.3 %backward_fine_0.1 = (f32[4,32,1024]{2,1,0:T(8,128)S(1)}, bf16[4,32,1024]{2,1,0:T(8,128)(2,1)S(1)}) custom-call(s32[1]{0:T(128)} %bitcast.filt, bf16[4,64,4096]{2,1,0:T(8,128)(2,1)S(1)} %get-tuple-element.206.grads, bf16[64,4096]{1,0:T(8,128)(2,1)} %collective-permute-done.14.low, bf16[64,4096]{1,0:T(8,128)(2,1)} %collective-permute-done.15.high, ...), custom_call_target="tpu_custom_call" | custom-call | tf_op jit(solution)/shard_map/backward_fine_0/pallas_call | solution.py:464
  135.7 1.7 collective-permute-done.19
  137.7 1.2 collective-permute-start.22
  138.9 1.3 collective-permute-start.20
  140.2 4.3 %backward_fine_1.1 = (f32[4,32,1024]{2,1,0:T(8,128)S(1)}, bf16[4,32,1024]{2,1,0:T(8,128)(2,1)S(1)}) custom-call(s32[1]{0:T(128)} %bitcast.filt, bf16[4,64,4096]{2,1,0:T(8,128)(2,1)S(1)} %get-tuple-element.206.grads, bf16[64,4096]{1,0:T(8,128)(2,1)} %collective-permute-done.14.low, bf16[64,4096]{1,0:T(8,128)(2,1)} %collective-permute-done.15.high, ...), custom_call_target="tpu_custom_call" | custom-call | tf_op jit(solution)/shard_map/backward_fine_1/pallas_call | solution.py:464
  144.5 1.8 %collective-permute-done.22 = bf16[4,32,1024]{2,1,0:T(8,128)(2,1)S(1)} collective-permute-done((bf16[4,32,1024]{2,1,0:T(8,128)(2,1)S(1)}, bf16[4,32,1024]{2,1,0:T(8,128)(2,1)S(1)}, u32[]{:S(2)}, u32[]{:S(2)}) %collective-permute-start.22) | collective-permute-done | bytes 262176 | tf_op jit(solution)/shard_map/ppermute | solution.py:396
  146.4 1.2 collective-permute-start.24
  147.6 2.2 %collective-permute-start.23 = (bf16[224,128]{1,0:T(8,128)(2,1)S(1)}, bf16[224,128]{1,0:T(8,128)(2,1)S(1)}, u32[]{:S(2)}, u32[]{:S(2)}) collective-permute-start(bf16[224,128]{1,0:T(8,128)(2,1)S(1)} %add_convert_fusion.7), channel_id=1, source_target_pairs={{0,8},{2,10},{4,12},{6,14},{8,0},{10,2},{12,4},{14,6},{16,24},{18,... | collective-permute-start | bytes 172040 | tf_op jit(solution)/shard_map/ppermute | solution.py:410
  150.1 4.3 %backward_fine_2.1 = (f32[4,32,1024]{2,1,0:T(8,128)S(1)}, bf16[4,32,1024]{2,1,0:T(8,128)(2,1)S(1)}) custom-call(s32[1]{0:T(128)} %bitcast.filt, bf16[4,64,4096]{2,1,0:T(8,128)(2,1)S(1)} %get-tuple-element.206.grads, bf16[64,4096]{1,0:T(8,128)(2,1)} %collective-permute-done.14.low, bf16[64,4096]{1,0:T(8,128)(2,1)} %collective-permute-done.15.high, ...), custom_call_target="tpu_custom_call" | custom-call | tf_op jit(solution)/shard_map/backward_fine_2/pallas_call | solution.py:464
  155.6 2.5 %collective-permute-start.25 = (bf16[224,128]{1,0:T(8,128)(2,1)S(1)}, bf16[224,128]{1,0:T(8,128)(2,1)S(1)}, u32[]{:S(2)}, u32[]{:S(2)}) collective-permute-start(bf16[224,128]{1,0:T(8,128)(2,1)S(1)} %add_convert_fusion.6), channel_id=1, source_target_pairs={{0,16},{2,18},{4,20},{6,22},{8,24},{10,26},{12,28},{14,30},{16,0},... | collective-permute-start | bytes 172040 | tf_op jit(solution)/shard_map/ppermute | solution.py:410
  158.1 1.3 convert_multiply_fusion
  159.4 4.5 %backward_fine_3.1 = (f32[4,32,1024]{2,1,0:T(8,128)S(1)}, bf16[4,32,1024]{2,1,0:T(8,128)(2,1)S(1)}) custom-call(s32[1]{0:T(128)} %bitcast.filt, bf16[4,64,4096]{2,1,0:T(8,128)(2,1)S(1)} %get-tuple-element.206.grads, bf16[64,4096]{1,0:T(8,128)(2,1)} %collective-permute-done.14.low, bf16[64,4096]{1,0:T(8,128)(2,1)} %collective-permute-done.15.high, ...), custom_call_target="tpu_custom_call" | custom-call | tf_op jit(solution)/shard_map/backward_fine_3/pallas_call | solution.py:464
  165.0 2.6 %collective-permute-start.27 = (bf16[224,128]{1,0:T(8,128)(2,1)S(1)}, bf16[224,128]{1,0:T(8,128)(2,1)S(1)}, u32[]{:S(2)}, u32[]{:S(2)}) collective-permute-start(bf16[224,128]{1,0:T(8,128)(2,1)S(1)} %add_convert_fusion.5), channel_id=1, source_target_pairs={{0,4},{2,6},{4,0},{6,2},{8,12},{10,14},{12,8},{14,10},{16,20},{18,... | collective-permute-start | bytes 172040 | tf_op jit(solution)/shard_map/ppermute | solution.py:410
  167.8 2.0 %collective-permute-done.27 = bf16[224,128]{1,0:T(8,128)(2,1)S(1)} collective-permute-done((bf16[224,128]{1,0:T(8,128)(2,1)S(1)}, bf16[224,128]{1,0:T(8,128)(2,1)S(1)}, u32[]{:S(2)}, u32[]{:S(2)}) %collective-permute-start.27) | collective-permute-done | bytes 57376 | tf_op jit(solution)/shard_map/ppermute | solution.py:410
  171.0 2.7 %copy.15 = f32[32,4,4096]{2,1,0:T(4,128)} copy(f32[32,4,4096]{2,0,1:T(8,128)S(1)} %maximum_bitcast_fusion) | data formatting | bytes 4194304
  (114 shorter events, 23.2 us)
Async XLA Ops:
  2.4 20.9 %copy-start.23 = (bf16[1728,64]{0,1:T(8,128)(2,1)S(1)}, bf16[1728,64]{0,1:T(8,128)(2,1)}, u32[]{:S(2)}) copy-start(bf16[1728,64]{0,1:T(8,128)(2,1)} %param.8) | copy-start | bytes 663556
  3.3 21.0 %copy-start.4 = (bf16[3456,128]{1,0:T(8,128)(2,1)S(1)}, bf16[3456,128]{1,0:T(8,128)(2,1)}, u32[]{:S(2)}) copy-start(bf16[3456,128]{1,0:T(8,128)(2,1)} %weights.2) | copy-start | bytes 2654212
  3.4 26.2 %copy-start.21 = (bf16[256,128]{1,0:T(8,128)(2,1)S(1)}, bf16[256,128]{1,0:T(8,128)(2,1)}, u32[]{:S(2)}) copy-start(bf16[256,128]{1,0:T(8,128)(2,1)} %constant.26.clone.refs_8_) | copy-start | bytes 196612
  3.4 15.8 %collective-permute-start.2 = (bf16[2,32,4096]{2,1,0:T(8,128)(2,1)S(1)}, bf16[2,32,4096]{2,1,0:T(8,128)(2,1)S(1)}, u32[]{:S(2)}, u32[]{:S(2)}) collective-permute-start(bf16[2,32,4096]{2,1,0:T(8,128)(2,1)S(1)} %pad_maximum_fusion), channel_id=1, source_target_pairs={{0,1},{1,0},{2,3},{3,2},{4,5},{5,4},{6,7},{7,6},{8,9},{9,8},{10,11... | collective-permute-start | bytes 1572872 | tf_op jit(solution)/shard_map/ppermute | solution.py:396
  6.4 19.4 %collective-permute-start = (bf16[32,4096]{1,0:T(8,128)(2,1)}, bf16[32,4096]{1,0:T(8,128)(2,1)}, u32[]{:S(2)}, u32[]{:S(2)}) collective-permute-start(bf16[32,4096]{1,0:T(8,128)(2,1)} %get-tuple-element.230), channel_id=1, source_target_pairs={{0,2},{2,4},{4,6},{6,8},{8,10},{10,12},{12,14},{14,16},{16,18},{18... | collective-permute-start | bytes 786440 | tf_op jit(solution)/shard_map/ppermute | solution.py:387
  8.6 17.3 %collective-permute-start.1 = (bf16[32,4096]{1,0:T(8,128)(2,1)}, bf16[32,4096]{1,0:T(8,128)(2,1)}, u32[]{:S(2)}, u32[]{:S(2)}) collective-permute-start(bf16[32,4096]{1,0:T(8,128)(2,1)} %get-tuple-element.231), channel_id=1, source_target_pairs={{2,0},{4,2},{6,4},{8,6},{10,8},{12,10},{14,12},{16,14},{18,16},{20... | collective-permute-start | bytes 786440 | tf_op jit(solution)/shard_map/ppermute | solution.py:392
  10.7 18.9 %collective-permute-start.5 = (bf16[2,32,4096]{2,1,0:T(8,128)(2,1)}, bf16[2,32,4096]{2,1,0:T(8,128)(2,1)S(1)}, u32[]{:S(2)}, u32[]{:S(2)}) collective-permute-start(bf16[2,32,4096]{2,1,0:T(8,128)(2,1)} %slice.91), channel_id=1, source_target_pairs={{0,1},{1,0},{2,3},{3,2},{4,5},{5,4},{6,7},{7,6},{8,9},{9,8},{10,11... | collective-permute-start | bytes 1572872 | tf_op jit(solution)/shard_map/ppermute | solution.py:396
  19.2 24.9 %copy-start = (bf16[2,32,4096]{2,1,0:T(8,128)(2,1)}, bf16[2,32,4096]{2,1,0:T(8,128)(2,1)S(1)}, u32[]{:S(2)}) copy-start(bf16[2,32,4096]{2,1,0:T(8,128)(2,1)S(1)} %collective-permute-done.2.refs_5_) | copy-start | bytes 1572868
  20.0 9.5 %collective-permute-start.3 = (bf16[32,4096]{1,0:T(8,128)(2,1)}, bf16[32,4096]{1,0:T(8,128)(2,1)}, u32[]{:S(2)}, u32[]{:S(2)}) collective-permute-start(bf16[32,4096]{1,0:T(8,128)(2,1)} %get-tuple-element.236), channel_id=1, source_target_pairs={{0,2},{2,4},{4,6},{6,8},{8,10},{10,12},{12,14},{14,16},{16,18},{18... | collective-permute-start | bytes 786440 | tf_op jit(solution)/shard_map/ppermute | solution.py:387
  22.0 7.5 %collective-permute-start.4 = (bf16[32,4096]{1,0:T(8,128)(2,1)}, bf16[32,4096]{1,0:T(8,128)(2,1)}, u32[]{:S(2)}, u32[]{:S(2)}) collective-permute-start(bf16[32,4096]{1,0:T(8,128)(2,1)} %get-tuple-element.235), channel_id=1, source_target_pairs={{2,0},{4,2},{6,4},{8,6},{10,8},{12,10},{14,12},{16,14},{18,16},{20... | collective-permute-start | bytes 786440 | tf_op jit(solution)/shard_map/ppermute | solution.py:392
  25.8 27.3 %copy-start.12 = (bf16[9,128,384]{2,1,0:T(8,128)(2,1)}, bf16[9,128,384]{2,1,0:T(8,128)(2,1)S(1)}, u32[]{:S(2)}) copy-start(bf16[9,128,384]{2,1,0:T(8,128)(2,1)S(1)} %get-tuple-element.115.weights) | copy-start | bytes 2654212
  29.6 23.6 %copy-start.2 = (bf16[2,32,4096]{2,1,0:T(8,128)(2,1)}, bf16[2,32,4096]{2,1,0:T(8,128)(2,1)S(1)}, u32[]{:S(2)}) copy-start(bf16[2,32,4096]{2,1,0:T(8,128)(2,1)S(1)} %collective-permute-done.5.refs_6_) | copy-start | bytes 1572868
  29.6 30.8 %copy-start.19 = (bf16[128,1,256]{2,0,1:T(8,128)(2,1)S(1)}, bf16[128,1,256]{2,0,1:T(8,128)(2,1)}, u32[]{:S(2)}) copy-start(bf16[128,1,256]{2,0,1:T(8,128)(2,1)} %param.10) | copy-start | bytes 196612
  44.1 1.3 copy-start.5
  45.4 7.8 %copy-start.10 = (bf16[2,64,1024]{2,1,0:T(8,128)(2,1)}, bf16[2,64,1024]{2,1,0:T(8,128)(2,1)S(1)}, u32[]{:S(2)}) copy-start(bf16[2,64,1024]{2,1,0:T(8,128)(2,1)S(1)} %get-tuple-element.114.own) | copy-start | bytes 786436
  45.4 7.7 %collective-permute-start.6 = (bf16[2,64,1024]{2,1,0:T(8,128)(2,1)S(1)}, bf16[2,64,1024]{2,1,0:T(8,128)(2,1)S(1)}, u32[]{:S(2)}, u32[]{:S(2)}) collective-permute-start(bf16[2,64,1024]{2,1,0:T(8,128)(2,1)S(1)} %get-tuple-element.114.own), channel_id=1, source_target_pairs={{0,1},{1,0},{2,3},{3,2},{4,5},{5,4},{6,7},{7,6},{8,9},{9,8},{10,11... | collective-permute-start | bytes 786440 | tf_op jit(solution)/shard_map/ppermute | solution.py:396
  53.2 5.9 %collective-permute-start.8 = (bf16[2,64,1024]{2,1,0:T(8,128)(2,1)S(1)}, bf16[2,64,1024]{2,1,0:T(8,128)(2,1)S(1)}, u32[]{:S(2)}, u32[]{:S(2)}) collective-permute-start(bf16[2,64,1024]{2,1,0:T(8,128)(2,1)S(1)} %pad_maximum_fusion.3), channel_id=1, source_target_pairs={{2,0},{4,2},{6,4},{8,6},{10,8},{12,10},{14,12},{16,14},{18,16},{20... | collective-permute-start | bytes 786440 | tf_op jit(solution)/shard_map/ppermute | solution.py:392
  55.2 5.2 %collective-permute-start.7 = (bf16[2,64,1024]{2,1,0:T(8,128)(2,1)}, bf16[2,64,1024]{2,1,0:T(8,128)(2,1)S(1)}, u32[]{:S(2)}, u32[]{:S(2)}) collective-permute-start(bf16[2,64,1024]{2,1,0:T(8,128)(2,1)} %pad_maximum_fusion.2), channel_id=1, source_target_pairs={{0,2},{2,4},{4,6},{6,8},{8,10},{10,12},{12,14},{14,16},{16,18},{18... | collective-permute-start | bytes 786440 | tf_op jit(solution)/shard_map/ppermute | solution.py:387
  61.4 1.2 copy-start.13
  62.5 1.0 copy-start.14
  67.1 12.2 %copy-start.7 = (bf16[2,128,1024]{2,1,0:T(8,128)(2,1)}, bf16[2,128,1024]{2,1,0:T(8,128)(2,1)S(1)}, u32[]{:S(2)}) copy-start(bf16[2,128,1024]{2,1,0:T(8,128)(2,1)S(1)} %get-tuple-element.121.grads) | copy-start | bytes 1572868
  67.2 12.2 %collective-permute-start.10 = (bf16[128,1024]{1,0:T(8,128)(2,1)S(1)}, bf16[128,1024]{1,0:T(8,128)(2,1)S(1)}, u32[]{:S(2)}, u32[]{:S(2)}) collective-permute-start(bf16[128,1024]{1,0:T(8,128)(2,1)S(1)} %get-tuple-element.118), channel_id=1, source_target_pairs={{2,0},{4,2},{6,4},{8,6},{10,8},{12,10},{14,12},{16,14},{18,16},{20... | collective-permute-start | bytes 786440 | tf_op jit(solution)/shard_map/ppermute | solution.py:392
  68.5 11.6 %collective-permute-start.9 = (bf16[128,1024]{1,0:T(8,128)(2,1)S(1)}, bf16[128,1024]{1,0:T(8,128)(2,1)S(1)}, u32[]{:S(2)}, u32[]{:S(2)}) collective-permute-start(bf16[128,1024]{1,0:T(8,128)(2,1)S(1)} %get-tuple-element.117), channel_id=1, source_target_pairs={{0,2},{2,4},{4,6},{6,8},{8,10},{10,12},{12,14},{14,16},{16,18},{18... | collective-permute-start | bytes 786440 | tf_op jit(solution)/shard_map/ppermute | solution.py:387
  80.8 9.9 %collective-permute-start.11 = (bf16[1728,128]{1,0:T(8,128)(2,1)S(1)}, bf16[1728,128]{1,0:T(8,128)(2,1)}, u32[]{:S(2)}, u32[]{:S(2)}) collective-permute-start(bf16[1728,128]{1,0:T(8,128)(2,1)S(1)} %broadcast_select_fusion.2), channel_id=1, source_target_pairs={{0,2},{2,0},{4,6},{6,4},{8,10},{10,8},{12,14},{14,12},{16,18},{18,... | collective-permute-start | bytes 1327112 | tf_op jit(solution)/shard_map/ppermute | solution.py:410
  84.7 1.0 copy-start.8
  90.7 11.3 %copy-start.6 = (bf16[4,64,4096]{2,1,0:T(8,128)(2,1)S(1)}, bf16[4,64,4096]{2,1,0:T(8,128)(2,1)}, u32[]{:S(2)}) copy-start(bf16[4,64,4096]{2,1,0:T(8,128)(2,1)} %copy-done.5) | copy-start | bytes 6291460
  90.7 11.3 %copy-start.20 = (bf16[128,256]{1,0:T(8,128)(2,1)S(1)}, bf16[128,256]{1,0:T(8,128)(2,1)}, u32[]{:S(2)}) copy-start(bf16[128,256]{1,0:T(8,128)(2,1)} %constant.27.clone.unpool) | copy-start | bytes 196612
  92.1 13.1 %copy-start.1 = (bf16[2,32,4096]{2,1,0:T(8,128)(2,1)S(1)}, bf16[2,32,4096]{2,1,0:T(8,128)(2,1)}, u32[]{:S(2)}) copy-start(bf16[2,32,4096]{2,1,0:T(8,128)(2,1)} %copy-done) | copy-start | bytes 1572868
  92.1 13.0 %copy-start.3 = (bf16[2,32,4096]{2,1,0:T(8,128)(2,1)S(1)}, bf16[2,32,4096]{2,1,0:T(8,128)(2,1)}, u32[]{:S(2)}) copy-start(bf16[2,32,4096]{2,1,0:T(8,128)(2,1)} %copy-done.2) | copy-start | bytes 1572868
  92.1 9.8 %collective-permute-start.13 = (bf16[2,64,1024]{2,1,0:T(8,128)(2,1)S(1)}, bf16[2,64,1024]{2,1,0:T(8,128)(2,1)S(1)}, u32[]{:S(2)}, u32[]{:S(2)}) collective-permute-start(bf16[2,64,1024]{2,1,0:T(8,128)(2,1)S(1)} %get-tuple-element.132), channel_id=1, source_target_pairs={{0,1},{1,0},{2,3},{3,2},{4,5},{5,4},{6,7},{7,6},{8,9},{9,8},{10,11... | collective-permute-start | bytes 786440 | tf_op jit(solution)/shard_map/ppermute | solution.py:396
  93.7 8.2 %collective-permute-start.12 = (bf16[864,128]{1,0:T(8,128)(2,1)S(1)}, bf16[864,128]{1,0:T(8,128)(2,1)S(1)}, u32[]{:S(2)}, u32[]{:S(2)}) collective-permute-start(bf16[864,128]{1,0:T(8,128)(2,1)S(1)} %broadcast_select_fusion.5), channel_id=1, source_target_pairs={{0,4},{2,6},{4,0},{6,2},{8,12},{10,14},{12,8},{14,10},{16,20},{18,... | collective-permute-start | bytes 663560 | tf_op jit(solution)/shard_map/ppermute | solution.py:410
  103.4 8.5 %collective-permute-start.16 = (bf16[864,128]{1,0:T(8,128)(2,1)S(1)}, bf16[864,128]{1,0:T(8,128)(2,1)S(1)}, u32[]{:S(2)}, u32[]{:S(2)}) collective-permute-start(bf16[864,128]{1,0:T(8,128)(2,1)S(1)} %add_convert_fusion.3), channel_id=1, source_target_pairs={{0,8},{2,10},{4,12},{6,14},{8,0},{10,2},{12,4},{14,6},{16,24},{18,... | collective-permute-start | bytes 663560 | tf_op jit(solution)/shard_map/ppermute | solution.py:410
  111.9 13.0 %copy-start.22 = (bf16[864,128]{1,0:T(8,128)(2,1)}, bf16[864,128]{1,0:T(8,128)(2,1)S(1)}, u32[]{:S(2)}) copy-start(bf16[864,128]{1,0:T(8,128)(2,1)S(1)} %add_convert_fusion.2) | copy-start | bytes 663556
  112.0 13.0 %collective-permute-start.17 = (bf16[864,128]{1,0:T(8,128)(2,1)S(1)}, bf16[864,128]{1,0:T(8,128)(2,1)S(1)}, u32[]{:S(2)}, u32[]{:S(2)}) collective-permute-start(bf16[864,128]{1,0:T(8,128)(2,1)S(1)} %add_convert_fusion.2), channel_id=1, source_target_pairs={{0,16},{2,18},{4,20},{6,22},{8,24},{10,26},{12,28},{14,30},{16,0},... | collective-permute-start | bytes 663560 | tf_op jit(solution)/shard_map/ppermute | solution.py:410
  114.6 14.3 %collective-permute-start.14 = (bf16[64,4096]{1,0:T(8,128)(2,1)}, bf16[64,4096]{1,0:T(8,128)(2,1)}, u32[]{:S(2)}, u32[]{:S(2)}) collective-permute-start(bf16[64,4096]{1,0:T(8,128)(2,1)} %get-tuple-element.136), channel_id=1, source_target_pairs={{0,2},{2,4},{4,6},{6,8},{8,10},{10,12},{12,14},{14,16},{16,18},{18... | collective-permute-start | bytes 1572872 | tf_op jit(solution)/shard_map/ppermute | solution.py:387
  116.7 12.2 %collective-permute-start.15 = (bf16[64,4096]{1,0:T(8,128)(2,1)}, bf16[64,4096]{1,0:T(8,128)(2,1)}, u32[]{:S(2)}, u32[]{:S(2)}) collective-permute-start(bf16[64,4096]{1,0:T(8,128)(2,1)} %get-tuple-element.137), channel_id=1, source_target_pairs={{2,0},{4,2},{6,4},{8,6},{10,8},{12,10},{14,12},{16,14},{18,16},{20... | collective-permute-start | bytes 1572872 | tf_op jit(solution)/shard_map/ppermute | solution.py:392
  128.9 8.5 %collective-permute-start.19 = (bf16[864,128]{1,0:T(8,128)(2,1)S(1)}, bf16[864,128]{1,0:T(8,128)(2,1)S(1)}, u32[]{:S(2)}, u32[]{:S(2)}) collective-permute-start(bf16[864,128]{1,0:T(8,128)(2,1)S(1)} %add_convert_fusion.1), channel_id=1, source_target_pairs={{0,4},{2,6},{4,0},{6,2},{8,12},{10,14},{12,8},{14,10},{16,20},{18,... | collective-permute-start | bytes 663560 | tf_op jit(solution)/shard_map/ppermute | solution.py:410
  131.4 4.3 %collective-permute-start.18 = (bf16[448,128]{1,0:T(8,128)(2,1)S(1)}, bf16[448,128]{1,0:T(8,128)(2,1)S(1)}, u32[]{:S(2)}, u32[]{:S(2)}) collective-permute-start(bf16[448,128]{1,0:T(8,128)(2,1)S(1)} %broadcast_select_fusion.8), channel_id=1, source_target_pairs={{0,2},{2,0},{4,6},{6,4},{8,10},{10,8},{12,14},{14,12},{16,18},{18,... | collective-permute-start | bytes 344072 | tf_op jit(solution)/shard_map/ppermute | solution.py:410
  137.6 8.8 %collective-permute-start.21 = (bf16[1728,128]{1,0:T(8,128)(2,1)S(1)}, bf16[1728,128]{1,0:T(8,128)(2,1)S(1)}, u32[]{:S(2)}, u32[]{:S(2)}) collective-permute-start(bf16[1728,128]{1,0:T(8,128)(2,1)S(1)} %pad_maximum_fusion.1), channel_id=1, source_target_pairs={{0,2},{2,0},{4,6},{6,4},{8,10},{10,8},{12,14},{14,12},{16,18},{18,... | collective-permute-start | bytes 1327112 | tf_op jit(solution)/shard_map/ppermute | solution.py:410
  137.7 8.7 %collective-permute-start.22 = (bf16[4,32,1024]{2,1,0:T(8,128)(2,1)S(1)}, bf16[4,32,1024]{2,1,0:T(8,128)(2,1)S(1)}, u32[]{:S(2)}, u32[]{:S(2)}) collective-permute-start(bf16[4,32,1024]{2,1,0:T(8,128)(2,1)S(1)} %get-tuple-element.187), channel_id=1, source_target_pairs={{0,1},{1,0},{2,3},{3,2},{4,5},{5,4},{6,7},{7,6},{8,9},{9,8},{10,11... | collective-permute-start | bytes 786440 | tf_op jit(solution)/shard_map/ppermute | solution.py:396
  138.9 5.7 %collective-permute-start.20 = (bf16[224,128]{1,0:T(8,128)(2,1)S(1)}, bf16[224,128]{1,0:T(8,128)(2,1)S(1)}, u32[]{:S(2)}, u32[]{:S(2)}) collective-permute-start(bf16[224,128]{1,0:T(8,128)(2,1)S(1)} %broadcast_select_fusion.11), channel_id=1, source_target_pairs={{0,4},{2,6},{4,0},{6,2},{8,12},{10,14},{12,8},{14,10},{16,20},{18,... | collective-permute-start | bytes 172040 | tf_op jit(solution)/shard_map/ppermute | solution.py:410
  146.4 8.0 %collective-permute-start.24 = (bf16[4,32,1024]{2,1,0:T(8,128)(2,1)S(1)}, bf16[4,32,1024]{2,1,0:T(8,128)(2,1)S(1)}, u32[]{:S(2)}, u32[]{:S(2)}) collective-permute-start(bf16[4,32,1024]{2,1,0:T(8,128)(2,1)S(1)} %get-tuple-element.200), channel_id=1, source_target_pairs={{0,1},{1,0},{2,3},{3,2},{4,5},{5,4},{6,7},{7,6},{8,9},{9,8},{10,11... | collective-permute-start | bytes 786440 | tf_op jit(solution)/shard_map/ppermute | solution.py:396
  147.6 6.8 %collective-permute-start.23 = (bf16[224,128]{1,0:T(8,128)(2,1)S(1)}, bf16[224,128]{1,0:T(8,128)(2,1)S(1)}, u32[]{:S(2)}, u32[]{:S(2)}) collective-permute-start(bf16[224,128]{1,0:T(8,128)(2,1)S(1)} %add_convert_fusion.7), channel_id=1, source_target_pairs={{0,8},{2,10},{4,12},{6,14},{8,0},{10,2},{12,4},{14,6},{16,24},{18,... | collective-permute-start | bytes 172040 | tf_op jit(solution)/shard_map/ppermute | solution.py:410
  154.5 9.5 %collective-permute-start.26 = (bf16[4,32,1024]{2,1,0:T(8,128)(2,1)S(1)}, bf16[4,32,1024]{2,1,0:T(8,128)(2,1)S(1)}, u32[]{:S(2)}, u32[]{:S(2)}) collective-permute-start(bf16[4,32,1024]{2,1,0:T(8,128)(2,1)S(1)} %get-tuple-element.213), channel_id=1, source_target_pairs={{0,1},{1,0},{2,3},{3,2},{4,5},{5,4},{6,7},{7,6},{8,9},{9,8},{10,11... | collective-permute-start | bytes 786440 | tf_op jit(solution)/shard_map/ppermute | solution.py:396
  155.6 8.4 %collective-permute-start.25 = (bf16[224,128]{1,0:T(8,128)(2,1)S(1)}, bf16[224,128]{1,0:T(8,128)(2,1)S(1)}, u32[]{:S(2)}, u32[]{:S(2)}) collective-permute-start(bf16[224,128]{1,0:T(8,128)(2,1)S(1)} %add_convert_fusion.6), channel_id=1, source_target_pairs={{0,16},{2,18},{4,20},{6,22},{8,24},{10,26},{12,28},{14,30},{16,0},... | collective-permute-start | bytes 172040 | tf_op jit(solution)/shard_map/ppermute | solution.py:410
  164.0 6.4 %collective-permute-start.28 = (bf16[4,32,1024]{2,1,0:T(8,128)(2,1)S(1)}, bf16[4,32,1024]{2,1,0:T(8,128)(2,1)S(1)}, u32[]{:S(2)}, u32[]{:S(2)}) collective-permute-start(bf16[4,32,1024]{2,1,0:T(8,128)(2,1)S(1)} %get-tuple-element.219), channel_id=1, source_target_pairs={{0,1},{1,0},{2,3},{3,2},{4,5},{5,4},{6,7},{7,6},{8,9},{9,8},{10,11... | collective-permute-start | bytes 786440 | tf_op jit(solution)/shard_map/ppermute | solution.py:396
  165.0 4.8 %collective-permute-start.27 = (bf16[224,128]{1,0:T(8,128)(2,1)S(1)}, bf16[224,128]{1,0:T(8,128)(2,1)S(1)}, u32[]{:S(2)}, u32[]{:S(2)}) collective-permute-start(bf16[224,128]{1,0:T(8,128)(2,1)S(1)} %add_convert_fusion.5), channel_id=1, source_target_pairs={{0,4},{2,6},{4,0},{6,2},{8,12},{10,14},{12,8},{14,10},{16,20},{18,... | collective-permute-start | bytes 172040 | tf_op jit(solution)/shard_map/ppermute | solution.py:410
  170.5 3.1 %collective-permute-start.29 = (bf16[448,128]{1,0:T(8,128)(2,1)S(1)}, bf16[448,128]{1,0:T(8,128)(2,1)S(1)}, u32[]{:S(2)}, u32[]{:S(2)}) collective-permute-start(bf16[448,128]{1,0:T(8,128)(2,1)S(1)} %pad_maximum_fusion.5), channel_id=1, source_target_pairs={{0,2},{2,0},{4,6},{6,4},{8,10},{10,8},{12,14},{14,12},{16,18},{18,... | collective-permute-start | bytes 344072 | tf_op jit(solution)/shard_map/ppermute | solution.py:410
  (7 other events, 6.0 us)

commit v3 on v2

--- a/solution.py
+++ b/solution.py
@@ -14,7 +14,6 @@
 LANES = 128
 BF = jnp.bfloat16
 F32 = jnp.float32
-VMEM_LIMIT = 24 * 2**20
 TILES = HH // 4
 ROWS = 16
 
@@ -27,7 +26,7 @@
     return lax.dot_general(a, b, (((1,), (1,)), ((), ())), preferred_element_type=F32)
 
 
-def call(body, outs, name, scratch=(), scalars=0, inputs=0):
+def call(body, outs, name, scratch=(), scalars=0, inputs=0, mib=12):
     specs = [pl.BlockSpec(memory_space=pltpu.SMEM)] * scalars
     specs += [pl.BlockSpec(memory_space=pltpu.VMEM)] * inputs
     return pl.pallas_call(
@@ -36,7 +35,7 @@
         in_specs=specs,
         out_specs=[pl.BlockSpec(memory_space=pltpu.VMEM)] * len(outs),
         scratch_shapes=list(scratch),
-        compiler_params=pltpu.CompilerParams(vmem_limit_bytes=VMEM_LIMIT),
+        compiler_params=pltpu.CompilerParams(vmem_limit_bytes=mib * 2**20),
         name=name,
     )
 
@@ -194,11 +193,11 @@
     lax.fori_loop(0, TILES, chunk, 0, unroll=2)
 
 
-def forward_coarse_kernel(filt, own, peer, low, high, weights, cot, spread, grads, windows, first_out, last_out):
+def forward_coarse_kernel(filt, own, peer, low, high, plow, phigh, weights, cot, spread, grads, windows, first_out, last_out):
     planes, chans, cells = own.shape
     mine = pl.multiple_of(filt[0] * chans, 32)
     theirs = pl.multiple_of((1 - filt[0]) * chans, 32)
-    sides = ((mine, low.at[0], own, high.at[0]), (theirs, low.at[1], peer, high.at[1]))
+    sides = ((mine, low, own, high), (theirs, plow, peer, phigh))
     for offset, below, middle, above in sides:
         refs = [below] + [middle.at[d] for d in range(planes)] + [above]
         for plane, ref in enumerate(refs):
@@ -523,11 +522,12 @@
         [pltpu.VMEM((planes + 2, 6 * own_in, (HH + 2) * LANES), BF)],
         scalars=1,
         inputs=9,
+        mib=20,
     )(which, *volumes, fine_forward, pool)
 
     pooled_peer = swap(pooled)
-    pool_low = to_next(jnp.stack([pooled[half_planes - 1], pooled_peer[half_planes - 1]]))
-    pool_high = to_previous(jnp.stack([pooled[0], pooled_peer[0]]))
+    pool_low, pool_high = to_next(pooled[half_planes - 1]), to_previous(pooled[0])
+    peer_low, peer_high = to_next(pooled_peer[half_planes - 1]), to_previous(pooled_peer[0])
     coarse_lanes = (TILES + 2) * LANES
     grad_four, coarse_windows, four_first, four_last = call(
         forward_coarse_kernel,
@@ -539,13 +539,15 @@
         ],
         "forward_coarse",
         scalars=1,
-        inputs=7,
+        inputs=9,
     )(
         which,
         pooled,
         pooled_peer,
         pool_low,
         pool_high,
+        peer_low,
+        peer_high,
         wide_forward,
         cotangent.reshape(outs, -1),
         spread,
@@ -593,6 +595,7 @@
                 [pltpu.VMEM((end - start, 6 * own_in, (HH + 2) * LANES), BF)],
                 scalars=1,
                 inputs=8 + len(fine_kernel),
+                mib=16,
             ),
             (which, *volumes, grad_three.reshape(planes * mid, cells), *fine_kernel),
         )

time: 176 us -> 176 us (level)
  waiting for transfers between devices: 31.1 us -> 23.3 us
  starting transfers between devices: 58.3 us -> 63.7 us
  local copies, waits for them, and re-layouts: 21.9 us -> 25.1 us
    ppermute x8, waiting for transfers between devices: 20.2 us -> 12.9 us  [swap(): return lax.ppermute(value, 'filt', [(0, 1), (1, 0)])]
    ppermute x12, starting transfers between devices: 22.1 us -> 24.3 us  [across(): return lax.ppermute(value, 'depth', [(i, i ^ bit) for i in range(count)])]
    unnamed x54 -> x52, local copies, waits for them, and re-layouts: 17 us -> 18.9 us
    ppermute x5 -> x6, starting transfers between devices: 18.3 us -> 19.9 us  [to_next(): return lax.ppermute(value, 'depth', [(i, i + 1) for i in range(count - 1)])]
    ppermute x5 -> x6, starting transfers between devices: 6.64 us -> 8.11 us  [to_previous(): return lax.ppermute(value, 'depth', [(i + 1, i) for i in range(count - 1)])]
  transfers between devices with their start and end apart: 30 -> 32, of which waited for: 9 -> 10; matrix products, arithmetic and copies ran while one was open for 7% -> 7% of each run, Pallas kernels for 21% -> 21%
where the time goes in v3:
time: 176 us; the launch traced here: 175 us
  starting transfers between devices  63.7 us (36%)
  Pallas kernels  56.5 us (32%)
  local copies, waits for them, and re-layouts  25.1 us (14%)
  waiting for transfers between devices  23.3 us (13%)
  other arithmetic  5.13 us (3%)
    pallas_call x7, Pallas kernels, beside(): kernel(*inputs)  34 us
    ppermute x12, starting transfers between devices, across(): return lax.ppermute(value, 'depth', [(i, i ^ bit) for i in range(count)])  24.3 us
    ppermute x6, starting transfers between devices, to_next(): return lax.ppermute(value, 'depth', [(i, i + 1) for i in range(count - 1)])  19.9 us
    unnamed x52, local copies, waits for them, and re-layouts  18.9 us
    pallas_call x1, Pallas kernels, body(): call(forward_fine_kernel, [((half_planes, mid, coarse), BF), ((planes, mi...  14.5 us
    ppermute x8, waiting for transfers between devices, swap(): return lax.ppermute(value, 'filt', [(0, 1), (1, 0)])  12.9 us
    ppermute x8, starting transfers between devices, swap(): return lax.ppermute(value, 'filt', [(0, 1), (1, 0)])  11.3 us
    ppermute x12, waiting for transfers between devices, across(): return lax.ppermute(value, 'depth', [(i, i ^ bit) for i in range(count)])  8.74 us
  transfers between devices with their start and end apart: 32, of which 10 were waited for; matrix products, arithmetic and copies ran while one was open for 7% of the time, Pallas kernels for 21%

profile of v3, /device:TPU:0, one launch (start us, length us, event | category | flops | bytes accessed | tf_op | source)
XLA Modules:
  0.0 174.9 jit_solution(7265715448193448265)
XLA Ops:
  0.6 1.8 %copy.18 = bf16[32,4,4096]{2,0,1:T(8,128)(2,1)S(1)} copy(bf16[32,4,4096]{2,1,0:T(4,128)(2,1)} %param.7) | data formatting | bytes 2097152 | tf_op args[0]
  3.4 3.0 %collective-permute-start.2 = (bf16[2,32,4096]{2,1,0:T(8,128)(2,1)S(1)}, bf16[2,32,4096]{2,1,0:T(8,128)(2,1)S(1)}, u32[]{:S(2)}, u32[]{:S(2)}) collective-permute-start(bf16[2,32,4096]{2,1,0:T(8,128)(2,1)S(1)} %pad_maximum_fusion), channel_id=1, source_target_pairs={{0,1},{1,0},{2,3},{3,2},{4,5},{5,4},{6,7},{7,6},{8,9},{9,8},{10,11... | collective-permute-start | bytes 1572872 | tf_op jit(solution)/shard_map/ppermute | solution.py:395
  6.4 2.2 %collective-permute-start = (bf16[32,4096]{1,0:T(8,128)(2,1)}, bf16[32,4096]{1,0:T(8,128)(2,1)}, u32[]{:S(2)}, u32[]{:S(2)}) collective-permute-start(bf16[32,4096]{1,0:T(8,128)(2,1)} %get-tuple-element.230), channel_id=1, source_target_pairs={{0,2},{2,4},{4,6},{6,8},{8,10},{10,12},{12,14},{14,16},{16,18},{18... | collective-permute-start | bytes 786440 | tf_op jit(solution)/shard_map/ppermute | solution.py:386
  8.6 1.3 collective-permute-start.1
  11.1 8.0 %collective-permute-done.2.refs_5_ = bf16[2,32,4096]{2,1,0:T(8,128)(2,1)S(1)} collective-permute-done((bf16[2,32,4096]{2,1,0:T(8,128)(2,1)S(1)}, bf16[2,32,4096]{2,1,0:T(8,128)(2,1)S(1)}, u32[]{:S(2)}, u32[]{:S(2)}) %collective-permute-start.2) | collective-permute-done | bytes 524320 | tf_op jit(solution)/shard_map/ppermute | solution.py:395
  20.0 2.0 %collective-permute-start.3 = (bf16[32,4096]{1,0:T(8,128)(2,1)}, bf16[32,4096]{1,0:T(8,128)(2,1)}, u32[]{:S(2)}, u32[]{:S(2)}) collective-permute-start(bf16[32,4096]{1,0:T(8,128)(2,1)} %get-tuple-element.236), channel_id=1, source_target_pairs={{0,2},{2,4},{4,6},{6,8},{8,10},{10,12},{12,14},{14,16},{16,18},{18... | collective-permute-start | bytes 786440 | tf_op jit(solution)/shard_map/ppermute | solution.py:386
  22.0 1.3 collective-permute-start.4
  23.3 1.9 %copy.14.fine = bf16[1728,64]{1,0:T(8,128)(2,1)} copy(bf16[1728,64]{0,1:T(8,128)(2,1)} %param.8) | data formatting | bytes 442368 | tf_op args[1]
  27.7 1.9 %collective-permute-done.5.refs_6_ = bf16[2,32,4096]{2,1,0:T(8,128)(2,1)S(1)} collective-permute-done((bf16[2,32,4096]{2,1,0:T(8,128)(2,1)}, bf16[2,32,4096]{2,1,0:T(8,128)(2,1)S(1)}, u32[]{:S(2)}, u32[]{:S(2)}) %collective-permute-start.5) | collective-permute-done | bytes 524320 | tf_op jit(solution)/shard_map/ppermute | solution.py:395
  29.6 14.5 %forward_fine.1 = (bf16[2,64,1024]{2,1,0:T(8,128)(2,1)S(1)}, bf16[4,64,4096]{2,1,0:T(8,128)(2,1)S(1)}) custom-call(s32[1]{0:T(128)} %bitcast.filt, bf16[4,32,4096]{2,1,0:T(8,128)(2,1)S(1)} %bitcast.29, bf16[32,4096]{1,0:T(8,128)(2,1)} %collective-permute-done.refs_1_, bf16[32,4096]{1,0:T(8,128)(2,1)} %collective-permute-done.1.refs_2_, ...), custom_call_target="tpu_custom_call" | custom-call | tf_op jit(solution)/shard_map/forward_fine/pallas_call | solution.py:518
  44.1 1.3 copy-done.5
  45.4 1.7 collective-permute-start.6
  47.8 3.8 %collective-permute-start.7 = (bf16[64,1024]{1,0:T(8,128)(2,1)}, bf16[64,1024]{1,0:T(8,128)(2,1)S(1)}, u32[]{:S(2)}, u32[]{:S(2)}) collective-permute-start(bf16[64,1024]{1,0:T(8,128)(2,1)} %get-tuple-element.242), channel_id=1, source_target_pairs={{0,2},{2,4},{4,6},{6,8},{8,10},{10,12},{12,14},{14,16},{16,18},{18... | collective-permute-start | bytes 393224 | tf_op jit(solution)/shard_map/ppermute | solution.py:386
  51.6 1.3 collective-permute-start.8
  53.9 1.3 collective-permute-start.10
  55.1 3.8 %collective-permute-start.9 = (bf16[64,1024]{1,0:T(8,128)(2,1)}, bf16[64,1024]{1,0:T(8,128)(2,1)S(1)}, u32[]{:S(2)}, u32[]{:S(2)}) collective-permute-start(bf16[64,1024]{1,0:T(8,128)(2,1)} %get-tuple-element.240), channel_id=1, source_target_pairs={{0,2},{2,4},{4,6},{6,8},{8,10},{10,12},{12,14},{14,16},{16,18},{18... | collective-permute-start | bytes 393224 | tf_op jit(solution)/shard_map/ppermute | solution.py:386
  63.3 3.6 %forward_coarse.1 = (bf16[2,128,1024]{2,1,0:T(8,128)(2,1)S(1)}, bf16[4,384,1280]{2,1,0:T(8,128)(2,1)S(1)}, bf16[128,1024]{1,0:T(8,128)(2,1)S(1)}, bf16[128,1024]{1,0:T(8,128)(2,1)S(1)}) custom-call(s32[1]{0:T(128)} %bitcast.filt, bf16[2,64,1024]{2,1,0:T(8,128)(2,1)S(1)} %copy-done.11, bf16[2,64,1024]{2,1,0:T(8,128)(2,1)S(1)} %collective-permute-done.6.peer, ...), custom_call_target="tpu_custom_call" | custom-call | tf_op jit(solution)/shard_map/forward_coarse/pallas_call | solution.py:532
  66.9 6.1 %collective-permute-start.11 = (bf16[128,1024]{1,0:T(8,128)(2,1)S(1)}, bf16[128,1024]{1,0:T(8,128)(2,1)S(1)}, u32[]{:S(2)}, u32[]{:S(2)}) collective-permute-start(bf16[128,1024]{1,0:T(8,128)(2,1)S(1)} %get-tuple-element.117), channel_id=1, source_target_pairs={{0,2},{2,4},{4,6},{6,8},{8,10},{10,12},{12,14},{14,16},{16,18},{18... | collective-permute-start | bytes 786440 | tf_op jit(solution)/shard_map/ppermute | solution.py:386
  73.0 1.5 collective-permute-start.12
  74.5 2.6 %kernel_grad_coarse.1 = bf16[3456,128]{1,0:T(8,128)(2,1)S(1)} custom-call(bf16[4,384,1280]{2,1,0:T(8,128)(2,1)S(1)} %get-tuple-element.119.windows, bf16[256,1024]{1,0:T(8,128)(2,1)S(1)} %bitcast.32), custom_call_target="tpu_custom_call" | custom-call | tf_op jit(solution)/shard_map/kernel_grad_coarse/pallas_call | solution.py:557
  79.0 4.8 %collective-permute-start.13 = (bf16[1728,128]{1,0:T(8,128)(2,1)S(1)}, bf16[1728,128]{1,0:T(8,128)(2,1)}, u32[]{:S(2)}, u32[]{:S(2)}) collective-permute-start(bf16[1728,128]{1,0:T(8,128)(2,1)S(1)} %broadcast_select_fusion.2), channel_id=1, source_target_pairs={{0,2},{2,0},{4,6},{6,4},{8,10},{10,8},{12,14},{14,12},{16,18},{18,... | collective-permute-start | bytes 1327112 | tf_op jit(solution)/shard_map/ppermute | solution.py:409
  86.7 3.0 %backward_coarse.1 = (f32[2,64,1024]{2,1,0:T(8,128)S(1)}, bf16[2,64,1024]{2,1,0:T(8,128)(2,1)S(1)}) custom-call(s32[1]{0:T(128)} %bitcast.filt, bf16[2,128,1024]{2,1,0:T(8,128)(2,1)S(1)} %copy-done.8, bf16[128,1024]{1,0:T(8,128)(2,1)S(1)} %copy-done.16, bf16[128,1024]{1,0:T(8,128)(2,1)S(1)} %copy-done.18, bf16[3456,128]{1,0:T(8,128)(2,1)S(1)} %copy-done.4), custom_call_target="tpu_custom_call" | custom-call | tf_op jit(solution)/shard_map/backward_coarse/pallas_call | solution.py:463
  89.7 1.3 add_convert_fusion
  91.1 1.6 collective-permute-start.15
  92.7 3.8 %collective-permute-start.14 = (bf16[864,128]{1,0:T(8,128)(2,1)S(1)}, bf16[864,128]{1,0:T(8,128)(2,1)S(1)}, u32[]{:S(2)}, u32[]{:S(2)}) collective-permute-start(bf16[864,128]{1,0:T(8,128)(2,1)S(1)} %broadcast_select_fusion.5), channel_id=1, source_target_pairs={{0,4},{2,6},{4,0},{6,2},{8,12},{10,14},{12,8},{14,10},{16,20},{18,... | collective-permute-start | bytes 663560 | tf_op jit(solution)/shard_map/ppermute | solution.py:409
  96.5 5.3 %collective-permute-done.14 = bf16[864,128]{1,0:T(8,128)(2,1)S(1)} collective-permute-done((bf16[864,128]{1,0:T(8,128)(2,1)S(1)}, bf16[864,128]{1,0:T(8,128)(2,1)S(1)}, u32[]{:S(2)}, u32[]{:S(2)}) %collective-permute-start.14) | collective-permute-done | bytes 221216 | tf_op jit(solution)/shard_map/ppermute | solution.py:409
  101.9 1.4 grad_fine.1
  103.3 1.6 collective-permute-start.18
  104.9 6.7 %kernel_grad_fine_0.1.refs_8_ = f32[1728,64]{1,0:T(8,128)S(1)} custom-call(s32[1]{0:T(128)} %bitcast.filt, bf16[4,32,4096]{2,1,0:T(8,128)(2,1)S(1)} %bitcast.30, bf16[32,4096]{1,0:T(8,128)(2,1)} %collective-permute-done.refs_1_, bf16[32,4096]{1,0:T(8,128)(2,1)} %collective-permute-done.1.refs_2_, bf16[32,4096]{1,0:T(8,128)(2,1)} %collective-permute-done.3.refs_3_, ...), custom_call_target="tpu_custom_call" | custom-call | tf_op jit(solution)/shard_map/kernel_grad_fine_0/pallas_call | solution.py:463
  111.7 2.0 %collective-permute-start.19 = (bf16[864,128]{1,0:T(8,128)(2,1)S(1)}, bf16[864,128]{1,0:T(8,128)(2,1)S(1)}, u32[]{:S(2)}, u32[]{:S(2)}) collective-permute-start(bf16[864,128]{1,0:T(8,128)(2,1)S(1)} %add_convert_fusion.2), channel_id=1, source_target_pairs={{0,16},{2,18},{4,20},{6,22},{8,24},{10,26},{12,28},{14,30},{16,0},... | collective-permute-start | bytes 663560 | tf_op jit(solution)/shard_map/ppermute | solution.py:409
  113.7 2.1 %collective-permute-start.16 = (bf16[64,4096]{1,0:T(8,128)(2,1)}, bf16[64,4096]{1,0:T(8,128)(2,1)}, u32[]{:S(2)}, u32[]{:S(2)}) collective-permute-start(bf16[64,4096]{1,0:T(8,128)(2,1)} %get-tuple-element.136), channel_id=1, source_target_pairs={{0,2},{2,4},{4,6},{6,8},{8,10},{10,12},{12,14},{14,16},{16,18},{18... | collective-permute-start | bytes 1572872 | tf_op jit(solution)/shard_map/ppermute | solution.py:386
  115.8 1.5 collective-permute-start.17
  117.3 6.8 %kernel_grad_fine_3.1 = f32[1728,64]{1,0:T(8,128)S(1)} custom-call(s32[1]{0:T(128)} %bitcast.filt, bf16[4,32,4096]{2,1,0:T(8,128)(2,1)S(1)} %bitcast.31, bf16[32,4096]{1,0:T(8,128)(2,1)} %collective-permute-done.refs_1_, bf16[32,4096]{1,0:T(8,128)(2,1)} %collective-permute-done.1.refs_2_, bf16[32,4096]{1,0:T(8,128)(2,1)} %collective-permute-done.3.refs_3_, ...), custom_call_target="tpu_custom_call" | custom-call | tf_op jit(solution)/shard_map/kernel_grad_fine_3/pallas_call | solution.py:463
  128.0 3.1 %collective-permute-start.21 = (bf16[864,128]{1,0:T(8,128)(2,1)S(1)}, bf16[864,128]{1,0:T(8,128)(2,1)S(1)}, u32[]{:S(2)}, u32[]{:S(2)}) collective-permute-start(bf16[864,128]{1,0:T(8,128)(2,1)S(1)} %add_convert_fusion.1), channel_id=1, source_target_pairs={{0,4},{2,6},{4,0},{6,2},{8,12},{10,14},{12,8},{14,10},{16,20},{18,... | collective-permute-start | bytes 663560 | tf_op jit(solution)/shard_map/ppermute | solution.py:409
  131.1 4.3 %backward_fine_0.1 = (f32[4,32,1024]{2,1,0:T(8,128)S(1)}, bf16[4,32,1024]{2,1,0:T(8,128)(2,1)S(1)}) custom-call(s32[1]{0:T(128)} %bitcast.filt, bf16[4,64,4096]{2,1,0:T(8,128)(2,1)S(1)} %get-tuple-element.206.grads, bf16[64,4096]{1,0:T(8,128)(2,1)} %collective-permute-done.16.low, bf16[64,4096]{1,0:T(8,128)(2,1)} %collective-permute-done.17.high, ...), custom_call_target="tpu_custom_call" | custom-call | tf_op jit(solution)/shard_map/backward_fine_0/pallas_call | solution.py:463
  135.4 1.4 collective-permute-done.21
  137.0 1.2 collective-permute-start.24
  139.4 4.3 %backward_fine_1.1 = (f32[4,32,1024]{2,1,0:T(8,128)S(1)}, bf16[4,32,1024]{2,1,0:T(8,128)(2,1)S(1)}) custom-call(s32[1]{0:T(128)} %bitcast.filt, bf16[4,64,4096]{2,1,0:T(8,128)(2,1)S(1)} %get-tuple-element.206.grads, bf16[64,4096]{1,0:T(8,128)(2,1)} %collective-permute-done.16.low, bf16[64,4096]{1,0:T(8,128)(2,1)} %collective-permute-done.17.high, ...), custom_call_target="tpu_custom_call" | custom-call | tf_op jit(solution)/shard_map/backward_fine_1/pallas_call | solution.py:463
  143.7 2.1 %collective-permute-done.24 = bf16[4,32,1024]{2,1,0:T(8,128)(2,1)S(1)} collective-permute-done((bf16[4,32,1024]{2,1,0:T(8,128)(2,1)S(1)}, bf16[4,32,1024]{2,1,0:T(8,128)(2,1)S(1)}, u32[]{:S(2)}, u32[]{:S(2)}) %collective-permute-start.24) | collective-permute-done | bytes 262176 | tf_op jit(solution)/shard_map/ppermute | solution.py:395
  145.8 1.2 collective-permute-start.26
  147.0 2.2 %collective-permute-start.25 = (bf16[224,128]{1,0:T(8,128)(2,1)S(1)}, bf16[224,128]{1,0:T(8,128)(2,1)S(1)}, u32[]{:S(2)}, u32[]{:S(2)}) collective-permute-start(bf16[224,128]{1,0:T(8,128)(2,1)S(1)} %add_convert_fusion.7), channel_id=1, source_target_pairs={{0,8},{2,10},{4,12},{6,14},{8,0},{10,2},{12,4},{14,6},{16,24},{18,... | collective-permute-start | bytes 172040 | tf_op jit(solution)/shard_map/ppermute | solution.py:409
  149.4 4.3 %backward_fine_2.1 = (f32[4,32,1024]{2,1,0:T(8,128)S(1)}, bf16[4,32,1024]{2,1,0:T(8,128)(2,1)S(1)}) custom-call(s32[1]{0:T(128)} %bitcast.filt, bf16[4,64,4096]{2,1,0:T(8,128)(2,1)S(1)} %get-tuple-element.206.grads, bf16[64,4096]{1,0:T(8,128)(2,1)} %collective-permute-done.16.low, bf16[64,4096]{1,0:T(8,128)(2,1)} %collective-permute-done.17.high, ...), custom_call_target="tpu_custom_call" | custom-call | tf_op jit(solution)/shard_map/backward_fine_2/pallas_call | solution.py:463
  155.0 3.0 %collective-permute-start.27 = (bf16[224,128]{1,0:T(8,128)(2,1)S(1)}, bf16[224,128]{1,0:T(8,128)(2,1)S(1)}, u32[]{:S(2)}, u32[]{:S(2)}) collective-permute-start(bf16[224,128]{1,0:T(8,128)(2,1)S(1)} %add_convert_fusion.6), channel_id=1, source_target_pairs={{0,16},{2,18},{4,20},{6,22},{8,24},{10,26},{12,28},{14,30},{16,0},... | collective-permute-start | bytes 172040 | tf_op jit(solution)/shard_map/ppermute | solution.py:409
  158.0 1.3 convert_multiply_fusion
  159.4 4.5 %backward_fine_3.1 = (f32[4,32,1024]{2,1,0:T(8,128)S(1)}, bf16[4,32,1024]{2,1,0:T(8,128)(2,1)S(1)}) custom-call(s32[1]{0:T(128)} %bitcast.filt, bf16[4,64,4096]{2,1,0:T(8,128)(2,1)S(1)} %get-tuple-element.206.grads, bf16[64,4096]{1,0:T(8,128)(2,1)} %collective-permute-done.16.low, bf16[64,4096]{1,0:T(8,128)(2,1)} %collective-permute-done.17.high, ...), custom_call_target="tpu_custom_call" | custom-call | tf_op jit(solution)/shard_map/backward_fine_3/pallas_call | solution.py:463
  164.9 2.7 %collective-permute-start.29 = (bf16[224,128]{1,0:T(8,128)(2,1)S(1)}, bf16[224,128]{1,0:T(8,128)(2,1)S(1)}, u32[]{:S(2)}, u32[]{:S(2)}) collective-permute-start(bf16[224,128]{1,0:T(8,128)(2,1)S(1)} %add_convert_fusion.5), channel_id=1, source_target_pairs={{0,4},{2,6},{4,0},{6,2},{8,12},{10,14},{12,8},{14,10},{16,20},{18,... | collective-permute-start | bytes 172040 | tf_op jit(solution)/shard_map/ppermute | solution.py:409
  167.7 2.0 %collective-permute-done.29 = bf16[224,128]{1,0:T(8,128)(2,1)S(1)} collective-permute-done((bf16[224,128]{1,0:T(8,128)(2,1)S(1)}, bf16[224,128]{1,0:T(8,128)(2,1)S(1)}, u32[]{:S(2)}, u32[]{:S(2)}) %collective-permute-start.29) | collective-permute-done | bytes 57376 | tf_op jit(solution)/shard_map/ppermute | solution.py:409
  170.9 2.7 %copy.15 = f32[32,4,4096]{2,1,0:T(4,128)} copy(f32[32,4,4096]{2,0,1:T(8,128)S(1)} %maximum_bitcast_fusion) | data formatting | bytes 4194304
  (114 shorter events, 26.7 us)
Async XLA Ops:
  3.3 21.9 %copy-start.4 = (bf16[3456,128]{1,0:T(8,128)(2,1)S(1)}, bf16[3456,128]{1,0:T(8,128)(2,1)}, u32[]{:S(2)}) copy-start(bf16[3456,128]{1,0:T(8,128)(2,1)} %weights.2) | copy-start | bytes 2654212
  3.4 26.2 %copy-start.21 = (bf16[256,128]{1,0:T(8,128)(2,1)S(1)}, bf16[256,128]{1,0:T(8,128)(2,1)}, u32[]{:S(2)}) copy-start(bf16[256,128]{1,0:T(8,128)(2,1)} %constant.26.clone.refs_8_) | copy-start | bytes 196612
  3.4 15.8 %collective-permute-start.2 = (bf16[2,32,4096]{2,1,0:T(8,128)(2,1)S(1)}, bf16[2,32,4096]{2,1,0:T(8,128)(2,1)S(1)}, u32[]{:S(2)}, u32[]{:S(2)}) collective-permute-start(bf16[2,32,4096]{2,1,0:T(8,128)(2,1)S(1)} %pad_maximum_fusion), channel_id=1, source_target_pairs={{0,1},{1,0},{2,3},{3,2},{4,5},{5,4},{6,7},{7,6},{8,9},{9,8},{10,11... | collective-permute-start | bytes 1572872 | tf_op jit(solution)/shard_map/ppermute | solution.py:395
  6.4 21.2 %collective-permute-start = (bf16[32,4096]{1,0:T(8,128)(2,1)}, bf16[32,4096]{1,0:T(8,128)(2,1)}, u32[]{:S(2)}, u32[]{:S(2)}) collective-permute-start(bf16[32,4096]{1,0:T(8,128)(2,1)} %get-tuple-element.230), channel_id=1, source_target_pairs={{0,2},{2,4},{4,6},{6,8},{8,10},{10,12},{12,14},{14,16},{16,18},{18... | collective-permute-start | bytes 786440 | tf_op jit(solution)/shard_map/ppermute | solution.py:386
  8.6 19.1 %collective-permute-start.1 = (bf16[32,4096]{1,0:T(8,128)(2,1)}, bf16[32,4096]{1,0:T(8,128)(2,1)}, u32[]{:S(2)}, u32[]{:S(2)}) collective-permute-start(bf16[32,4096]{1,0:T(8,128)(2,1)} %get-tuple-element.231), channel_id=1, source_target_pairs={{2,0},{4,2},{6,4},{8,6},{10,8},{12,10},{14,12},{16,14},{18,16},{20... | collective-permute-start | bytes 786440 | tf_op jit(solution)/shard_map/ppermute | solution.py:391
  10.7 18.9 %collective-permute-start.5 = (bf16[2,32,4096]{2,1,0:T(8,128)(2,1)}, bf16[2,32,4096]{2,1,0:T(8,128)(2,1)S(1)}, u32[]{:S(2)}, u32[]{:S(2)}) collective-permute-start(bf16[2,32,4096]{2,1,0:T(8,128)(2,1)} %slice.91), channel_id=1, source_target_pairs={{0,1},{1,0},{2,3},{3,2},{4,5},{5,4},{6,7},{7,6},{8,9},{9,8},{10,11... | collective-permute-start | bytes 1572872 | tf_op jit(solution)/shard_map/ppermute | solution.py:395
  19.2 24.9 %copy-start = (bf16[2,32,4096]{2,1,0:T(8,128)(2,1)}, bf16[2,32,4096]{2,1,0:T(8,128)(2,1)S(1)}, u32[]{:S(2)}) copy-start(bf16[2,32,4096]{2,1,0:T(8,128)(2,1)S(1)} %collective-permute-done.2.refs_5_) | copy-start | bytes 1572868
  20.0 9.5 %collective-permute-start.3 = (bf16[32,4096]{1,0:T(8,128)(2,1)}, bf16[32,4096]{1,0:T(8,128)(2,1)}, u32[]{:S(2)}, u32[]{:S(2)}) collective-permute-start(bf16[32,4096]{1,0:T(8,128)(2,1)} %get-tuple-element.236), channel_id=1, source_target_pairs={{0,2},{2,4},{4,6},{6,8},{8,10},{10,12},{12,14},{14,16},{16,18},{18... | collective-permute-start | bytes 786440 | tf_op jit(solution)/shard_map/ppermute | solution.py:386
  22.0 7.6 %collective-permute-start.4 = (bf16[32,4096]{1,0:T(8,128)(2,1)}, bf16[32,4096]{1,0:T(8,128)(2,1)}, u32[]{:S(2)}, u32[]{:S(2)}) collective-permute-start(bf16[32,4096]{1,0:T(8,128)(2,1)} %get-tuple-element.235), channel_id=1, source_target_pairs={{2,0},{4,2},{6,4},{8,6},{10,8},{12,10},{14,12},{16,14},{18,16},{20... | collective-permute-start | bytes 786440 | tf_op jit(solution)/shard_map/ppermute | solution.py:391
  29.6 24.3 %copy-start.2 = (bf16[2,32,4096]{2,1,0:T(8,128)(2,1)}, bf16[2,32,4096]{2,1,0:T(8,128)(2,1)S(1)}, u32[]{:S(2)}) copy-start(bf16[2,32,4096]{2,1,0:T(8,128)(2,1)S(1)} %collective-permute-done.5.refs_6_) | copy-start | bytes 1572868
  29.6 30.6 %copy-start.19 = (bf16[128,1,256]{2,0,1:T(8,128)(2,1)S(1)}, bf16[128,1,256]{2,0,1:T(8,128)(2,1)}, u32[]{:S(2)}) copy-start(bf16[128,1,256]{2,0,1:T(8,128)(2,1)} %param.10) | copy-start | bytes 196612
  44.1 1.3 copy-start.5
  45.4 8.4 %copy-start.10 = (bf16[2,64,1024]{2,1,0:T(8,128)(2,1)}, bf16[2,64,1024]{2,1,0:T(8,128)(2,1)S(1)}, u32[]{:S(2)}) copy-start(bf16[2,64,1024]{2,1,0:T(8,128)(2,1)S(1)} %get-tuple-element.114.own) | copy-start | bytes 786436
  45.4 7.7 %collective-permute-start.6 = (bf16[2,64,1024]{2,1,0:T(8,128)(2,1)S(1)}, bf16[2,64,1024]{2,1,0:T(8,128)(2,1)S(1)}, u32[]{:S(2)}, u32[]{:S(2)}) collective-permute-start(bf16[2,64,1024]{2,1,0:T(8,128)(2,1)S(1)} %get-tuple-element.114.own), channel_id=1, source_target_pairs={{0,1},{1,0},{2,3},{3,2},{4,5},{5,4},{6,7},{7,6},{8,9},{9,8},{10,11... | collective-permute-start | bytes 786440 | tf_op jit(solution)/shard_map/ppermute | solution.py:395
  47.8 11.2 %collective-permute-start.7 = (bf16[64,1024]{1,0:T(8,128)(2,1)}, bf16[64,1024]{1,0:T(8,128)(2,1)S(1)}, u32[]{:S(2)}, u32[]{:S(2)}) collective-permute-start(bf16[64,1024]{1,0:T(8,128)(2,1)} %get-tuple-element.242), channel_id=1, source_target_pairs={{0,2},{2,4},{4,6},{6,8},{8,10},{10,12},{12,14},{14,16},{16,18},{18... | collective-permute-start | bytes 393224 | tf_op jit(solution)/shard_map/ppermute | solution.py:386
  51.6 7.4 %collective-permute-start.8 = (bf16[64,1024]{1,0:T(8,128)(2,1)S(1)}, bf16[64,1024]{1,0:T(8,128)(2,1)S(1)}, u32[]{:S(2)}, u32[]{:S(2)}) collective-permute-start(bf16[64,1024]{1,0:T(8,128)(2,1)S(1)} %get-tuple-element.241), channel_id=1, source_target_pairs={{2,0},{4,2},{6,4},{8,6},{10,8},{12,10},{14,12},{16,14},{18,16},{20... | collective-permute-start | bytes 393224 | tf_op jit(solution)/shard_map/ppermute | solution.py:391
  53.9 5.2 %collective-permute-start.10 = (bf16[64,1024]{1,0:T(8,128)(2,1)}, bf16[64,1024]{1,0:T(8,128)(2,1)S(1)}, u32[]{:S(2)}, u32[]{:S(2)}) collective-permute-start(bf16[64,1024]{1,0:T(8,128)(2,1)} %get-tuple-element.239), channel_id=1, source_target_pairs={{2,0},{4,2},{6,4},{8,6},{10,8},{12,10},{14,12},{16,14},{18,16},{20... | collective-permute-start | bytes 393224 | tf_op jit(solution)/shard_map/ppermute | solution.py:391
  55.1 5.0 %collective-permute-start.9 = (bf16[64,1024]{1,0:T(8,128)(2,1)}, bf16[64,1024]{1,0:T(8,128)(2,1)S(1)}, u32[]{:S(2)}, u32[]{:S(2)}) collective-permute-start(bf16[64,1024]{1,0:T(8,128)(2,1)} %get-tuple-element.240), channel_id=1, source_target_pairs={{0,2},{2,4},{4,6},{6,8},{8,10},{10,12},{12,14},{14,16},{16,18},{18... | collective-permute-start | bytes 393224 | tf_op jit(solution)/shard_map/ppermute | solution.py:386
  61.1 1.2 copy-start.13
  62.3 1.0 copy-start.14
  66.9 10.2 %copy-start.7 = (bf16[2,128,1024]{2,1,0:T(8,128)(2,1)}, bf16[2,128,1024]{2,1,0:T(8,128)(2,1)S(1)}, u32[]{:S(2)}) copy-start(bf16[2,128,1024]{2,1,0:T(8,128)(2,1)S(1)} %get-tuple-element.121.grads) | copy-start | bytes 1572868
  66.9 10.2 %collective-permute-start.11 = (bf16[128,1024]{1,0:T(8,128)(2,1)S(1)}, bf16[128,1024]{1,0:T(8,128)(2,1)S(1)}, u32[]{:S(2)}, u32[]{:S(2)}) collective-permute-start(bf16[128,1024]{1,0:T(8,128)(2,1)S(1)} %get-tuple-element.117), channel_id=1, source_target_pairs={{0,2},{2,4},{4,6},{6,8},{8,10},{10,12},{12,14},{14,16},{16,18},{18... | collective-permute-start | bytes 786440 | tf_op jit(solution)/shard_map/ppermute | solution.py:386
  73.0 5.3 %collective-permute-start.12 = (bf16[128,1024]{1,0:T(8,128)(2,1)S(1)}, bf16[128,1024]{1,0:T(8,128)(2,1)S(1)}, u32[]{:S(2)}, u32[]{:S(2)}) collective-permute-start(bf16[128,1024]{1,0:T(8,128)(2,1)S(1)} %get-tuple-element.118), channel_id=1, source_target_pairs={{2,0},{4,2},{6,4},{8,6},{10,8},{12,10},{14,12},{16,14},{18,16},{20... | collective-permute-start | bytes 786440 | tf_op jit(solution)/shard_map/ppermute | solution.py:391
  79.0 10.7 %collective-permute-start.13 = (bf16[1728,128]{1,0:T(8,128)(2,1)S(1)}, bf16[1728,128]{1,0:T(8,128)(2,1)}, u32[]{:S(2)}, u32[]{:S(2)}) collective-permute-start(bf16[1728,128]{1,0:T(8,128)(2,1)S(1)} %broadcast_select_fusion.2), channel_id=1, source_target_pairs={{0,2},{2,0},{4,6},{6,4},{8,10},{10,8},{12,14},{14,12},{16,18},{18,... | collective-permute-start | bytes 1327112 | tf_op jit(solution)/shard_map/ppermute | solution.py:409
  83.7 1.0 copy-start.8
  89.7 12.2 %copy-start.6 = (bf16[4,64,4096]{2,1,0:T(8,128)(2,1)S(1)}, bf16[4,64,4096]{2,1,0:T(8,128)(2,1)}, u32[]{:S(2)}) copy-start(bf16[4,64,4096]{2,1,0:T(8,128)(2,1)} %copy-done.5) | copy-start | bytes 6291460
  89.7 12.2 %copy-start.20 = (bf16[128,256]{1,0:T(8,128)(2,1)S(1)}, bf16[128,256]{1,0:T(8,128)(2,1)}, u32[]{:S(2)}) copy-start(bf16[128,256]{1,0:T(8,128)(2,1)} %constant.27.clone.unpool) | copy-start | bytes 196612
  91.1 13.8 %copy-start.1 = (bf16[2,32,4096]{2,1,0:T(8,128)(2,1)S(1)}, bf16[2,32,4096]{2,1,0:T(8,128)(2,1)}, u32[]{:S(2)}) copy-start(bf16[2,32,4096]{2,1,0:T(8,128)(2,1)} %copy-done) | copy-start | bytes 1572868
  91.1 13.8 %copy-start.3 = (bf16[2,32,4096]{2,1,0:T(8,128)(2,1)S(1)}, bf16[2,32,4096]{2,1,0:T(8,128)(2,1)}, u32[]{:S(2)}) copy-start(bf16[2,32,4096]{2,1,0:T(8,128)(2,1)} %copy-done.2) | copy-start | bytes 1572868
  91.1 10.6 %collective-permute-start.15 = (bf16[2,64,1024]{2,1,0:T(8,128)(2,1)S(1)}, bf16[2,64,1024]{2,1,0:T(8,128)(2,1)S(1)}, u32[]{:S(2)}, u32[]{:S(2)}) collective-permute-start(bf16[2,64,1024]{2,1,0:T(8,128)(2,1)S(1)} %get-tuple-element.132), channel_id=1, source_target_pairs={{0,1},{1,0},{2,3},{3,2},{4,5},{5,4},{6,7},{7,6},{8,9},{9,8},{10,11... | collective-permute-start | bytes 786440 | tf_op jit(solution)/shard_map/ppermute | solution.py:395
  92.7 9.1 %collective-permute-start.14 = (bf16[864,128]{1,0:T(8,128)(2,1)S(1)}, bf16[864,128]{1,0:T(8,128)(2,1)S(1)}, u32[]{:S(2)}, u32[]{:S(2)}) collective-permute-start(bf16[864,128]{1,0:T(8,128)(2,1)S(1)} %broadcast_select_fusion.5), channel_id=1, source_target_pairs={{0,4},{2,6},{4,0},{6,2},{8,12},{10,14},{12,8},{14,10},{16,20},{18,... | collective-permute-start | bytes 663560 | tf_op jit(solution)/shard_map/ppermute | solution.py:409
  103.3 8.3 %collective-permute-start.18 = (bf16[864,128]{1,0:T(8,128)(2,1)S(1)}, bf16[864,128]{1,0:T(8,128)(2,1)S(1)}, u32[]{:S(2)}, u32[]{:S(2)}) collective-permute-start(bf16[864,128]{1,0:T(8,128)(2,1)S(1)} %add_convert_fusion.3), channel_id=1, source_target_pairs={{0,8},{2,10},{4,12},{6,14},{8,0},{10,2},{12,4},{14,6},{16,24},{18,... | collective-permute-start | bytes 663560 | tf_op jit(solution)/shard_map/ppermute | solution.py:409
  111.7 12.4 %copy-start.22 = (bf16[864,128]{1,0:T(8,128)(2,1)}, bf16[864,128]{1,0:T(8,128)(2,1)S(1)}, u32[]{:S(2)}) copy-start(bf16[864,128]{1,0:T(8,128)(2,1)S(1)} %add_convert_fusion.2) | copy-start | bytes 663556
  111.7 12.4 %collective-permute-start.19 = (bf16[864,128]{1,0:T(8,128)(2,1)S(1)}, bf16[864,128]{1,0:T(8,128)(2,1)S(1)}, u32[]{:S(2)}, u32[]{:S(2)}) collective-permute-start(bf16[864,128]{1,0:T(8,128)(2,1)S(1)} %add_convert_fusion.2), channel_id=1, source_target_pairs={{0,16},{2,18},{4,20},{6,22},{8,24},{10,26},{12,28},{14,30},{16,0},... | collective-permute-start | bytes 663560 | tf_op jit(solution)/shard_map/ppermute | solution.py:409
  113.7 14.3 %collective-permute-start.16 = (bf16[64,4096]{1,0:T(8,128)(2,1)}, bf16[64,4096]{1,0:T(8,128)(2,1)}, u32[]{:S(2)}, u32[]{:S(2)}) collective-permute-start(bf16[64,4096]{1,0:T(8,128)(2,1)} %get-tuple-element.136), channel_id=1, source_target_pairs={{0,2},{2,4},{4,6},{6,8},{8,10},{10,12},{12,14},{14,16},{16,18},{18... | collective-permute-start | bytes 1572872 | tf_op jit(solution)/shard_map/ppermute | solution.py:386
  115.8 12.2 %collective-permute-start.17 = (bf16[64,4096]{1,0:T(8,128)(2,1)}, bf16[64,4096]{1,0:T(8,128)(2,1)}, u32[]{:S(2)}, u32[]{:S(2)}) collective-permute-start(bf16[64,4096]{1,0:T(8,128)(2,1)} %get-tuple-element.137), channel_id=1, source_target_pairs={{2,0},{4,2},{6,4},{8,6},{10,8},{12,10},{14,12},{16,14},{18,16},{20... | collective-permute-start | bytes 1572872 | tf_op jit(solution)/shard_map/ppermute | solution.py:391
  128.0 8.8 %collective-permute-start.21 = (bf16[864,128]{1,0:T(8,128)(2,1)S(1)}, bf16[864,128]{1,0:T(8,128)(2,1)S(1)}, u32[]{:S(2)}, u32[]{:S(2)}) collective-permute-start(bf16[864,128]{1,0:T(8,128)(2,1)S(1)} %add_convert_fusion.1), channel_id=1, source_target_pairs={{0,4},{2,6},{4,0},{6,2},{8,12},{10,14},{12,8},{14,10},{16,20},{18,... | collective-permute-start | bytes 663560 | tf_op jit(solution)/shard_map/ppermute | solution.py:409
  131.1 4.3 %collective-permute-start.20 = (bf16[448,128]{1,0:T(8,128)(2,1)S(1)}, bf16[448,128]{1,0:T(8,128)(2,1)S(1)}, u32[]{:S(2)}, u32[]{:S(2)}) collective-permute-start(bf16[448,128]{1,0:T(8,128)(2,1)S(1)} %broadcast_select_fusion.8), channel_id=1, source_target_pairs={{0,2},{2,0},{4,6},{6,4},{8,10},{10,8},{12,14},{14,12},{16,18},{18,... | collective-permute-start | bytes 344072 | tf_op jit(solution)/shard_map/ppermute | solution.py:409
  137.0 8.8 %collective-permute-start.23 = (bf16[1728,128]{1,0:T(8,128)(2,1)S(1)}, bf16[1728,128]{1,0:T(8,128)(2,1)S(1)}, u32[]{:S(2)}, u32[]{:S(2)}) collective-permute-start(bf16[1728,128]{1,0:T(8,128)(2,1)S(1)} %pad_maximum_fusion.1), channel_id=1, source_target_pairs={{0,2},{2,0},{4,6},{6,4},{8,10},{10,8},{12,14},{14,12},{16,18},{18,... | collective-permute-start | bytes 1327112 | tf_op jit(solution)/shard_map/ppermute | solution.py:409
  137.0 8.7 %collective-permute-start.24 = (bf16[4,32,1024]{2,1,0:T(8,128)(2,1)S(1)}, bf16[4,32,1024]{2,1,0:T(8,128)(2,1)S(1)}, u32[]{:S(2)}, u32[]{:S(2)}) collective-permute-start(bf16[4,32,1024]{2,1,0:T(8,128)(2,1)S(1)} %get-tuple-element.187), channel_id=1, source_target_pairs={{0,1},{1,0},{2,3},{3,2},{4,5},{5,4},{6,7},{7,6},{8,9},{9,8},{10,11... | collective-permute-start | bytes 786440 | tf_op jit(solution)/shard_map/ppermute | solution.py:395
  138.3 5.4 %collective-permute-start.22 = (bf16[224,128]{1,0:T(8,128)(2,1)S(1)}, bf16[224,128]{1,0:T(8,128)(2,1)S(1)}, u32[]{:S(2)}, u32[]{:S(2)}) collective-permute-start(bf16[224,128]{1,0:T(8,128)(2,1)S(1)} %broadcast_select_fusion.11), channel_id=1, source_target_pairs={{0,4},{2,6},{4,0},{6,2},{8,12},{10,14},{12,8},{14,10},{16,20},{18,... | collective-permute-start | bytes 172040 | tf_op jit(solution)/shard_map/ppermute | solution.py:409
  145.8 8.0 %collective-permute-start.26 = (bf16[4,32,1024]{2,1,0:T(8,128)(2,1)S(1)}, bf16[4,32,1024]{2,1,0:T(8,128)(2,1)S(1)}, u32[]{:S(2)}, u32[]{:S(2)}) collective-permute-start(bf16[4,32,1024]{2,1,0:T(8,128)(2,1)S(1)} %get-tuple-element.200), channel_id=1, source_target_pairs={{0,1},{1,0},{2,3},{3,2},{4,5},{5,4},{6,7},{7,6},{8,9},{9,8},{10,11... | collective-permute-start | bytes 786440 | tf_op jit(solution)/shard_map/ppermute | solution.py:395
  147.0 6.8 %collective-permute-start.25 = (bf16[224,128]{1,0:T(8,128)(2,1)S(1)}, bf16[224,128]{1,0:T(8,128)(2,1)S(1)}, u32[]{:S(2)}, u32[]{:S(2)}) collective-permute-start(bf16[224,128]{1,0:T(8,128)(2,1)S(1)} %add_convert_fusion.7), channel_id=1, source_target_pairs={{0,8},{2,10},{4,12},{6,14},{8,0},{10,2},{12,4},{14,6},{16,24},{18,... | collective-permute-start | bytes 172040 | tf_op jit(solution)/shard_map/ppermute | solution.py:409
  153.8 10.1 %collective-permute-start.28 = (bf16[4,32,1024]{2,1,0:T(8,128)(2,1)S(1)}, bf16[4,32,1024]{2,1,0:T(8,128)(2,1)S(1)}, u32[]{:S(2)}, u32[]{:S(2)}) collective-permute-start(bf16[4,32,1024]{2,1,0:T(8,128)(2,1)S(1)} %get-tuple-element.213), channel_id=1, source_target_pairs={{0,1},{1,0},{2,3},{3,2},{4,5},{5,4},{6,7},{7,6},{8,9},{9,8},{10,11... | collective-permute-start | bytes 786440 | tf_op jit(solution)/shard_map/ppermute | solution.py:395
  155.0 8.9 %collective-permute-start.27 = (bf16[224,128]{1,0:T(8,128)(2,1)S(1)}, bf16[224,128]{1,0:T(8,128)(2,1)S(1)}, u32[]{:S(2)}, u32[]{:S(2)}) collective-permute-start(bf16[224,128]{1,0:T(8,128)(2,1)S(1)} %add_convert_fusion.6), channel_id=1, source_target_pairs={{0,16},{2,18},{4,20},{6,22},{8,24},{10,26},{12,28},{14,30},{16,0},... | collective-permute-start | bytes 172040 | tf_op jit(solution)/shard_map/ppermute | solution.py:409
  164.0 6.4 %collective-permute-start.30 = (bf16[4,32,1024]{2,1,0:T(8,128)(2,1)S(1)}, bf16[4,32,1024]{2,1,0:T(8,128)(2,1)S(1)}, u32[]{:S(2)}, u32[]{:S(2)}) collective-permute-start(bf16[4,32,1024]{2,1,0:T(8,128)(2,1)S(1)} %get-tuple-element.219), channel_id=1, source_target_pairs={{0,1},{1,0},{2,3},{3,2},{4,5},{5,4},{6,7},{7,6},{8,9},{9,8},{10,11... | collective-permute-start | bytes 786440 | tf_op jit(solution)/shard_map/ppermute | solution.py:395
  164.9 4.8 %collective-permute-start.29 = (bf16[224,128]{1,0:T(8,128)(2,1)S(1)}, bf16[224,128]{1,0:T(8,128)(2,1)S(1)}, u32[]{:S(2)}, u32[]{:S(2)}) collective-permute-start(bf16[224,128]{1,0:T(8,128)(2,1)S(1)} %add_convert_fusion.5), channel_id=1, source_target_pairs={{0,4},{2,6},{4,0},{6,2},{8,12},{10,14},{12,8},{14,10},{16,20},{18,... | collective-permute-start | bytes 172040 | tf_op jit(solution)/shard_map/ppermute | solution.py:409
  170.4 3.1 %collective-permute-start.31 = (bf16[448,128]{1,0:T(8,128)(2,1)S(1)}, bf16[448,128]{1,0:T(8,128)(2,1)S(1)}, u32[]{:S(2)}, u32[]{:S(2)}) collective-permute-start(bf16[448,128]{1,0:T(8,128)(2,1)S(1)} %pad_maximum_fusion.3), channel_id=1, source_target_pairs={{0,2},{2,0},{4,6},{6,4},{8,10},{10,8},{12,14},{14,12},{16,18},{18,... | collective-permute-start | bytes 344072 | tf_op jit(solution)/shard_map/ppermute | solution.py:409
  (8 other events, 6.9 us)
